TPU v7x, 32 devices: a whole 2x2x4 slice. The times are simulated.
32 devices in a mesh: rows: 16 (over z, y, x), cols: 2 (over core).
Axes of the slice: x: 2, y: 2, z: 4, core: 2. Of those that a mesh axis runs over, the one named last changes fastest.
Arguments:
- sketch: bfloat16 [131072, 256], P(('rows', 'cols')), may hold values from -6 to 6
- blocks: bfloat16 [256, 256, 256], P(('rows', 'cols')), may hold values from -0.375 to 0.375
- block_rows: int32 [256], P(('rows', 'cols')), may hold values from 0 to 3, as said below
- block_cols: int32 [256], P(('rows', 'cols')), may hold values from 0 to 255
- counts: int32 [32], P(('rows', 'cols')), may hold values from 1 to 8, as said below
Outputs:
- basis: float32 [16384, 256], P(('rows', 'cols'))
- factor: float32 [256, 256], replicated
Inputs may be any that keep to these rules, and one draw needn't show every extreme that they name: Within one device's 8 slots the pairs (block_rows, block_cols) are distinct. `counts`: some device has exactly 8 live slots.
All inputs are finite; a program needn't handle non-finite values.
Results may differ from a plain program's by a relative error of at most 0.0003.
Values may be sent and summed in bfloat16 or wider, within the bound.
No kernel may reach another device: no remote copies, remote signals or barrier semaphores. Data moves between devices by JAX's collectives and lax.ppermute only.
A program may use at most 64 MiB of HBM per device.

v0:
```python
import functools

import jax
import jax.numpy as jnp
from jax import lax
from jax.experimental import pallas as pl
from jax.experimental.pallas import tpu as pltpu
from jax.sharding import PartitionSpec as P

RB = 4
HIGHEST = lax.Precision.HIGHEST
VMEM = pl.BlockSpec(memory_space=pltpu.VMEM)
SMEM = pl.BlockSpec(memory_space=pltpu.SMEM)
MIB = 1024 * 1024


ACROSS = (*range(11, 21), 22, 24, 28, 36)
WITHIN = (5, 6, 7, 8, 9, 10, 12)


def table_kernel(cols_ref, counts_ref, out_ref):
    slots = cols_ref.shape[0]
    lane = lax.broadcasted_iota(jnp.int32, out_ref.shape, 2)
    table = jnp.where(lane == slots, counts_ref[0], 0)
    for s in range(slots):
        table = jnp.where(lane == s, cols_ref[s], table)
    out_ref[...] = table


def table_copies(block_cols, counts, devices):
    return pl.pallas_call(
        table_kernel,
        out_shape=jax.ShapeDtypeStruct((devices, 1, 128), jnp.int32),
        in_specs=[SMEM, SMEM],
        out_specs=VMEM,
        compiler_params=pltpu.CompilerParams(vmem_limit_bytes=24 * MIB),
        name="table_copies",
    )(block_cols, counts)


def over(values, size):
    return values >> (size.bit_length() - 1)


def plan_kernel(slots, per, within, across, table_ref, places_ref, lists_ref, *level_refs):
    devices = table_ref.shape[0]
    rows, cols = lax.axis_size("rows"), lax.axis_size("cols")
    panel = per * rows
    part = panel // 2
    groups = [range(at, min(at + 64, devices)) for at in range(0, devices, 64)]

    def read(group):
        table = table_ref[group.start : group.stop, 0, :]
        lane = lax.broadcasted_iota(jnp.int32, table.shape, 1)
        counts = table[:, slots : slots + 1]
        table = jnp.where(lane < counts, table, -1)
        block = lax.broadcasted_iota(jnp.int32, (len(group), panel), 1)
        return table, counts, [table[:, s : s + 1] == block for s in range(slots)]

    lines = -(-cols // 8) * 8
    line = lax.broadcasted_iota(jnp.int32, (3 * lines, panel), 0)
    ids = lax.broadcasted_iota(jnp.int32, (1, panel), 1)
    asks = jnp.zeros((3 * lines, panel), jnp.float32)
    for group in groups:
        _, _, asked = read(group)
        some = jnp.where(functools.reduce(jnp.logical_or, asked), 1.0, 0.0).astype(jnp.bfloat16)
        shape = (3 * lines, len(group))
        number = lax.broadcasted_iota(jnp.int32, shape, 0)
        device = lax.broadcasted_iota(jnp.int32, shape, 1) + group.start
        core, side = device & (cols - 1), over(device, devices // 2)
        reads = (number == core) | (number == lines * (1 + side) + core)
        asks += jnp.dot(jnp.where(reads, 1.0, 0.0).astype(jnp.bfloat16), some, preferred_element_type=jnp.float32)
    own_half = (line >= lines) & (over(line - lines, lines) == over(lax.broadcasted_iota(jnp.int32, line.shape, 1), part))
    asks = jnp.where((asks > 0.5) & jnp.logical_not(own_half), 1.0, 0.0)
    first = lax.broadcasted_iota(jnp.int32, (panel, panel), 0)
    second = lax.broadcasted_iota(jnp.int32, (panel, panel), 1)
    after = first > second
    near = jnp.where(after & ((first ^ second) < per), 1.0, 0.0).astype(jnp.bfloat16)
    after = jnp.where(after, 1.0, 0.0).astype(jnp.bfloat16)
    same = jnp.where(first == second, 1.0, 0.0).astype(jnp.bfloat16)
    nt = (((1,), (1,)), ((), ()))

    def ranks(a, b):
        return lax.dot_general(a, b, nt, preferred_element_type=jnp.float32)

    short = asks.astype(jnp.bfloat16)
    near_rank = ranks(short, near)
    far_rank = ranks(short, after)
    longest = jnp.max(jnp.where(line < lines, near_rank + asks, 0.0)).astype(jnp.int32)
    level_refs[0][0] = sum((longest > level).astype(jnp.int32) for level in within)
    longest = jnp.max(jnp.where(line < lines, 0.0, far_rank + asks)).astype(jnp.int32)
    level_refs[1][0] = sum((longest > level).astype(jnp.int32) for level in across)
    me = lax.axis_index("rows")
    half, c = over(me, rows // 2), lax.axis_index("cols")

    def row(values, number):
        return jnp.sum(jnp.where(line == number, values, 0.0), axis=0, keepdims=True)

    here = (ids & -per) - half * part + row(near_rank, c).astype(jnp.int32)
    there = part + row(far_rank, lines * (1 + half) + c).astype(jnp.int32)
    place = jnp.where(over(ids, part) == half, here, there)
    chosen = jnp.zeros(places_ref.shape, jnp.float32)
    for group in groups:
        table, _, asked = read(group)
        lane = lax.broadcasted_iota(jnp.int32, table.shape, 1)
        places = jnp.zeros(table.shape, jnp.int32)
        for s in range(slots):
            found = jnp.sum(jnp.where(asked[s], place, 0), axis=1, keepdims=True)
            places = jnp.where(lane == s, found, places)
        shape = (places_ref.shape[0], len(group))
        number = lax.broadcasted_iota(jnp.int32, shape, 0)
        device = lax.broadcasted_iota(jnp.int32, shape, 1) + group.start
        reads = functools.reduce(
            jnp.logical_or,
            [(number == i) & (device == (me ^ d) * cols + c) for i, d in enumerate(distances(shape[0]))],
        )
        chosen += jnp.dot(
            jnp.where(reads, 1.0, 0.0).astype(jnp.bfloat16),
            places.astype(jnp.float32).astype(jnp.bfloat16),
            preferred_element_type=jnp.float32,
        )
    places_ref[...] = chosen.astype(jnp.int32)
    line = lax.broadcasted_iota(jnp.int32, (panel, 3 * lines), 1)

    def column(values, number):
        return jnp.sum(jnp.where(line == number, values, 0.0), axis=1, keepdims=True)

    turned, near_rank, far_rank = ranks(same, short), ranks(near, short), ranks(after, short)
    ids = lax.broadcasted_iota(jnp.int32, (panel, 1), 0)
    number = lax.broadcasted_iota(jnp.int32, (panel, lists_ref.shape[1]), 1)
    near_rank = column(near_rank, c).astype(jnp.int32)
    here = (ids & -per) - half * part + near_rank
    other = lines * (2 - half) + c
    sent = (column(turned, other) > 0.5) & (column(far_rank, other).astype(jnp.int32) == number)
    sent = jnp.sum(jnp.where(sent, here, 0), axis=0, keepdims=True)
    kept = (column(turned, c) > 0.5) & (over(ids, per) == me) & (near_rank == number)
    kept = jnp.sum(jnp.where(kept, ids & (per - 1), 0), axis=0, keepdims=True)
    lists_ref[...] = jnp.where(lax.broadcasted_iota(jnp.int32, lists_ref.shape, 0) == 0, sent, kept)


def plan(table, slots, per, within, across):
    devices = table.shape[0]
    return pl.pallas_call(
        functools.partial(plan_kernel, slots, per, within, across),
        out_shape=(
            jax.ShapeDtypeStruct((lax.axis_size("rows") // 2, 128), jnp.int32),
            jax.ShapeDtypeStruct((8, 128), jnp.int32),
            jax.ShapeDtypeStruct((1,), jnp.int32),
            jax.ShapeDtypeStruct((1,), jnp.int32),
        ),
        in_specs=[VMEM],
        out_specs=(VMEM, VMEM, SMEM, SMEM),
        compiler_params=pltpu.CompilerParams(vmem_limit_bytes=48 * MIB),
        name="plan",
    )(table)


def distances(members):
    return [0, *sorted(range(1, members), key=lambda d: (-d.bit_count(), -d))]


def turn_kernel(sketch_ref, out_ref):
    members = out_ref.shape[0]
    me = lax.axis_index("rows") % members
    for i, d in enumerate(distances(members)):
        out_ref[i] = sketch_ref[:, me ^ d]


def turn(sketch):
    blocks, members, height, columns = sketch.shape
    return pl.pallas_call(
        turn_kernel,
        out_shape=jax.ShapeDtypeStruct((members, blocks, height, columns), sketch.dtype),
        in_specs=[VMEM],
        out_specs=VMEM,
        compiler_params=pltpu.CompilerParams(vmem_limit_bytes=24 * MIB),
        cost_estimate=pl.CostEstimate(flops=0, bytes_accessed=4 * sketch.size, transcendentals=0),
        name="turn_stripes",
    )(sketch)


def cut_kernel(lists_ref, stripes_ref, *out_refs):
    for k in range(out_refs[0].shape[0]):
        for i, out_ref in enumerate(out_refs):
            out_ref[k] = stripes_ref[i, lists_ref[1, k]]


def cut(lists, stripes, count):
    members, _, height, columns = stripes.shape
    return pl.pallas_call(
        cut_kernel,
        out_shape=(jax.ShapeDtypeStruct((count, height, columns), stripes.dtype),) * members,
        in_specs=[SMEM, VMEM],
        out_specs=(VMEM,) * members,
        compiler_params=pltpu.CompilerParams(vmem_limit_bytes=24 * MIB),
        name="cut_stripes",
    )(lists, stripes)


def order_kernel(*refs):
    *stripe_refs, all_ref = refs
    members = len(stripe_refs)
    me = lax.axis_index("rows") % members
    per = all_ref.shape[0] // members
    for ref, d in zip(stripe_refs, distances(members)):
        all_ref[pl.ds((me ^ d) * per, ref.shape[0])] = ref[...]


def order(stripes, per):
    _, height, columns = stripes[0].shape
    return pl.pallas_call(
        order_kernel,
        out_shape=jax.ShapeDtypeStruct((len(stripes) * per, height, columns), stripes[0].dtype),
        in_specs=[VMEM] * len(stripes),
        out_specs=VMEM,
        compiler_params=pltpu.CompilerParams(vmem_limit_bytes=24 * MIB),
        name="order_stripes",
    )(*stripes)


def list_kernel(list_ref, all_ref, out_ref):
    for k in range(out_ref.shape[0]):
        out_ref[k] = all_ref[list_ref[0, k]]


def listed(numbers, stripes, count):
    return pl.pallas_call(
        list_kernel,
        out_shape=jax.ShapeDtypeStruct((count, *stripes.shape[1:]), stripes.dtype),
        in_specs=[SMEM, VMEM],
        out_specs=VMEM,
        compiler_params=pltpu.CompilerParams(vmem_limit_bytes=24 * MIB),
        name="listed_stripes",
    )(numbers, stripes)


def pick_kernel(places_ref, own_ref, other_ref, *refs):
    *out_refs, whole = refs
    here = own_ref.shape[0]
    whole[:here] = own_ref[...]
    whole[here:] = other_ref[...]
    for i, out_ref in enumerate(out_refs):
        for s in range(out_ref.shape[0]):
            out_ref[s] = whole[jnp.minimum(places_ref[i, s], whole.shape[0] - 1)]


def pick(places, own, other, slots, members):
    shape = own.shape[1:]
    return pl.pallas_call(
        pick_kernel,
        out_shape=(jax.ShapeDtypeStruct((slots, *shape), own.dtype),) * members,
        in_specs=[SMEM, VMEM, VMEM],
        out_specs=(VMEM,) * members,
        scratch_shapes=[pltpu.VMEM((own.shape[0] + other.shape[0], *shape), own.dtype)],
        compiler_params=pltpu.CompilerParams(vmem_limit_bytes=24 * MIB),
        name="pick_stripes",
    )(places, own, other)


def product_kernel(rows_ref, counts_ref, blocks_ref, *refs):
    *chosen_refs, out_ref, whole = refs
    slots, width, _ = blocks_ref.shape
    columns = out_ref.shape[1]
    members = len(chosen_refs)
    me = lax.axis_index("rows") % members
    for ref, d in zip(chosen_refs, distances(members) if members > 1 else [0]):
        whole[me ^ d] = ref[...]
    out_ref[...] = jnp.zeros_like(out_ref)
    for s in range(slots):
        piece = whole[:, s].reshape(width, columns)
        product = jnp.dot(blocks_ref[s], piece, preferred_element_type=jnp.float32)
        at = pl.ds(pl.multiple_of(rows_ref[s] * width, width), width)
        out_ref[at, :] += jnp.where(s < counts_ref[0], product, 0.0)


def block_products(block_rows, counts, blocks, chosen):
    _, width, _ = blocks.shape
    columns = chosen[0].shape[-1]
    return pl.pallas_call(
        product_kernel,
        out_shape=jax.ShapeDtypeStruct((RB * width, columns), jnp.float32),
        in_specs=[SMEM, SMEM, VMEM] + [VMEM] * len(chosen),
        out_specs=VMEM,
        scratch_shapes=[pltpu.VMEM((len(chosen), *chosen[0].shape), chosen[0].dtype)],
        compiler_params=pltpu.CompilerParams(vmem_limit_bytes=24 * MIB),
        name="block_products",
    )(block_rows, counts, blocks, *chosen)


def gram_kernel(mine_ref, other_ref, own_ref, *refs):
    *gram_refs, slab = refs
    c = lax.axis_index("cols")
    me = lax.axis_index("rows") % len(gram_refs)
    share, (height, width) = own_ref.shape[0], gram_refs[0].shape
    slab[...] = mine_ref[...] + other_ref[...]
    own_ref[...] = slab[pl.ds(pl.multiple_of(c * share, share), share), :]
    right = slab[:, pl.ds(pl.multiple_of(c * width, width), width)]
    gram = lax.dot_general(
        slab[...], right, (((0,), (0,)), ((), ())), precision=HIGHEST, preferred_element_type=jnp.float32
    )
    for q in range(len(gram_refs)):
        for d in range(len(gram_refs)):

            @pl.when(me ^ d == q)
            def _():
                gram_refs[d][...] = gram[q * height : (q + 1) * height]


def sum_and_gram(mine, other):
    rows, columns = mine.shape
    return pl.pallas_call(
        gram_kernel,
        out_shape=(
            jax.ShapeDtypeStruct((rows // 2, columns), jnp.float32),
            *[jax.ShapeDtypeStruct((columns // 4, columns // 2), jnp.float32)] * 4,
        ),
        in_specs=[VMEM, VMEM],
        out_specs=(VMEM,) * 5,
        scratch_shapes=[pltpu.VMEM((rows, columns), jnp.float32)],
        compiler_params=pltpu.CompilerParams(vmem_limit_bytes=24 * MIB),
        name="sum_and_gram",
    )(mine, other)


def stack_kernel(*refs):
    *quarter_refs, out_ref = refs
    me = lax.axis_index("rows") % len(quarter_refs)
    height = quarter_refs[0].shape[0]
    for d, ref in enumerate(quarter_refs):
        out_ref[pl.ds(pl.multiple_of((me ^ d) * height, height), height), :] = ref[...]


def stack(quarters):
    height, width = quarters[0].shape
    return pl.pallas_call(
        stack_kernel,
        out_shape=jax.ShapeDtypeStruct((len(quarters) * height, width), jnp.float32),
        in_specs=[VMEM] * len(quarters),
        out_specs=VMEM,
        compiler_params=pltpu.CompilerParams(vmem_limit_bytes=24 * MIB),
        name="stack_quarters",
    )(*quarters)


def matmul(a, b, precision):
    return jnp.dot(a, b, precision=precision, preferred_element_type=jnp.float32)


def matmul_nt(a, b, precision):
    return lax.dot_general(
        a, b, (((1,), (1,)), ((), ())), precision=precision, preferred_element_type=jnp.float32
    )


def split_matmul(times, passes, a, b):
    a_high, b_high = a.astype(jnp.bfloat16), b.astype(jnp.bfloat16)
    result = times(a_high, b_high, None)
    if passes == 3:
        a_low = (a - a_high.astype(jnp.float32)).astype(jnp.bfloat16)
        b_low = (b - b_high.astype(jnp.float32)).astype(jnp.bfloat16)
        result += times(a_high, b_low, None) + times(a_low, b_high, None)
    return result


def factor_kernel(total_rows, *refs):
    *gram_refs, own_ref, basis_ref, factor_ref, whole, scaled, inverse, product = refs
    n = factor_ref.shape[0]
    if len(gram_refs) == 1:
        whole[...] = gram_refs[0][...]
    else:
        c = lax.axis_index("cols")
        width = n // 2
        whole[:, pl.ds(pl.multiple_of(c * width, width), width)] = gram_refs[0][...]
        whole[:, pl.ds(pl.multiple_of((1 - c) * width, width), width)] = gram_refs[1][...]
    row_ids = lax.broadcasted_iota(jnp.int32, (n, n), 0)
    col_ids = lax.broadcasted_iota(jnp.int32, (n, n), 1)
    diagonal = row_ids == col_ids
    identity = diagonal.astype(jnp.float32)
    half = jnp.where(row_ids > col_ids, 1.0, jnp.where(diagonal, 0.5, 0.0))
    gram = whole[...]
    on_diagonal = jnp.where(diagonal, gram, 0.0)
    down = jnp.sqrt(jnp.sum(on_diagonal, axis=1, keepdims=True))
    across = jnp.sqrt(jnp.sum(on_diagonal, axis=0, keepdims=True))
    up_down = 1.0 / down
    up_across = 1.0 / across
    scaled[...] = gram * up_down * up_across

    def refine(times, times_nt):
        w = inverse[...]
        upper = times(w, scaled[...])
        residual = times_nt(upper, w) - identity
        step = residual * half
        inverse[...] = w - matmul(step, w, lax.Precision.DEFAULT)
        product[...] = upper - matmul(step, upper, lax.Precision.DEFAULT)
        return jnp.sum(residual * residual)

    def exactly(times):
        return functools.partial(times, precision=HIGHEST)

    inverse[...] = identity - (scaled[...] - identity) * half
    for passes in (1, 3):
        refine(functools.partial(split_matmul, matmul, passes), functools.partial(split_matmul, matmul_nt, passes))

    def going(state):
        step, size = state
        return (step < 8) & (size > 1e-6)

    def advance(state):
        return state[0] + 1, refine(exactly(matmul), exactly(matmul_nt))

    _, size = lax.while_loop(going, advance, (jnp.int32(0), jnp.float32(1.0)))

    @pl.when(jnp.logical_not(size <= 1e-6))
    def _():
        inverse[...] = identity
        ids = lax.broadcasted_iota(jnp.int32, (n, 1), 0)

        def eliminate(j, carry):
            pivot_row = scaled[pl.ds(j, 1), :]
            inverse_row = inverse[pl.ds(j, 1), :]
            column = jnp.sum(jnp.where(col_ids == j, scaled[...], 0.0), axis=1, keepdims=True)
            pivot = jnp.sum(jnp.where(ids == j, column, 0.0), axis=0, keepdims=True)
            root = 1.0 / jnp.sqrt(pivot)
            ratio = jnp.where(ids > j, column / pivot, jnp.where(ids == j, 1.0 - root, 0.0))
            scaled[...] = scaled[...] - ratio * pivot_row
            inverse[...] = inverse[...] - ratio * inverse_row
            return carry

        lax.fori_loop(0, n, eliminate, 0)
        product[...] = matmul(inverse[...], whole[...] * up_down * up_across, HIGHEST)

    w = inverse[...]
    root_rows = jnp.sqrt(jnp.float32(total_rows))
    upper = product[...] * across / root_rows
    factor_ref[...] = jnp.where(row_ids <= col_ids, upper, 0.0)
    basis_ref[...] = matmul_nt(own_ref[...] * up_across, w, HIGHEST) * root_rows


def factor_and_basis(total_rows, grams, own):
    columns = own.shape[1]
    return pl.pallas_call(
        functools.partial(factor_kernel, total_rows),
        out_shape=(
            jax.ShapeDtypeStruct(own.shape, jnp.float32),
            jax.ShapeDtypeStruct((columns, columns), jnp.float32),
        ),
        in_specs=[VMEM] * (len(grams) + 1),
        out_specs=(VMEM, VMEM),
        scratch_shapes=[pltpu.VMEM((columns, columns), jnp.float32)] * 4,
        compiler_params=pltpu.CompilerParams(vmem_limit_bytes=24 * MIB),
        name="factor_and_basis",
    )(*grams, own)


def exchange(pieces, rows):
    order = distances(len(pieces))
    return [
        lax.ppermute(piece, "rows", [(r, r ^ d) for r in range(rows)]) if d else piece
        for piece, d in zip(pieces, order)
    ]


def fetch(sketch, block_cols, counts, slots, width):
    rows, cols = lax.axis_size("rows"), lax.axis_size("cols")
    members = rows // 2
    height = width // members
    columns = sketch.shape[1]
    sketch = sketch.reshape(-1, members, height, columns)
    per = sketch.shape[0]
    largest = min(per * members, slots * members, 128)
    within = tuple(level for level in WITHIN if level < per)
    across = tuple(level for level in ACROSS if level < largest and members <= 8)
    stripes = turn(sketch)
    table = table_copies(block_cols, counts, rows * cols)
    table = lax.all_to_all(table, ("rows", "cols"), split_axis=0, concat_axis=0, tiled=True)
    places, lists, near, far = plan(table, slots, per, within, across)

    def within_half(count):
        def run():
            return order(exchange(cut(lists, stripes, count), rows), per)

        return run

    own = lax.switch(near[0], [within_half(count) for count in (*within, per)])

    def across_halves(count):
        def run():
            swap = [(r, (r + members) % rows) for r in range(rows)]
            other = lax.ppermute(listed(lists, own, count), "rows", swap)
            return pick(places, own, other, slots, members)

        return run

    picked = lax.switch(far[0], [across_halves(count) for count in (*across, largest)])
    return exchange(picked, rows)


def moved(piece, rows, d):
    return lax.ppermute(piece, "rows", [(r, r ^ d) for r in range(rows)])


def gram_halves(quarters, rows):
    first, *rest = quarters
    for d, quarter in enumerate(rest):
        first = first + moved(quarter, rows, d + 1)
    total = (first + moved(first, rows, 4)) + (moved(first, rows, 8) + moved(first, rows, 12))
    half = stack([total] + [moved(total, rows, d) for d in range(1, 4)])
    return half, lax.ppermute(half, "cols", [(0, 1), (1, 0)])


def local(sketch, blocks, block_rows, block_cols, counts):
    slots, width, _ = blocks.shape
    columns = sketch.shape[1]
    rows, cols = lax.axis_size("rows"), lax.axis_size("cols")
    chosen = fetch(sketch, block_cols, counts, slots, width)
    if chosen[0].shape[1] % 16:
        order = jnp.argsort(lax.axis_index("rows") % len(chosen) ^ jnp.array(distances(len(chosen))))
        chosen = [jnp.stack(chosen)[order].swapaxes(0, 1).reshape(1, slots, width, columns)[0]]
    partial_rows = block_products(block_rows, counts, blocks, chosen)
    if (rows, cols) == (16, 2):
        other = lax.ppermute(partial_rows, "cols", [(0, 1), (1, 0)])
        own, *quarters = sum_and_gram(partial_rows, other)
        grams = gram_halves(quarters, rows)
    else:
        own = lax.psum_scatter(partial_rows, "cols", scatter_dimension=0, tiled=True)
        grams = [lax.psum(matmul(own.T, own, HIGHEST), ("rows", "cols"))]
    return factor_and_basis(RB * width * rows, grams, own)


def solution(mesh):
    in_specs = (
        P(("rows", "cols"), None),
        P(("rows", "cols"), None, None),
        P(("rows", "cols")),
        P(("rows", "cols")),
        P(("rows", "cols")),
    )
    out_specs = (P(("rows", "cols"), None), P())
    return jax.shard_map(local, mesh=mesh, in_specs=in_specs, out_specs=out_specs, check_vma=False)
```

profile of v0, /device:TPU:0, one launch (start us, length us, event | category | flops | bytes accessed | tf_op | source)
XLA Modules:
  0.0 156.9 jit_solution(8491999897979728137)
XLA Ops:
  1.3 0.6 copy-done.3
  1.9 1.2 table_copies.1
  3.1 7.3 %all-to-all-start = ((s32[32,1,128]{2,1,0:T(1,128)}), s32[32,1,128]{2,1,0:T(1,128)S(1)}, u32[]{:S(2)}, u32[]{:S(2)}) async-start(s32[32,1,128]{2,1,0:T(1,128)} %table_copies.1), calls=%async_computation | async-start | bytes 32768 | tf_op jit(solution)/shard_map/all_to_all | solution.py:475
  10.4 1.6 %copy-done = bf16[4096,256]{1,0:T(8,128)(2,1)S(1)} copy-done((bf16[4096,256]{1,0:T(8,128)(2,1)S(1)}, bf16[4096,256]{1,0:T(8,128)(2,1)}, u32[]{:S(2)}) %copy-start) | copy-done | bytes 2097176
  12.0 0.1 turn_stripes.1
  12.1 5.3 %all-to-all-done.table_ref = s32[32,1,128]{2,1,0:T(1,128)S(1)} async-done(((s32[32,1,128]{2,1,0:T(1,128)}), s32[32,1,128]{2,1,0:T(1,128)S(1)}, u32[]{:S(2)}, u32[]{:S(2)}) %all-to-all-start) | async-done | bytes 16416 | tf_op jit(solution)/shard_map/all_to_all | solution.py:475
  17.5 1.3 plan.1
  20.1 14.8 %conditional.2 = (bf16[128,32,256]{2,1,0:T(8,128)(2,1)S(1)}) conditional(s32[]{:T(128)} %bitcast.1, (s32[8,128]{1,0:T(8,128)S(1)}, bf16[8,16,32,256]{3,2,1,0:T(8,128)(2,1)S(1)}) %tuple.76, (s32[8,128]{1,0:T(8,128)S(1)}, bf16[8,16,32,256]{3,2,1,0:T(8,128)(2,1)S(1)}) %tuple.76, (s32[8,128]{1,0:T(8,128)S(1)}, ...), branch_computations={%region_0.0_spmd, %region_1.0_spmd, %region_2.0_spmd, %region_3.0_... | conditional | bytes 7340320 | solution.py:484
  20.1 0.7 cut_stripes.9
  20.8 0.7 collective-permute-start.7
  21.4 2.3 %collective-permute-start.8 = (bf16[6,32,256]{2,1,0:T(8,128)(2,1)S(1)}, bf16[6,32,256]{2,1,0:T(8,128)(2,1)S(1)}, u32[]{:S(2)}, u32[]{:S(2)}) collective-permute-start(bf16[6,32,256]{2,1,0:T(8,128)(2,1)S(1)} %get-tuple-element.145), channel_id=1, source_target_pairs={{0,12},{2,14},{4,8},{6,10},{8,4},{10,6},{12,0},{14,2},{16,28},{18,... | collective-permute-start | bytes 294920 | tf_op jit(solution)/shard_map/cond/branch_1_fun/ppermute | solution.py:458
  23.7 1.5 collective-permute-start.9
  25.2 0.6 collective-permute-start.10
  25.8 1.4 collective-permute-start.11
  27.3 1.9 %collective-permute-done.7.refs_1_ = bf16[6,32,256]{2,1,0:T(8,128)(2,1)S(1)} collective-permute-done((bf16[6,32,256]{2,1,0:T(8,128)(2,1)S(1)}, bf16[6,32,256]{2,1,0:T(8,128)(2,1)S(1)}, u32[]{:S(2)}, u32[]{:S(2)}) %collective-permute-start.7) | collective-permute-done | bytes 98336 | tf_op jit(solution)/shard_map/cond/branch_1_fun/ppermute | solution.py:458
  29.1 0.4 collective-permute-start.12
  29.6 0.6 collective-permute-done.8.refs_2_
  30.2 1.2 collective-permute-start.13
  31.3 0.3 collective-permute-done.9.refs_3_
  31.6 1.6 %collective-permute-done.10.refs_4_ = bf16[6,32,256]{2,1,0:T(8,128)(2,1)S(1)} collective-permute-done((bf16[6,32,256]{2,1,0:T(8,128)(2,1)S(1)}, bf16[6,32,256]{2,1,0:T(8,128)(2,1)S(1)}, u32[]{:S(2)}, u32[]{:S(2)}) %collective-permute-start.10) | collective-permute-done | bytes 98336 | tf_op jit(solution)/shard_map/cond/branch_1_fun/ppermute | solution.py:458
  33.2 0.8 collective-permute-done.12.refs_6_
  34.0 0.8 collective-permute-done.13.refs_7_
  34.8 0.1 order_stripes.9
  34.9 16.9 %conditional.3 = ((bf16[8,32,256]{2,1,0:T(8,128)(2,1)S(1)}, bf16[8,32,256]{2,1,0:T(8,128)(2,1)S(1)}, bf16[8,32,256]{2,1,0:T(8,128)(2,1)S(1)}, bf16[8,32,256]{2,1...) conditional(s32[]{:T(128)} %bitcast, (s32[8,128]{1,0:T(8,128)S(1)}, ...), branch_computations={%region_8.0_spmd, %region_9.0_spmd, %region_10.0_spmd, %region_11.... | conditional | bytes 4194352 | solution.py:494
  34.9 0.6 listed_stripes.23
  35.6 0.5 collective-permute-start.64
  36.1 14.1 %collective-permute-done.64.other_ref = bf16[19,32,256]{2,1,0:T(8,128)(2,1)S(1)} collective-permute-done((bf16[19,32,256]{2,1,0:T(8,128)(2,1)S(1)}, bf16[19,32,256]{2,1,0:T(8,128)(2,1)S(1)}, u32[]{:S(2)}, u32[]{:S(2)}) %collective-permute-start.64) | collective-permute-done | bytes 311328 | tf_op jit(solution)/shard_map/cond/branch_8_fun/ppermute | solution.py:489
  50.2 1.6 %pick_stripes.23 = (bf16[8,32,256]{2,1,0:T(8,128)(2,1)S(1)}, bf16[8,32,256]{2,1,0:T(8,128)(2,1)S(1)}, bf16[8,32,256]{2,1,0:T(8,128)(2,1)S(1)}, bf16[8,32,256]{2,...) custom-call(s32[8,128]{1,0:T(8,128)S(1)} %get-tuple-element.235.plac, ...), custom_call_target="tpu_custom_call" | custom-call | tf_op jit(solution)/shard_map/cond/branch_8_fun/pick_stripes/pallas_call | solution.py:249
  51.8 3.0 %collective-permute-start.72 = (bf16[8,32,256]{2,1,0:T(8,128)(2,1)S(1)}, bf16[8,32,256]{2,1,0:T(8,128)(2,1)S(1)}, u32[]{:S(2)}, u32[]{:S(2)}) collective-permute-start(bf16[8,32,256]{2,1,0:T(8,128)(2,1)S(1)} %get-tuple-element.281), channel_id=1, source_target_pairs={{0,12},{2,14},{4,8},{6,10},{8,4},{10,6},{12,0},{14,2},{16,28},{18,... | collective-permute-start | bytes 393224 | tf_op jit(solution)/shard_map/ppermute | solution.py:458
  54.8 0.9 collective-permute-start.73
  55.7 1.5 collective-permute-start.74
  57.1 1.9 %collective-permute-start.75 = (bf16[8,32,256]{2,1,0:T(8,128)(2,1)}, bf16[8,32,256]{2,1,0:T(8,128)(2,1)S(1)}, u32[]{:S(2)}, u32[]{:S(2)}) collective-permute-start(bf16[8,32,256]{2,1,0:T(8,128)(2,1)} %get-tuple-element.284), channel_id=1, source_target_pairs={{0,8},{2,10},{4,12},{6,14},{8,0},{10,2},{12,4},{14,6},{16,24},{18,... | collective-permute-start | bytes 393224 | tf_op jit(solution)/shard_map/ppermute | solution.py:458
  59.1 1.7 %collective-permute-done.71.refs_1_ = bf16[8,32,256]{2,1,0:T(8,128)(2,1)S(1)} collective-permute-done((bf16[8,32,256]{2,1,0:T(8,128)(2,1)S(1)}, bf16[8,32,256]{2,1,0:T(8,128)(2,1)S(1)}, u32[]{:S(2)}, u32[]{:S(2)}) %collective-permute-start.71) | collective-permute-done | bytes 131104 | tf_op jit(solution)/shard_map/ppermute | solution.py:458
  60.8 1.5 collective-permute-start.76
  62.3 0.3 collective-permute-done.72.refs_2_
  62.6 1.4 collective-permute-start.77
  64.0 1.6 %collective-permute-done.73.refs_3_ = bf16[8,32,256]{2,1,0:T(8,128)(2,1)S(1)} collective-permute-done((bf16[8,32,256]{2,1,0:T(8,128)(2,1)}, bf16[8,32,256]{2,1,0:T(8,128)(2,1)S(1)}, u32[]{:S(2)}, u32[]{:S(2)}) %collective-permute-start.73) | collective-permute-done | bytes 131104 | tf_op jit(solution)/shard_map/ppermute | solution.py:458
  65.6 0.1 collective-permute-done.74.refs_4_
  65.7 0.3 collective-permute-done.75.refs_5_
  66.0 0.9 collective-permute-done.76.refs_6_
  66.9 1.3 collective-permute-done.77.refs_7_
  68.1 1.1 block_products.1.mine_ref
  69.3 0.1 collective-permute-start.78
  69.3 2.6 %collective-permute-done.78.other_ref = f32[1024,256]{1,0:T(8,128)S(1)} collective-permute-done((f32[1024,256]{1,0:T(8,128)S(1)}, f32[1024,256]{1,0:T(8,128)S(1)}, u32[]{:S(2)}, u32[]{:S(2)}) %collective-permute-start.78) | collective-permute-done | bytes 1048608 | tf_op jit(solution)/shard_map/ppermute | solution.py:521
  72.0 1.5 sum_and_gram.1
  73.5 1.1 collective-permute-start.79
  74.7 1.6 %collective-permute-start.80 = (f32[64,128]{1,0:T(8,128)S(1)}, f32[64,128]{1,0:T(8,128)S(1)}, u32[]{:S(2)}, u32[]{:S(2)}) collective-permute-start(f32[64,128]{1,0:T(8,128)S(1)} %get-tuple-element.289), channel_id=1, source_target_pairs={{0,4},{2,6},{4,0},{6,2},{8,12},{10,14},{12,8},{14,10},{16,20},{18,... | collective-permute-start | bytes 98312 | tf_op jit(solution)/shard_map/ppermute | solution.py:499
  76.3 0.8 collective-permute-start.81
  77.1 0.4 collective-permute-done.79
  77.5 1.1 collective-permute-done.80
  78.6 2.5 %collective-permute-done.81 = f32[64,128]{1,0:T(8,128)S(1)} collective-permute-done((f32[64,128]{1,0:T(8,128)S(1)}, f32[64,128]{1,0:T(8,128)S(1)}, u32[]{:S(2)}, u32[]{:S(2)}) %collective-permute-start.81) | collective-permute-done | bytes 32800 | tf_op jit(solution)/shard_map/ppermute | solution.py:499
  81.1 0.7 collective-permute-start.84
  81.8 3.8 %collective-permute-start.82 = (f32[64,128]{1,0:T(8,128)S(1)}, f32[64,128]{1,0:T(8,128)S(1)}, u32[]{:S(2)}, u32[]{:S(2)}) collective-permute-start(f32[64,128]{1,0:T(8,128)S(1)} %add_add_fusion.1), channel_id=1, source_target_pairs={{0,8},{2,10},{4,12},{6,14},{8,0},{10,2},{12,4},{14,6},{16,24},{18,... | collective-permute-start | bytes 98312 | tf_op jit(solution)/shard_map/ppermute | solution.py:499
  85.6 1.4 collective-permute-done.84
  87.0 0.5 collective-permute-done.82
  87.5 0.9 collective-permute-start.87
  88.4 1.3 collective-permute-start.86
  89.7 1.3 collective-permute-start.85
  91.0 1.4 collective-permute-done.87.refs_3_
  92.5 0.2 collective-permute-done.86.refs_2_
  92.7 1.0 collective-permute-done.85.refs_1_
  93.6 0.1 collective-permute-start.88
  93.7 1.3 collective-permute-done.88.refs_1_
  95.0 61.8 %factor_and_basis.1 = (f32[512,256]{1,0:T(8,128)}, f32[256,256]{1,0:T(8,128)}) custom-call(f32[256,128]{1,0:T(8,128)S(1)} %stack_quarters.1.refs_0_, f32[256,128]{1,0:T(8,128)S(1)} %collective-permute-done.88.refs_1_, f32[512,256]{1,0:T(8,128)S(1)} %get-tuple-element.291.refs_2_), custom_call_target="tpu_custom_call" | custom-call | tf_op jit(solution)/shard_map/factor_and_basis/pallas_call | solution.py:441
  (13 shorter events, 0.1 us)
Async XLA Ops:
  1.3 0.7 copy-start.3
  3.1 14.4 %all-to-all-start = ((s32[32,1,128]{2,1,0:T(1,128)}), s32[32,1,128]{2,1,0:T(1,128)S(1)}, u32[]{:S(2)}, u32[]{:S(2)}) async-start(s32[32,1,128]{2,1,0:T(1,128)} %table_copies.1), calls=%async_computation | async-start | bytes 32768 | tf_op jit(solution)/shard_map/all_to_all | solution.py:475
  10.4 1.6 %copy-start = (bf16[4096,256]{1,0:T(8,128)(2,1)S(1)}, bf16[4096,256]{1,0:T(8,128)(2,1)}, u32[]{:S(2)}) copy-start(bf16[4096,256]{1,0:T(8,128)(2,1)} %param.28) | copy-start | bytes 6291460
  20.8 8.4 %collective-permute-start.7 = (bf16[6,32,256]{2,1,0:T(8,128)(2,1)S(1)}, bf16[6,32,256]{2,1,0:T(8,128)(2,1)S(1)}, u32[]{:S(2)}, u32[]{:S(2)}) collective-permute-start(bf16[6,32,256]{2,1,0:T(8,128)(2,1)S(1)} %get-tuple-element.144), channel_id=1, source_target_pairs={{0,14},{2,12},{4,10},{6,8},{8,6},{10,4},{12,2},{14,0},{16,30},{18,... | collective-permute-start | bytes 294920 | tf_op jit(solution)/shard_map/cond/branch_1_fun/ppermute | solution.py:458
  21.4 8.7 %collective-permute-start.8 = (bf16[6,32,256]{2,1,0:T(8,128)(2,1)S(1)}, bf16[6,32,256]{2,1,0:T(8,128)(2,1)S(1)}, u32[]{:S(2)}, u32[]{:S(2)}) collective-permute-start(bf16[6,32,256]{2,1,0:T(8,128)(2,1)S(1)} %get-tuple-element.145), channel_id=1, source_target_pairs={{0,12},{2,14},{4,8},{6,10},{8,4},{10,6},{12,0},{14,2},{16,28},{18,... | collective-permute-start | bytes 294920 | tf_op jit(solution)/shard_map/cond/branch_1_fun/ppermute | solution.py:458
  23.7 7.9 %collective-permute-start.9 = (bf16[6,32,256]{2,1,0:T(8,128)(2,1)S(1)}, bf16[6,32,256]{2,1,0:T(8,128)(2,1)S(1)}, u32[]{:S(2)}, u32[]{:S(2)}) collective-permute-start(bf16[6,32,256]{2,1,0:T(8,128)(2,1)S(1)} %get-tuple-element.146), channel_id=1, source_target_pairs={{0,10},{2,8},{4,14},{6,12},{8,2},{10,0},{12,6},{14,4},{16,26},{18,... | collective-permute-start | bytes 294920 | tf_op jit(solution)/shard_map/cond/branch_1_fun/ppermute | solution.py:458
  25.2 8.0 %collective-permute-start.10 = (bf16[6,32,256]{2,1,0:T(8,128)(2,1)S(1)}, bf16[6,32,256]{2,1,0:T(8,128)(2,1)S(1)}, u32[]{:S(2)}, u32[]{:S(2)}) collective-permute-start(bf16[6,32,256]{2,1,0:T(8,128)(2,1)S(1)} %get-tuple-element.147), channel_id=1, source_target_pairs={{0,6},{2,4},{4,2},{6,0},{8,14},{10,12},{12,10},{14,8},{16,22},{18,... | collective-permute-start | bytes 294920 | tf_op jit(solution)/shard_map/cond/branch_1_fun/ppermute | solution.py:458
  25.8 7.4 %collective-permute-start.11 = (bf16[6,32,256]{2,1,0:T(8,128)(2,1)S(1)}, bf16[6,32,256]{2,1,0:T(8,128)(2,1)S(1)}, u32[]{:S(2)}, u32[]{:S(2)}) collective-permute-start(bf16[6,32,256]{2,1,0:T(8,128)(2,1)S(1)} %get-tuple-element.148), channel_id=1, source_target_pairs={{0,8},{2,10},{4,12},{6,14},{8,0},{10,2},{12,4},{14,6},{16,24},{18,... | collective-permute-start | bytes 294920 | tf_op jit(solution)/shard_map/cond/branch_1_fun/ppermute | solution.py:458
  29.1 4.9 %collective-permute-start.12 = (bf16[6,32,256]{2,1,0:T(8,128)(2,1)S(1)}, bf16[6,32,256]{2,1,0:T(8,128)(2,1)S(1)}, u32[]{:S(2)}, u32[]{:S(2)}) collective-permute-start(bf16[6,32,256]{2,1,0:T(8,128)(2,1)S(1)} %get-tuple-element.149), channel_id=1, source_target_pairs={{0,4},{2,6},{4,0},{6,2},{8,12},{10,14},{12,8},{14,10},{16,20},{18,... | collective-permute-start | bytes 294920 | tf_op jit(solution)/shard_map/cond/branch_1_fun/ppermute | solution.py:458
  30.2 4.6 %collective-permute-start.13 = (bf16[6,32,256]{2,1,0:T(8,128)(2,1)S(1)}, bf16[6,32,256]{2,1,0:T(8,128)(2,1)S(1)}, u32[]{:S(2)}, u32[]{:S(2)}) collective-permute-start(bf16[6,32,256]{2,1,0:T(8,128)(2,1)S(1)} %get-tuple-element.150), channel_id=1, source_target_pairs={{0,2},{2,0},{4,6},{6,4},{8,10},{10,8},{12,14},{14,12},{16,18},{18,... | collective-permute-start | bytes 294920 | tf_op jit(solution)/shard_map/cond/branch_1_fun/ppermute | solution.py:458
  34.9 33.2 %copy-start.1 = (bf16[8,256,256]{2,1,0:T(8,128)(2,1)S(1)}, bf16[8,256,256]{2,1,0:T(8,128)(2,1)}, u32[]{:S(2)}) copy-start(bf16[8,256,256]{2,1,0:T(8,128)(2,1)} %blocks_ref.1) | copy-start | bytes 3145732
  34.9 33.2 %copy-start.2 = (s32[8]{0:T(128)S(1)}, s32[8]{0:T(128)}, u32[]{:S(2)}) copy-start(s32[8]{0:T(128)} %rows_ref.1) | copy-start | bytes 100
  35.6 14.6 %collective-permute-start.64 = (bf16[19,32,256]{2,1,0:T(8,128)(2,1)S(1)}, bf16[19,32,256]{2,1,0:T(8,128)(2,1)S(1)}, u32[]{:S(2)}, u32[]{:S(2)}) collective-permute-start(bf16[19,32,256]{2,1,0:T(8,128)(2,1)S(1)} %listed_stripes.23), channel_id=1, source_target_pairs={{0,16},{2,18},{4,20},{6,22},{8,24},{10,26},{12,28},{14,30},{16,0},... | collective-permute-start | bytes 933896 | tf_op jit(solution)/shard_map/cond/branch_8_fun/ppermute | solution.py:489
  51.8 9.0 %collective-permute-start.71 = (bf16[8,32,256]{2,1,0:T(8,128)(2,1)S(1)}, bf16[8,32,256]{2,1,0:T(8,128)(2,1)S(1)}, u32[]{:S(2)}, u32[]{:S(2)}) collective-permute-start(bf16[8,32,256]{2,1,0:T(8,128)(2,1)S(1)} %get-tuple-element.280), channel_id=1, source_target_pairs={{0,14},{2,12},{4,10},{6,8},{8,6},{10,4},{12,2},{14,0},{16,30},{18,... | collective-permute-start | bytes 393224 | tf_op jit(solution)/shard_map/ppermute | solution.py:458
  51.8 10.8 %collective-permute-start.72 = (bf16[8,32,256]{2,1,0:T(8,128)(2,1)S(1)}, bf16[8,32,256]{2,1,0:T(8,128)(2,1)S(1)}, u32[]{:S(2)}, u32[]{:S(2)}) collective-permute-start(bf16[8,32,256]{2,1,0:T(8,128)(2,1)S(1)} %get-tuple-element.281), channel_id=1, source_target_pairs={{0,12},{2,14},{4,8},{6,10},{8,4},{10,6},{12,0},{14,2},{16,28},{18,... | collective-permute-start | bytes 393224 | tf_op jit(solution)/shard_map/ppermute | solution.py:458
  54.8 10.9 %collective-permute-start.73 = (bf16[8,32,256]{2,1,0:T(8,128)(2,1)}, bf16[8,32,256]{2,1,0:T(8,128)(2,1)S(1)}, u32[]{:S(2)}, u32[]{:S(2)}) collective-permute-start(bf16[8,32,256]{2,1,0:T(8,128)(2,1)} %get-tuple-element.282), channel_id=1, source_target_pairs={{0,10},{2,8},{4,14},{6,12},{8,2},{10,0},{12,6},{14,4},{16,26},{18,... | collective-permute-start | bytes 393224 | tf_op jit(solution)/shard_map/ppermute | solution.py:458
  55.7 10.0 %collective-permute-start.74 = (bf16[8,32,256]{2,1,0:T(8,128)(2,1)}, bf16[8,32,256]{2,1,0:T(8,128)(2,1)S(1)}, u32[]{:S(2)}, u32[]{:S(2)}) collective-permute-start(bf16[8,32,256]{2,1,0:T(8,128)(2,1)} %get-tuple-element.283), channel_id=1, source_target_pairs={{0,6},{2,4},{4,2},{6,0},{8,14},{10,12},{12,10},{14,8},{16,22},{18,... | collective-permute-start | bytes 393224 | tf_op jit(solution)/shard_map/ppermute | solution.py:458
  57.1 8.8 %collective-permute-start.75 = (bf16[8,32,256]{2,1,0:T(8,128)(2,1)}, bf16[8,32,256]{2,1,0:T(8,128)(2,1)S(1)}, u32[]{:S(2)}, u32[]{:S(2)}) collective-permute-start(bf16[8,32,256]{2,1,0:T(8,128)(2,1)} %get-tuple-element.284), channel_id=1, source_target_pairs={{0,8},{2,10},{4,12},{6,14},{8,0},{10,2},{12,4},{14,6},{16,24},{18,... | collective-permute-start | bytes 393224 | tf_op jit(solution)/shard_map/ppermute | solution.py:458
  60.8 6.1 %collective-permute-start.76 = (bf16[8,32,256]{2,1,0:T(8,128)(2,1)}, bf16[8,32,256]{2,1,0:T(8,128)(2,1)S(1)}, u32[]{:S(2)}, u32[]{:S(2)}) collective-permute-start(bf16[8,32,256]{2,1,0:T(8,128)(2,1)} %get-tuple-element.285), channel_id=1, source_target_pairs={{0,4},{2,6},{4,0},{6,2},{8,12},{10,14},{12,8},{14,10},{16,20},{18,... | collective-permute-start | bytes 393224 | tf_op jit(solution)/shard_map/ppermute | solution.py:458
  62.6 5.5 %collective-permute-start.77 = (bf16[8,32,256]{2,1,0:T(8,128)(2,1)}, bf16[8,32,256]{2,1,0:T(8,128)(2,1)S(1)}, u32[]{:S(2)}, u32[]{:S(2)}) collective-permute-start(bf16[8,32,256]{2,1,0:T(8,128)(2,1)} %get-tuple-element.286), channel_id=1, source_target_pairs={{0,2},{2,0},{4,6},{6,4},{8,10},{10,8},{12,14},{14,12},{16,18},{18,... | collective-permute-start | bytes 393224 | tf_op jit(solution)/shard_map/ppermute | solution.py:458
  69.3 2.7 %collective-permute-start.78 = (f32[1024,256]{1,0:T(8,128)S(1)}, f32[1024,256]{1,0:T(8,128)S(1)}, u32[]{:S(2)}, u32[]{:S(2)}) collective-permute-start(f32[1024,256]{1,0:T(8,128)S(1)} %block_products.1.mine_ref), channel_id=1, source_target_pairs={{0,1},{1,0},{2,3},{3,2},{4,5},{5,4},{6,7},{7,6},{8,9},{9,8},{10,11... | collective-permute-start | bytes 3145736 | tf_op jit(solution)/shard_map/ppermute | solution.py:521
  73.5 4.0 %collective-permute-start.79 = (f32[64,128]{1,0:T(8,128)S(1)}, f32[64,128]{1,0:T(8,128)S(1)}, u32[]{:S(2)}, u32[]{:S(2)}) collective-permute-start(f32[64,128]{1,0:T(8,128)S(1)} %get-tuple-element.288), channel_id=1, source_target_pairs={{0,2},{2,0},{4,6},{6,4},{8,10},{10,8},{12,14},{14,12},{16,18},{18,... | collective-permute-start | bytes 98312 | tf_op jit(solution)/shard_map/ppermute | solution.py:499
  74.7 3.9 %collective-permute-start.80 = (f32[64,128]{1,0:T(8,128)S(1)}, f32[64,128]{1,0:T(8,128)S(1)}, u32[]{:S(2)}, u32[]{:S(2)}) collective-permute-start(f32[64,128]{1,0:T(8,128)S(1)} %get-tuple-element.289), channel_id=1, source_target_pairs={{0,4},{2,6},{4,0},{6,2},{8,12},{10,14},{12,8},{14,10},{16,20},{18,... | collective-permute-start | bytes 98312 | tf_op jit(solution)/shard_map/ppermute | solution.py:499
  76.3 4.8 %collective-permute-start.81 = (f32[64,128]{1,0:T(8,128)S(1)}, f32[64,128]{1,0:T(8,128)S(1)}, u32[]{:S(2)}, u32[]{:S(2)}) collective-permute-start(f32[64,128]{1,0:T(8,128)S(1)} %get-tuple-element.290), channel_id=1, source_target_pairs={{0,6},{2,4},{4,2},{6,0},{8,14},{10,12},{12,10},{14,8},{16,22},{18,... | collective-permute-start | bytes 98312 | tf_op jit(solution)/shard_map/ppermute | solution.py:499
  81.1 5.8 %collective-permute-start.84 = (f32[64,128]{1,0:T(8,128)S(1)}, f32[64,128]{1,0:T(8,128)S(1)}, u32[]{:S(2)}, u32[]{:S(2)}) collective-permute-start(f32[64,128]{1,0:T(8,128)S(1)} %add_add_fusion.1), channel_id=1, source_target_pairs={{0,24},{2,26},{4,28},{6,30},{8,16},{10,18},{12,20},{14,22},{16,8},... | collective-permute-start | bytes 98312 | tf_op jit(solution)/shard_map/ppermute | solution.py:499
  81.8 5.2 %collective-permute-start.83 = (f32[64,128]{1,0:T(8,128)S(1)}, f32[64,128]{1,0:T(8,128)S(1)}, u32[]{:S(2)}, u32[]{:S(2)}) collective-permute-start(f32[64,128]{1,0:T(8,128)S(1)} %add_add_fusion.1), channel_id=1, source_target_pairs={{0,16},{2,18},{4,20},{6,22},{8,24},{10,26},{12,28},{14,30},{16,0},... | collective-permute-start | bytes 98312 | tf_op jit(solution)/shard_map/ppermute | solution.py:499
  81.8 5.7 %collective-permute-start.82 = (f32[64,128]{1,0:T(8,128)S(1)}, f32[64,128]{1,0:T(8,128)S(1)}, u32[]{:S(2)}, u32[]{:S(2)}) collective-permute-start(f32[64,128]{1,0:T(8,128)S(1)} %add_add_fusion.1), channel_id=1, source_target_pairs={{0,8},{2,10},{4,12},{6,14},{8,0},{10,2},{12,4},{14,6},{16,24},{18,... | collective-permute-start | bytes 98312 | tf_op jit(solution)/shard_map/ppermute | solution.py:499
  87.5 5.0 %collective-permute-start.87 = (f32[64,128]{1,0:T(8,128)S(1)}, f32[64,128]{1,0:T(8,128)S(1)}, u32[]{:S(2)}, u32[]{:S(2)}) collective-permute-start(f32[64,128]{1,0:T(8,128)S(1)} %add_add_fusion.refs_0_), channel_id=1, source_target_pairs={{0,6},{2,4},{4,2},{6,0},{8,14},{10,12},{12,10},{14,8},{16,22},{18,... | collective-permute-start | bytes 98312 | tf_op jit(solution)/shard_map/ppermute | solution.py:499
  88.4 4.3 %collective-permute-start.86 = (f32[64,128]{1,0:T(8,128)S(1)}, f32[64,128]{1,0:T(8,128)S(1)}, u32[]{:S(2)}, u32[]{:S(2)}) collective-permute-start(f32[64,128]{1,0:T(8,128)S(1)} %add_add_fusion.refs_0_), channel_id=1, source_target_pairs={{0,4},{2,6},{4,0},{6,2},{8,12},{10,14},{12,8},{14,10},{16,20},{18,... | collective-permute-start | bytes 98312 | tf_op jit(solution)/shard_map/ppermute | solution.py:499
  89.7 3.9 %collective-permute-start.85 = (f32[64,128]{1,0:T(8,128)S(1)}, f32[64,128]{1,0:T(8,128)S(1)}, u32[]{:S(2)}, u32[]{:S(2)}) collective-permute-start(f32[64,128]{1,0:T(8,128)S(1)} %add_add_fusion.refs_0_), channel_id=1, source_target_pairs={{0,2},{2,0},{4,6},{6,4},{8,10},{10,8},{12,14},{14,12},{16,18},{18,... | collective-permute-start | bytes 98312 | tf_op jit(solution)/shard_map/ppermute | solution.py:499
  93.6 1.4 collective-permute-start.88
where the time goes:
time: 155 us; the launch traced here: 157 us
  Pallas kernels  70 us (45%)
  waiting for transfers between devices  43.9 us (28%)
  starting transfers between devices  37.9 us (24%)
  between operations  2.7 us (2%)
  local copies, waits for them, and re-layouts  2.25 us (1%)
    pallas_call x1, Pallas kernels, factor_and_basis(): pl.pallas_call(functools.partial(factor_kernel, total_rows), out_shape=(j...  61.8 us
    ppermute x14, starting transfers between devices, exchange(): lax.ppermute(piece, 'rows', [(r, r ^ d) for r in range(rows)])  18.4 us
    ppermute x1, waiting for transfers between devices, run(): other = lax.ppermute(listed(lists, own, count), 'rows', swap)  14.1 us
    ppermute x14, waiting for transfers between devices, exchange(): lax.ppermute(piece, 'rows', [(r, r ^ d) for r in range(rows)])  12 us
    ppermute x9, starting transfers between devices, moved(): return lax.ppermute(piece, 'rows', [(r, r ^ d) for r in range(rows)])  11.6 us
    ppermute x9, waiting for transfers between devices, moved(): return lax.ppermute(piece, 'rows', [(r, r ^ d) for r in range(rows)])  8.49 us
    all_to_all x1, starting transfers between devices, fetch(): lax.all_to_all(table, ('rows', 'cols'), split_axis=0, concat_axis=0, tile...  7.3 us
    all_to_all x1, waiting for transfers between devices, fetch(): lax.all_to_all(table, ('rows', 'cols'), split_axis=0, concat_axis=0, tile...  5.34 us
  transfers between devices with their start and end apart: 27, of which 25 were waited for; matrix products, arithmetic and copies ran while one was open for 0% of the time, Pallas kernels for 0%

commit v1 on v0

--- a/solution.py
+++ b/solution.py
@@ -33,7 +33,6 @@
         out_shape=jax.ShapeDtypeStruct((devices, 1, 128), jnp.int32),
         in_specs=[SMEM, SMEM],
         out_specs=VMEM,
-        compiler_params=pltpu.CompilerParams(vmem_limit_bytes=24 * MIB),
         name="table_copies",
     )(block_cols, counts)
 
@@ -156,7 +155,12 @@
 
 
 def distances(members):
-    return [0, *sorted(range(1, members), key=lambda d: (-d.bit_count(), -d))]
+    order = [0]
+    for near in sorted(range(1, members), key=lambda d: (d.bit_count(), d)):
+        far = (members - 1) ^ near
+        if near not in order and far:
+            order += [near, far]
+    return [*order[:-2], members - 1, *order[-2:]] if members > 2 else list(range(members))
 
 
 def turn_kernel(sketch_ref, out_ref):
@@ -385,13 +389,14 @@
     up_across = 1.0 / across
     scaled[...] = gram * up_down * up_across
 
-    def refine(times, times_nt):
+    def refine(times, times_nt, last=False):
         w = inverse[...]
         upper = times(w, scaled[...])
         residual = times_nt(upper, w) - identity
         step = residual * half
         inverse[...] = w - matmul(step, w, lax.Precision.DEFAULT)
-        product[...] = upper - matmul(step, upper, lax.Precision.DEFAULT)
+        if last:
+            product[...] = upper - matmul(step, upper, lax.Precision.DEFAULT)
         return jnp.sum(residual * residual)
 
     def exactly(times):
@@ -406,7 +411,7 @@
         return (step < 8) & (size > 1e-6)
 
     def advance(state):
-        return state[0] + 1, refine(exactly(matmul), exactly(matmul_nt))
+        return state[0] + 1, refine(exactly(matmul), exactly(matmul_nt), last=True)
 
     _, size = lax.while_loop(going, advance, (jnp.int32(0), jnp.float32(1.0)))
 

time: 155 us -> 155 us (level); the launches traced: 157 us -> 155 us
  transfers between devices with their start and end apart: 27 -> 27, of which waited for: 25 -> 21; matrix products, arithmetic and copies ran while one was open for 0% -> 0% of each run, Pallas kernels for 0% -> 0%
where the time goes in v1:
time: 155 us
  Pallas kernels  70.1 us (45%)
  waiting for transfers between devices  43.3 us (28%)
  starting transfers between devices  37.1 us (24%)
  between operations  2.69 us (2%)
  local copies, waits for them, and re-layouts  1.6 us (1%)
    pallas_call x1, Pallas kernels, factor_and_basis(): pl.pallas_call(functools.partial(factor_kernel, total_rows), out_shape=(j...  61.8 us
    ppermute x14, starting transfers between devices, exchange(): lax.ppermute(piece, 'rows', [(r, r ^ d) for r in range(rows)])  17.6 us
    ppermute x1, waiting for transfers between devices, run(): other = lax.ppermute(listed(lists, own, count), 'rows', swap)  13.7 us
    ppermute x14, waiting for transfers between devices, exchange(): lax.ppermute(piece, 'rows', [(r, r ^ d) for r in range(rows)])  12.1 us
    ppermute x9, starting transfers between devices, moved(): return lax.ppermute(piece, 'rows', [(r, r ^ d) for r in range(rows)])  11.6 us
    ppermute x9, waiting for transfers between devices, moved(): return lax.ppermute(piece, 'rows', [(r, r ^ d) for r in range(rows)])  8.2 us
    all_to_all x1, starting transfers between devices, fetch(): lax.all_to_all(table, ('rows', 'cols'), split_axis=0, concat_axis=0, tile...  7.3 us
    all_to_all x1, waiting for transfers between devices, fetch(): lax.all_to_all(table, ('rows', 'cols'), split_axis=0, concat_axis=0, tile...  5.34 us
  transfers between devices with their start and end apart: 27, of which 21 were waited for; matrix products, arithmetic and copies ran while one was open for 0% of the time, Pallas kernels for 0%

profile of v1, /device:TPU:0, one launch (start us, length us, event | category | flops | bytes accessed | tf_op | source)
XLA Modules:
  0.0 155.0 jit_solution(2354269235756477063)
XLA Ops:
  1.3 1.3 table_copies.1
  2.6 7.3 %all-to-all-start = ((s32[32,1,128]{2,1,0:T(1,128)}), s32[32,1,128]{2,1,0:T(1,128)S(1)}, u32[]{:S(2)}, u32[]{:S(2)}) async-start(s32[32,1,128]{2,1,0:T(1,128)} %table_copies.1), calls=%async_computation | async-start | bytes 32768 | tf_op jit(solution)/shard_map/all_to_all | solution.py:480
  9.9 0.0 copy-start
  9.9 1.6 %copy-done = bf16[4096,256]{1,0:T(8,128)(2,1)S(1)} copy-done((bf16[4096,256]{1,0:T(8,128)(2,1)S(1)}, bf16[4096,256]{1,0:T(8,128)(2,1)}, u32[]{:S(2)}) %copy-start) | copy-done | bytes 2097176
  11.5 0.1 turn_stripes.1
  11.6 5.3 %all-to-all-done.table_ref = s32[32,1,128]{2,1,0:T(1,128)S(1)} async-done(((s32[32,1,128]{2,1,0:T(1,128)}), s32[32,1,128]{2,1,0:T(1,128)S(1)}, u32[]{:S(2)}, u32[]{:S(2)}) %all-to-all-start) | async-done | bytes 16416 | tf_op jit(solution)/shard_map/all_to_all | solution.py:480
  16.9 1.3 plan.1
  19.5 15.3 %conditional.2 = (bf16[128,32,256]{2,1,0:T(8,128)(2,1)S(1)}) conditional(s32[]{:T(128)} %bitcast.1, (s32[8,128]{1,0:T(8,128)S(1)}, bf16[8,16,32,256]{3,2,1,0:T(8,128)(2,1)S(1)}) %tuple.76, (s32[8,128]{1,0:T(8,128)S(1)}, bf16[8,16,32,256]{3,2,1,0:T(8,128)(2,1)S(1)}) %tuple.76, (s32[8,128]{1,0:T(8,128)S(1)}, ...), branch_computations={%region_0.0_spmd, %region_1.0_spmd, %region_2.0_spmd, %region_3.0_... | conditional | bytes 7340320 | solution.py:489
  19.6 0.7 cut_stripes.10
  20.2 0.6 collective-permute-start.14
  20.8 0.7 collective-permute-start.15
  21.5 1.4 collective-permute-start.16
  22.9 2.4 %collective-permute-start.17 = (bf16[7,32,256]{2,1,0:T(8,128)(2,1)S(1)}, bf16[7,32,256]{2,1,0:T(8,128)(2,1)S(1)}, u32[]{:S(2)}, u32[]{:S(2)}) collective-permute-start(bf16[7,32,256]{2,1,0:T(8,128)(2,1)S(1)} %get-tuple-element.157), channel_id=1, source_target_pairs={{0,10},{2,8},{4,14},{6,12},{8,2},{10,0},{12,6},{14,4},{16,26},{18,... | collective-permute-start | bytes 344072 | tf_op jit(solution)/shard_map/cond/branch_2_fun/ppermute | solution.py:463
  25.2 0.6 collective-permute-start.18
  25.9 0.0 collective-permute-done.14.refs_1_
  25.9 1.4 collective-permute-start.19
  27.3 0.4 collective-permute-done.15.refs_2_
  27.7 2.0 %collective-permute-start.20 = (bf16[7,32,256]{2,1,0:T(8,128)(2,1)S(1)}, bf16[7,32,256]{2,1,0:T(8,128)(2,1)S(1)}, u32[]{:S(2)}, u32[]{:S(2)}) collective-permute-start(bf16[7,32,256]{2,1,0:T(8,128)(2,1)S(1)} %get-tuple-element.160), channel_id=1, source_target_pairs={{0,6},{2,4},{4,2},{6,0},{8,14},{10,12},{12,10},{14,8},{16,22},{18,... | collective-permute-start | bytes 344072 | tf_op jit(solution)/shard_map/cond/branch_2_fun/ppermute | solution.py:463
  29.6 0.0 collective-permute-done.16.refs_3_
  29.6 0.6 collective-permute-done.17.refs_4_
  30.2 3.3 %collective-permute-done.18.refs_5_ = bf16[7,32,256]{2,1,0:T(8,128)(2,1)S(1)} collective-permute-done((bf16[7,32,256]{2,1,0:T(8,128)(2,1)S(1)}, bf16[7,32,256]{2,1,0:T(8,128)(2,1)S(1)}, u32[]{:S(2)}, u32[]{:S(2)}) %collective-permute-start.18) | collective-permute-done | bytes 114720 | tf_op jit(solution)/shard_map/cond/branch_2_fun/ppermute | solution.py:463
  33.5 1.2 collective-permute-done.20.refs_7_
  34.7 0.1 order_stripes.10
  34.8 0.0 copy-start.1
  34.8 0.0 copy-start.2
  34.8 16.5 %conditional.3 = ((bf16[8,32,256]{2,1,0:T(8,128)(2,1)S(1)}, bf16[8,32,256]{2,1,0:T(8,128)(2,1)S(1)}, bf16[8,32,256]{2,1,0:T(8,128)(2,1)S(1)}, bf16[8,32,256]{2,1...) conditional(s32[]{:T(128)} %bitcast, (s32[8,128]{1,0:T(8,128)S(1)}, ...), branch_computations={%region_8.0_spmd, %region_9.0_spmd, %region_10.0_spmd, %region_11.... | conditional | bytes 4194352 | solution.py:499
  34.9 0.6 listed_stripes.20
  35.5 0.5 collective-permute-start.61
  36.0 13.7 %collective-permute-done.61.other_ref = bf16[16,32,256]{2,1,0:T(8,128)(2,1)S(1)} collective-permute-done((bf16[16,32,256]{2,1,0:T(8,128)(2,1)S(1)}, bf16[16,32,256]{2,1,0:T(8,128)(2,1)S(1)}, u32[]{:S(2)}, u32[]{:S(2)}) %collective-permute-start.61) | collective-permute-done | bytes 262176 | tf_op jit(solution)/shard_map/cond/branch_5_fun/ppermute | solution.py:494
  49.7 1.6 %pick_stripes.20 = (bf16[8,32,256]{2,1,0:T(8,128)(2,1)S(1)}, bf16[8,32,256]{2,1,0:T(8,128)(2,1)S(1)}, bf16[8,32,256]{2,1,0:T(8,128)(2,1)S(1)}, bf16[8,32,256]{2,...) custom-call(s32[8,128]{1,0:T(8,128)S(1)} %get-tuple-element.226.plac, ...), custom_call_target="tpu_custom_call" | custom-call | tf_op jit(solution)/shard_map/cond/branch_5_fun/pick_stripes/pallas_call | solution.py:253
  51.3 0.5 collective-permute-start.73
  51.8 4.4 %collective-permute-start.74 = (bf16[8,32,256]{2,1,0:T(8,128)(2,1)}, bf16[8,32,256]{2,1,0:T(8,128)(2,1)S(1)}, u32[]{:S(2)}, u32[]{:S(2)}) collective-permute-start(bf16[8,32,256]{2,1,0:T(8,128)(2,1)} %get-tuple-element.283), channel_id=1, source_target_pairs={{0,10},{2,8},{4,14},{6,12},{8,2},{10,0},{12,6},{14,4},{16,26},{18,... | collective-permute-start | bytes 393224 | tf_op jit(solution)/shard_map/ppermute | solution.py:463
  56.3 0.0 collective-permute-done.71.refs_1_
  56.3 1.4 collective-permute-start.76
  57.7 0.8 collective-permute-done.72.refs_2_
  58.4 2.2 %collective-permute-start.77 = (bf16[8,32,256]{2,1,0:T(8,128)(2,1)}, bf16[8,32,256]{2,1,0:T(8,128)(2,1)S(1)}, u32[]{:S(2)}, u32[]{:S(2)}) collective-permute-start(bf16[8,32,256]{2,1,0:T(8,128)(2,1)} %get-tuple-element.286), channel_id=1, source_target_pairs={{0,6},{2,4},{4,2},{6,0},{8,14},{10,12},{12,10},{14,8},{16,22},{18,... | collective-permute-start | bytes 393224 | tf_op jit(solution)/shard_map/ppermute | solution.py:463
  60.7 1.2 collective-permute-done.74.refs_4_
  61.9 3.4 %collective-permute-done.75.refs_5_ = bf16[8,32,256]{2,1,0:T(8,128)(2,1)S(1)} collective-permute-done((bf16[8,32,256]{2,1,0:T(8,128)(2,1)}, bf16[8,32,256]{2,1,0:T(8,128)(2,1)S(1)}, u32[]{:S(2)}, u32[]{:S(2)}) %collective-permute-start.75) | collective-permute-done | bytes 131104 | tf_op jit(solution)/shard_map/ppermute | solution.py:463
  65.3 1.2 collective-permute-done.77.refs_7_
  66.6 1.1 block_products.1.mine_ref
  67.7 0.1 collective-permute-start.78
  67.8 2.6 %collective-permute-done.78.other_ref = f32[1024,256]{1,0:T(8,128)S(1)} collective-permute-done((f32[1024,256]{1,0:T(8,128)S(1)}, f32[1024,256]{1,0:T(8,128)S(1)}, u32[]{:S(2)}, u32[]{:S(2)}) %collective-permute-start.78) | collective-permute-done | bytes 1048608 | tf_op jit(solution)/shard_map/ppermute | solution.py:526
  70.5 1.5 sum_and_gram.1
  72.0 0.5 collective-permute-start.79
  72.5 0.9 collective-permute-start.80
  73.4 2.1 %collective-permute-start.81 = (f32[64,128]{1,0:T(8,128)S(1)}, f32[64,128]{1,0:T(8,128)S(1)}, u32[]{:S(2)}, u32[]{:S(2)}) collective-permute-start(f32[64,128]{1,0:T(8,128)S(1)} %get-tuple-element.290), channel_id=1, source_target_pairs={{0,6},{2,4},{4,2},{6,0},{8,14},{10,12},{12,10},{14,8},{16,22},{18,... | collective-permute-start | bytes 98312 | tf_op jit(solution)/shard_map/ppermute | solution.py:504
  75.6 0.4 collective-permute-done.79
  76.0 0.5 collective-permute-done.80
  76.5 1.8 %collective-permute-done.81 = f32[64,128]{1,0:T(8,128)S(1)} collective-permute-done((f32[64,128]{1,0:T(8,128)S(1)}, f32[64,128]{1,0:T(8,128)S(1)}, u32[]{:S(2)}, u32[]{:S(2)}) %collective-permute-start.81) | collective-permute-done | bytes 32800 | tf_op jit(solution)/shard_map/ppermute | solution.py:504
  78.3 1.4 collective-permute-start.84
  79.7 1.2 collective-permute-start.83
  80.9 1.8 %collective-permute-start.82 = (f32[64,128]{1,0:T(8,128)S(1)}, f32[64,128]{1,0:T(8,128)S(1)}, u32[]{:S(2)}, u32[]{:S(2)}) collective-permute-start(f32[64,128]{1,0:T(8,128)S(1)} %add_add_fusion.1), channel_id=1, source_target_pairs={{0,8},{2,10},{4,12},{6,14},{8,0},{10,2},{12,4},{14,6},{16,24},{18,... | collective-permute-start | bytes 98312 | tf_op jit(solution)/shard_map/ppermute | solution.py:504
  82.7 1.3 collective-permute-done.84
  84.0 0.7 collective-permute-done.83
  84.8 0.3 collective-permute-done.82
  85.1 2.1 %collective-permute-start.87 = (f32[64,128]{1,0:T(8,128)S(1)}, f32[64,128]{1,0:T(8,128)S(1)}, u32[]{:S(2)}, u32[]{:S(2)}) collective-permute-start(f32[64,128]{1,0:T(8,128)S(1)} %add_add_fusion.refs_0_), channel_id=1, source_target_pairs={{0,6},{2,4},{4,2},{6,0},{8,14},{10,12},{12,10},{14,8},{16,22},{18,... | collective-permute-start | bytes 98312 | tf_op jit(solution)/shard_map/ppermute | solution.py:504
  87.2 0.7 collective-permute-start.86
  87.9 0.8 collective-permute-start.85
  88.7 1.3 collective-permute-done.87.refs_3_
  90.0 1.1 collective-permute-done.86.refs_2_
  91.1 0.7 collective-permute-done.85.refs_1_
  91.8 0.1 collective-permute-start.88
  91.9 1.3 collective-permute-done.88.refs_1_
  93.2 61.8 %factor_and_basis.1 = (f32[512,256]{1,0:T(8,128)}, f32[256,256]{1,0:T(8,128)}) custom-call(f32[256,128]{1,0:T(8,128)S(1)} %stack_quarters.1.refs_0_, f32[256,128]{1,0:T(8,128)S(1)} %collective-permute-done.88.refs_1_, f32[512,256]{1,0:T(8,128)S(1)} %get-tuple-element.291.refs_2_), custom_call_target="tpu_custom_call" | custom-call | tf_op jit(solution)/shard_map/factor_and_basis/pallas_call | solution.py:446
  (11 shorter events, 0.1 us)
Async XLA Ops:
  2.6 14.4 %all-to-all-start = ((s32[32,1,128]{2,1,0:T(1,128)}), s32[32,1,128]{2,1,0:T(1,128)S(1)}, u32[]{:S(2)}, u32[]{:S(2)}) async-start(s32[32,1,128]{2,1,0:T(1,128)} %table_copies.1), calls=%async_computation | async-start | bytes 32768 | tf_op jit(solution)/shard_map/all_to_all | solution.py:480
  9.9 1.6 %copy-start = (bf16[4096,256]{1,0:T(8,128)(2,1)S(1)}, bf16[4096,256]{1,0:T(8,128)(2,1)}, u32[]{:S(2)}) copy-start(bf16[4096,256]{1,0:T(8,128)(2,1)} %param.28) | copy-start | bytes 6291460
  20.2 5.6 %collective-permute-start.14 = (bf16[7,32,256]{2,1,0:T(8,128)(2,1)S(1)}, bf16[7,32,256]{2,1,0:T(8,128)(2,1)S(1)}, u32[]{:S(2)}, u32[]{:S(2)}) collective-permute-start(bf16[7,32,256]{2,1,0:T(8,128)(2,1)S(1)} %get-tuple-element.154), channel_id=1, source_target_pairs={{0,2},{2,0},{4,6},{6,4},{8,10},{10,8},{12,14},{14,12},{16,18},{18,... | collective-permute-start | bytes 344072 | tf_op jit(solution)/shard_map/cond/branch_2_fun/ppermute | solution.py:463
  20.8 6.8 %collective-permute-start.15 = (bf16[7,32,256]{2,1,0:T(8,128)(2,1)S(1)}, bf16[7,32,256]{2,1,0:T(8,128)(2,1)S(1)}, u32[]{:S(2)}, u32[]{:S(2)}) collective-permute-start(bf16[7,32,256]{2,1,0:T(8,128)(2,1)S(1)} %get-tuple-element.155), channel_id=1, source_target_pairs={{0,12},{2,14},{4,8},{6,10},{8,4},{10,6},{12,0},{14,2},{16,28},{18,... | collective-permute-start | bytes 344072 | tf_op jit(solution)/shard_map/cond/branch_2_fun/ppermute | solution.py:463
  21.5 8.2 %collective-permute-start.16 = (bf16[7,32,256]{2,1,0:T(8,128)(2,1)S(1)}, bf16[7,32,256]{2,1,0:T(8,128)(2,1)S(1)}, u32[]{:S(2)}, u32[]{:S(2)}) collective-permute-start(bf16[7,32,256]{2,1,0:T(8,128)(2,1)S(1)} %get-tuple-element.156), channel_id=1, source_target_pairs={{0,4},{2,6},{4,0},{6,2},{8,12},{10,14},{12,8},{14,10},{16,20},{18,... | collective-permute-start | bytes 344072 | tf_op jit(solution)/shard_map/cond/branch_2_fun/ppermute | solution.py:463
  22.9 7.4 %collective-permute-start.17 = (bf16[7,32,256]{2,1,0:T(8,128)(2,1)S(1)}, bf16[7,32,256]{2,1,0:T(8,128)(2,1)S(1)}, u32[]{:S(2)}, u32[]{:S(2)}) collective-permute-start(bf16[7,32,256]{2,1,0:T(8,128)(2,1)S(1)} %get-tuple-element.157), channel_id=1, source_target_pairs={{0,10},{2,8},{4,14},{6,12},{8,2},{10,0},{12,6},{14,4},{16,26},{18,... | collective-permute-start | bytes 344072 | tf_op jit(solution)/shard_map/cond/branch_2_fun/ppermute | solution.py:463
  25.2 8.3 %collective-permute-start.18 = (bf16[7,32,256]{2,1,0:T(8,128)(2,1)S(1)}, bf16[7,32,256]{2,1,0:T(8,128)(2,1)S(1)}, u32[]{:S(2)}, u32[]{:S(2)}) collective-permute-start(bf16[7,32,256]{2,1,0:T(8,128)(2,1)S(1)} %get-tuple-element.158), channel_id=1, source_target_pairs={{0,14},{2,12},{4,10},{6,8},{8,6},{10,4},{12,2},{14,0},{16,30},{18,... | collective-permute-start | bytes 344072 | tf_op jit(solution)/shard_map/cond/branch_2_fun/ppermute | solution.py:463
  25.9 7.7 %collective-permute-start.19 = (bf16[7,32,256]{2,1,0:T(8,128)(2,1)S(1)}, bf16[7,32,256]{2,1,0:T(8,128)(2,1)S(1)}, u32[]{:S(2)}, u32[]{:S(2)}) collective-permute-start(bf16[7,32,256]{2,1,0:T(8,128)(2,1)S(1)} %get-tuple-element.159), channel_id=1, source_target_pairs={{0,8},{2,10},{4,12},{6,14},{8,0},{10,2},{12,4},{14,6},{16,24},{18,... | collective-permute-start | bytes 344072 | tf_op jit(solution)/shard_map/cond/branch_2_fun/ppermute | solution.py:463
  27.7 7.0 %collective-permute-start.20 = (bf16[7,32,256]{2,1,0:T(8,128)(2,1)S(1)}, bf16[7,32,256]{2,1,0:T(8,128)(2,1)S(1)}, u32[]{:S(2)}, u32[]{:S(2)}) collective-permute-start(bf16[7,32,256]{2,1,0:T(8,128)(2,1)S(1)} %get-tuple-element.160), channel_id=1, source_target_pairs={{0,6},{2,4},{4,2},{6,0},{8,14},{10,12},{12,10},{14,8},{16,22},{18,... | collective-permute-start | bytes 344072 | tf_op jit(solution)/shard_map/cond/branch_2_fun/ppermute | solution.py:463
  34.8 31.8 %copy-start.1 = (bf16[8,256,256]{2,1,0:T(8,128)(2,1)S(1)}, bf16[8,256,256]{2,1,0:T(8,128)(2,1)}, u32[]{:S(2)}) copy-start(bf16[8,256,256]{2,1,0:T(8,128)(2,1)} %blocks_ref.1) | copy-start | bytes 3145732
  34.8 31.8 %copy-start.2 = (s32[8]{0:T(128)S(1)}, s32[8]{0:T(128)}, u32[]{:S(2)}) copy-start(s32[8]{0:T(128)} %rows_ref.1) | copy-start | bytes 100
  35.5 14.2 %collective-permute-start.61 = (bf16[16,32,256]{2,1,0:T(8,128)(2,1)S(1)}, bf16[16,32,256]{2,1,0:T(8,128)(2,1)S(1)}, u32[]{:S(2)}, u32[]{:S(2)}) collective-permute-start(bf16[16,32,256]{2,1,0:T(8,128)(2,1)S(1)} %listed_stripes.20), channel_id=1, source_target_pairs={{0,16},{2,18},{4,20},{6,22},{8,24},{10,26},{12,28},{14,30},{16,0},... | collective-permute-start | bytes 786440 | tf_op jit(solution)/shard_map/cond/branch_5_fun/ppermute | solution.py:494
  51.3 5.0 %collective-permute-start.71 = (bf16[8,32,256]{2,1,0:T(8,128)(2,1)S(1)}, bf16[8,32,256]{2,1,0:T(8,128)(2,1)S(1)}, u32[]{:S(2)}, u32[]{:S(2)}) collective-permute-start(bf16[8,32,256]{2,1,0:T(8,128)(2,1)S(1)} %get-tuple-element.280), channel_id=1, source_target_pairs={{0,2},{2,0},{4,6},{6,4},{8,10},{10,8},{12,14},{14,12},{16,18},{18,... | collective-permute-start | bytes 393224 | tf_op jit(solution)/shard_map/ppermute | solution.py:463
  51.3 7.1 %collective-permute-start.72 = (bf16[8,32,256]{2,1,0:T(8,128)(2,1)S(1)}, bf16[8,32,256]{2,1,0:T(8,128)(2,1)S(1)}, u32[]{:S(2)}, u32[]{:S(2)}) collective-permute-start(bf16[8,32,256]{2,1,0:T(8,128)(2,1)S(1)} %get-tuple-element.281), channel_id=1, source_target_pairs={{0,12},{2,14},{4,8},{6,10},{8,4},{10,6},{12,0},{14,2},{16,28},{18,... | collective-permute-start | bytes 393224 | tf_op jit(solution)/shard_map/ppermute | solution.py:463
  51.3 9.3 %collective-permute-start.73 = (bf16[8,32,256]{2,1,0:T(8,128)(2,1)}, bf16[8,32,256]{2,1,0:T(8,128)(2,1)S(1)}, u32[]{:S(2)}, u32[]{:S(2)}) collective-permute-start(bf16[8,32,256]{2,1,0:T(8,128)(2,1)} %get-tuple-element.282), channel_id=1, source_target_pairs={{0,4},{2,6},{4,0},{6,2},{8,12},{10,14},{12,8},{14,10},{16,20},{18,... | collective-permute-start | bytes 393224 | tf_op jit(solution)/shard_map/ppermute | solution.py:463
  51.8 10.1 %collective-permute-start.74 = (bf16[8,32,256]{2,1,0:T(8,128)(2,1)}, bf16[8,32,256]{2,1,0:T(8,128)(2,1)S(1)}, u32[]{:S(2)}, u32[]{:S(2)}) collective-permute-start(bf16[8,32,256]{2,1,0:T(8,128)(2,1)} %get-tuple-element.283), channel_id=1, source_target_pairs={{0,10},{2,8},{4,14},{6,12},{8,2},{10,0},{12,6},{14,4},{16,26},{18,... | collective-permute-start | bytes 393224 | tf_op jit(solution)/shard_map/ppermute | solution.py:463
  56.3 9.1 %collective-permute-start.75 = (bf16[8,32,256]{2,1,0:T(8,128)(2,1)}, bf16[8,32,256]{2,1,0:T(8,128)(2,1)S(1)}, u32[]{:S(2)}, u32[]{:S(2)}) collective-permute-start(bf16[8,32,256]{2,1,0:T(8,128)(2,1)} %get-tuple-element.284), channel_id=1, source_target_pairs={{0,14},{2,12},{4,10},{6,8},{8,6},{10,4},{12,2},{14,0},{16,30},{18,... | collective-permute-start | bytes 393224 | tf_op jit(solution)/shard_map/ppermute | solution.py:463
  56.3 9.1 %collective-permute-start.76 = (bf16[8,32,256]{2,1,0:T(8,128)(2,1)}, bf16[8,32,256]{2,1,0:T(8,128)(2,1)S(1)}, u32[]{:S(2)}, u32[]{:S(2)}) collective-permute-start(bf16[8,32,256]{2,1,0:T(8,128)(2,1)} %get-tuple-element.285), channel_id=1, source_target_pairs={{0,8},{2,10},{4,12},{6,14},{8,0},{10,2},{12,4},{14,6},{16,24},{18,... | collective-permute-start | bytes 393224 | tf_op jit(solution)/shard_map/ppermute | solution.py:463
  58.4 8.2 %collective-permute-start.77 = (bf16[8,32,256]{2,1,0:T(8,128)(2,1)}, bf16[8,32,256]{2,1,0:T(8,128)(2,1)S(1)}, u32[]{:S(2)}, u32[]{:S(2)}) collective-permute-start(bf16[8,32,256]{2,1,0:T(8,128)(2,1)} %get-tuple-element.286), channel_id=1, source_target_pairs={{0,6},{2,4},{4,2},{6,0},{8,14},{10,12},{12,10},{14,8},{16,22},{18,... | collective-permute-start | bytes 393224 | tf_op jit(solution)/shard_map/ppermute | solution.py:463
  67.7 2.7 %collective-permute-start.78 = (f32[1024,256]{1,0:T(8,128)S(1)}, f32[1024,256]{1,0:T(8,128)S(1)}, u32[]{:S(2)}, u32[]{:S(2)}) collective-permute-start(f32[1024,256]{1,0:T(8,128)S(1)} %block_products.1.mine_ref), channel_id=1, source_target_pairs={{0,1},{1,0},{2,3},{3,2},{4,5},{5,4},{6,7},{7,6},{8,9},{9,8},{10,11... | collective-permute-start | bytes 3145736 | tf_op jit(solution)/shard_map/ppermute | solution.py:526
  72.0 4.0 %collective-permute-start.79 = (f32[64,128]{1,0:T(8,128)S(1)}, f32[64,128]{1,0:T(8,128)S(1)}, u32[]{:S(2)}, u32[]{:S(2)}) collective-permute-start(f32[64,128]{1,0:T(8,128)S(1)} %get-tuple-element.288), channel_id=1, source_target_pairs={{0,2},{2,0},{4,6},{6,4},{8,10},{10,8},{12,14},{14,12},{16,18},{18,... | collective-permute-start | bytes 98312 | tf_op jit(solution)/shard_map/ppermute | solution.py:504
  72.5 3.9 %collective-permute-start.80 = (f32[64,128]{1,0:T(8,128)S(1)}, f32[64,128]{1,0:T(8,128)S(1)}, u32[]{:S(2)}, u32[]{:S(2)}) collective-permute-start(f32[64,128]{1,0:T(8,128)S(1)} %get-tuple-element.289), channel_id=1, source_target_pairs={{0,4},{2,6},{4,0},{6,2},{8,12},{10,14},{12,8},{14,10},{16,20},{18,... | collective-permute-start | bytes 98312 | tf_op jit(solution)/shard_map/ppermute | solution.py:504
  73.4 4.8 %collective-permute-start.81 = (f32[64,128]{1,0:T(8,128)S(1)}, f32[64,128]{1,0:T(8,128)S(1)}, u32[]{:S(2)}, u32[]{:S(2)}) collective-permute-start(f32[64,128]{1,0:T(8,128)S(1)} %get-tuple-element.290), channel_id=1, source_target_pairs={{0,6},{2,4},{4,2},{6,0},{8,14},{10,12},{12,10},{14,8},{16,22},{18,... | collective-permute-start | bytes 98312 | tf_op jit(solution)/shard_map/ppermute | solution.py:504
  78.3 5.8 %collective-permute-start.84 = (f32[64,128]{1,0:T(8,128)S(1)}, f32[64,128]{1,0:T(8,128)S(1)}, u32[]{:S(2)}, u32[]{:S(2)}) collective-permute-start(f32[64,128]{1,0:T(8,128)S(1)} %add_add_fusion.1), channel_id=1, source_target_pairs={{0,24},{2,26},{4,28},{6,30},{8,16},{10,18},{12,20},{14,22},{16,8},... | collective-permute-start | bytes 98312 | tf_op jit(solution)/shard_map/ppermute | solution.py:504
  79.7 5.1 %collective-permute-start.83 = (f32[64,128]{1,0:T(8,128)S(1)}, f32[64,128]{1,0:T(8,128)S(1)}, u32[]{:S(2)}, u32[]{:S(2)}) collective-permute-start(f32[64,128]{1,0:T(8,128)S(1)} %add_add_fusion.1), channel_id=1, source_target_pairs={{0,16},{2,18},{4,20},{6,22},{8,24},{10,26},{12,28},{14,30},{16,0},... | collective-permute-start | bytes 98312 | tf_op jit(solution)/shard_map/ppermute | solution.py:504
  80.9 4.2 %collective-permute-start.82 = (f32[64,128]{1,0:T(8,128)S(1)}, f32[64,128]{1,0:T(8,128)S(1)}, u32[]{:S(2)}, u32[]{:S(2)}) collective-permute-start(f32[64,128]{1,0:T(8,128)S(1)} %add_add_fusion.1), channel_id=1, source_target_pairs={{0,8},{2,10},{4,12},{6,14},{8,0},{10,2},{12,4},{14,6},{16,24},{18,... | collective-permute-start | bytes 98312 | tf_op jit(solution)/shard_map/ppermute | solution.py:504
  85.1 4.9 %collective-permute-start.87 = (f32[64,128]{1,0:T(8,128)S(1)}, f32[64,128]{1,0:T(8,128)S(1)}, u32[]{:S(2)}, u32[]{:S(2)}) collective-permute-start(f32[64,128]{1,0:T(8,128)S(1)} %add_add_fusion.refs_0_), channel_id=1, source_target_pairs={{0,6},{2,4},{4,2},{6,0},{8,14},{10,12},{12,10},{14,8},{16,22},{18,... | collective-permute-start | bytes 98312 | tf_op jit(solution)/shard_map/ppermute | solution.py:504
  87.2 3.9 %collective-permute-start.86 = (f32[64,128]{1,0:T(8,128)S(1)}, f32[64,128]{1,0:T(8,128)S(1)}, u32[]{:S(2)}, u32[]{:S(2)}) collective-permute-start(f32[64,128]{1,0:T(8,128)S(1)} %add_add_fusion.refs_0_), channel_id=1, source_target_pairs={{0,4},{2,6},{4,0},{6,2},{8,12},{10,14},{12,8},{14,10},{16,20},{18,... | collective-permute-start | bytes 98312 | tf_op jit(solution)/shard_map/ppermute | solution.py:504
  87.9 3.9 %collective-permute-start.85 = (f32[64,128]{1,0:T(8,128)S(1)}, f32[64,128]{1,0:T(8,128)S(1)}, u32[]{:S(2)}, u32[]{:S(2)}) collective-permute-start(f32[64,128]{1,0:T(8,128)S(1)} %add_add_fusion.refs_0_), channel_id=1, source_target_pairs={{0,2},{2,0},{4,6},{6,4},{8,10},{10,8},{12,14},{14,12},{16,18},{18,... | collective-permute-start | bytes 98312 | tf_op jit(solution)/shard_map/ppermute | solution.py:504
  91.8 1.4 collective-permute-start.88

commit v2 on v1

--- a/solution.py
+++ b/solution.py
@@ -326,6 +326,22 @@
     )(mine, other)
 
 
+def add_kernel(*refs):
+    *piece_refs, out_ref = refs
+    out_ref[...] = functools.reduce(jnp.add, [ref[...] for ref in piece_refs])
+
+
+def add(pieces):
+    return pl.pallas_call(
+        add_kernel,
+        out_shape=jax.ShapeDtypeStruct(pieces[0].shape, jnp.float32),
+        in_specs=[VMEM] * len(pieces),
+        out_specs=VMEM,
+        compiler_params=pltpu.CompilerParams(vmem_limit_bytes=24 * MIB),
+        name="add_pieces",
+    )(*pieces)
+
+
 def stack_kernel(*refs):
     *quarter_refs, out_ref = refs
     me = lax.axis_index("rows") % len(quarter_refs)
@@ -505,9 +521,7 @@
 
 
 def gram_halves(quarters, rows):
-    first, *rest = quarters
-    for d, quarter in enumerate(rest):
-        first = first + moved(quarter, rows, d + 1)
+    first = add([quarters[0]] + [moved(quarters[d], rows, d) for d in (3, 1, 2)])
     total = (first + moved(first, rows, 4)) + (moved(first, rows, 8) + moved(first, rows, 12))
     half = stack([total] + [moved(total, rows, d) for d in range(1, 4)])
     return half, lax.ppermute(half, "cols", [(0, 1), (1, 0)])

time: 155 us -> 153 us (0.987); the launches traced: 155 us -> 151 us
  waiting for transfers between devices: 43.3 us -> 38.1 us
  starting transfers between devices: 37.1 us -> 38.9 us
    ppermute x14, waiting for transfers between devices: 12.1 us -> 8.94 us  [exchange(): lax.ppermute(piece, 'rows', [(r, r ^ d) for r in range(rows)])]
    ppermute x1, waiting for transfers between devices: 13.7 us -> 11.4 us  [run(): other = lax.ppermute(listed(lists, own, count), 'rows', swap)]
    ppermute x14, starting transfers between devices: 17.6 us -> 19.3 us  [exchange(): lax.ppermute(piece, 'rows', [(r, r ^ d) for r in range(rows)])]
  transfers between devices with their start and end apart: 27 -> 27, of which waited for: 21 -> 19; matrix products, arithmetic and copies ran while one was open for 0% -> 0% of each run, Pallas kernels for 0% -> 0%
where the time goes in v2:
time: 153 us; the launch traced here: 151 us
  Pallas kernels  70.1 us (46%)
  starting transfers between devices  38.9 us (25%)
  waiting for transfers between devices  38.1 us (25%)
  between operations  2.69 us (2%)
  local copies, waits for them, and re-layouts  1.6 us (1%)
    pallas_call x1, Pallas kernels, factor_and_basis(): pl.pallas_call(functools.partial(factor_kernel, total_rows), out_shape=(j...  61.8 us
    ppermute x14, starting transfers between devices, exchange(): lax.ppermute(piece, 'rows', [(r, r ^ d) for r in range(rows)])  19.3 us
    ppermute x9, starting transfers between devices, moved(): return lax.ppermute(piece, 'rows', [(r, r ^ d) for r in range(rows)])  11.6 us
    ppermute x1, waiting for transfers between devices, run(): other = lax.ppermute(listed(lists, own, count), 'rows', swap)  11.4 us
    ppermute x14, waiting for transfers between devices, exchange(): lax.ppermute(piece, 'rows', [(r, r ^ d) for r in range(rows)])  8.94 us
    ppermute x9, waiting for transfers between devices, moved(): return lax.ppermute(piece, 'rows', [(r, r ^ d) for r in range(rows)])  8.41 us
    all_to_all x1, starting transfers between devices, fetch(): lax.all_to_all(table, ('rows', 'cols'), split_axis=0, concat_axis=0, tile...  7.3 us
    all_to_all x1, waiting for transfers between devices, fetch(): lax.all_to_all(table, ('rows', 'cols'), split_axis=0, concat_axis=0, tile...  5.34 us
  transfers between devices with their start and end apart: 27, of which 19 were waited for; matrix products, arithmetic and copies ran while one was open for 0% of the time, Pallas kernels for 0%

profile of v2, /device:TPU:0, one launch (start us, length us, event | category | flops | bytes accessed | tf_op | source)
XLA Modules:
  0.0 151.5 jit_solution(895812086702329353)
XLA Ops:
  1.3 1.3 table_copies.1
  2.6 7.3 %all-to-all-start = ((s32[32,1,128]{2,1,0:T(1,128)}), s32[32,1,128]{2,1,0:T(1,128)S(1)}, u32[]{:S(2)}, u32[]{:S(2)}) async-start(s32[32,1,128]{2,1,0:T(1,128)} %table_copies.1), calls=%async_computation | async-start | bytes 32768 | tf_op jit(solution)/shard_map/all_to_all | solution.py:496
  9.9 0.0 copy-start
  9.9 1.6 %copy-done = bf16[4096,256]{1,0:T(8,128)(2,1)S(1)} copy-done((bf16[4096,256]{1,0:T(8,128)(2,1)S(1)}, bf16[4096,256]{1,0:T(8,128)(2,1)}, u32[]{:S(2)}) %copy-start) | copy-done | bytes 2097176
  11.5 0.1 turn_stripes.1
  11.6 5.3 %all-to-all-done.table_ref = s32[32,1,128]{2,1,0:T(1,128)S(1)} async-done(((s32[32,1,128]{2,1,0:T(1,128)}), s32[32,1,128]{2,1,0:T(1,128)S(1)}, u32[]{:S(2)}, u32[]{:S(2)}) %all-to-all-start) | async-done | bytes 16416 | tf_op jit(solution)/shard_map/all_to_all | solution.py:496
  16.9 1.3 plan.1
  19.5 13.9 %conditional.2 = (bf16[128,32,256]{2,1,0:T(8,128)(2,1)S(1)}) conditional(s32[]{:T(128)} %bitcast.1, (s32[8,128]{1,0:T(8,128)S(1)}, bf16[8,16,32,256]{3,2,1,0:T(8,128)(2,1)S(1)}) %tuple.76, (s32[8,128]{1,0:T(8,128)S(1)}, bf16[8,16,32,256]{3,2,1,0:T(8,128)(2,1)S(1)}) %tuple.76, (s32[8,128]{1,0:T(8,128)S(1)}, ...), branch_computations={%region_0.0_spmd, %region_1.0_spmd, %region_2.0_spmd, %region_3.0_... | conditional | bytes 7340320 | solution.py:505
  19.6 0.7 cut_stripes.9
  20.2 0.6 collective-permute-start.7
  20.8 0.7 collective-permute-start.8
  21.5 1.4 collective-permute-start.9
  22.9 2.4 %collective-permute-start.10 = (bf16[6,32,256]{2,1,0:T(8,128)(2,1)S(1)}, bf16[6,32,256]{2,1,0:T(8,128)(2,1)S(1)}, u32[]{:S(2)}, u32[]{:S(2)}) collective-permute-start(bf16[6,32,256]{2,1,0:T(8,128)(2,1)S(1)} %get-tuple-element.147), channel_id=1, source_target_pairs={{0,10},{2,8},{4,14},{6,12},{8,2},{10,0},{12,6},{14,4},{16,26},{18,... | collective-permute-start | bytes 294920 | tf_op jit(solution)/shard_map/cond/branch_1_fun/ppermute | solution.py:479
  25.2 0.6 collective-permute-start.11
  25.9 1.4 collective-permute-start.12
  27.3 2.3 %collective-permute-start.13 = (bf16[6,32,256]{2,1,0:T(8,128)(2,1)S(1)}, bf16[6,32,256]{2,1,0:T(8,128)(2,1)S(1)}, u32[]{:S(2)}, u32[]{:S(2)}) collective-permute-start(bf16[6,32,256]{2,1,0:T(8,128)(2,1)S(1)} %get-tuple-element.150), channel_id=1, source_target_pairs={{0,6},{2,4},{4,2},{6,0},{8,14},{10,12},{12,10},{14,8},{16,22},{18,... | collective-permute-start | bytes 294920 | tf_op jit(solution)/shard_map/cond/branch_1_fun/ppermute | solution.py:479
  29.6 2.6 %collective-permute-done.11.refs_5_ = bf16[6,32,256]{2,1,0:T(8,128)(2,1)S(1)} collective-permute-done((bf16[6,32,256]{2,1,0:T(8,128)(2,1)S(1)}, bf16[6,32,256]{2,1,0:T(8,128)(2,1)S(1)}, u32[]{:S(2)}, u32[]{:S(2)}) %collective-permute-start.11) | collective-permute-done | bytes 98336 | tf_op jit(solution)/shard_map/cond/branch_1_fun/ppermute | solution.py:479
  32.3 1.1 collective-permute-done.13.refs_7_
  33.3 0.1 order_stripes.9
  33.4 0.0 copy-start.1
  33.4 0.0 copy-start.2
  33.4 14.2 %conditional.3 = ((bf16[8,32,256]{2,1,0:T(8,128)(2,1)S(1)}, bf16[8,32,256]{2,1,0:T(8,128)(2,1)S(1)}, bf16[8,32,256]{2,1,0:T(8,128)(2,1)S(1)}, bf16[8,32,256]{2,1...) conditional(s32[]{:T(128)} %bitcast, (s32[8,128]{1,0:T(8,128)S(1)}, ...), branch_computations={%region_8.0_spmd, %region_9.0_spmd, %region_10.0_spmd, %region_11.... | conditional | bytes 4194352 | solution.py:515
  33.5 0.6 listed_stripes.18
  34.1 0.5 collective-permute-start.59
  34.6 11.4 %collective-permute-done.59.other_ref = bf16[14,32,256]{2,1,0:T(8,128)(2,1)S(1)} collective-permute-done((bf16[14,32,256]{2,1,0:T(8,128)(2,1)S(1)}, bf16[14,32,256]{2,1,0:T(8,128)(2,1)S(1)}, u32[]{:S(2)}, u32[]{:S(2)}) %collective-permute-start.59) | collective-permute-done | bytes 229408 | tf_op jit(solution)/shard_map/cond/branch_3_fun/ppermute | solution.py:510
  46.0 1.6 %pick_stripes.18 = (bf16[8,32,256]{2,1,0:T(8,128)(2,1)S(1)}, bf16[8,32,256]{2,1,0:T(8,128)(2,1)S(1)}, bf16[8,32,256]{2,1,0:T(8,128)(2,1)S(1)}, bf16[8,32,256]{2,...) custom-call(s32[8,128]{1,0:T(8,128)S(1)} %get-tuple-element.220.plac, ...), custom_call_target="tpu_custom_call" | custom-call | tf_op jit(solution)/shard_map/cond/branch_3_fun/pick_stripes/pallas_call | solution.py:253
  47.6 0.7 collective-permute-start.71
  48.3 0.0 collective-permute-start.72
  48.3 1.5 %collective-permute-start.73 = (bf16[8,32,256]{2,1,0:T(8,128)(2,1)}, bf16[8,32,256]{2,1,0:T(8,128)(2,1)S(1)}, u32[]{:S(2)}, u32[]{:S(2)}) collective-permute-start(bf16[8,32,256]{2,1,0:T(8,128)(2,1)} %get-tuple-element.282), channel_id=1, source_target_pairs={{0,4},{2,6},{4,0},{6,2},{8,12},{10,14},{12,8},{14,10},{16,20},{18,... | collective-permute-start | bytes 393224 | tf_op jit(solution)/shard_map/ppermute | solution.py:479
  49.9 2.7 %collective-permute-start.74 = (bf16[8,32,256]{2,1,0:T(8,128)(2,1)}, bf16[8,32,256]{2,1,0:T(8,128)(2,1)S(1)}, u32[]{:S(2)}, u32[]{:S(2)}) collective-permute-start(bf16[8,32,256]{2,1,0:T(8,128)(2,1)} %get-tuple-element.283), channel_id=1, source_target_pairs={{0,10},{2,8},{4,14},{6,12},{8,2},{10,0},{12,6},{14,4},{16,26},{18,... | collective-permute-start | bytes 393224 | tf_op jit(solution)/shard_map/ppermute | solution.py:479
  52.6 0.6 collective-permute-start.75
  53.1 0.0 collective-permute-done.71.refs_1_
  53.1 2.6 %collective-permute-start.76 = (bf16[8,32,256]{2,1,0:T(8,128)(2,1)}, bf16[8,32,256]{2,1,0:T(8,128)(2,1)S(1)}, u32[]{:S(2)}, u32[]{:S(2)}) collective-permute-start(bf16[8,32,256]{2,1,0:T(8,128)(2,1)} %get-tuple-element.285), channel_id=1, source_target_pairs={{0,8},{2,10},{4,12},{6,14},{8,0},{10,2},{12,4},{14,6},{16,24},{18,... | collective-permute-start | bytes 393224 | tf_op jit(solution)/shard_map/ppermute | solution.py:479
  55.7 0.0 collective-permute-done.72.refs_2_
  55.7 1.8 %collective-permute-start.77 = (bf16[8,32,256]{2,1,0:T(8,128)(2,1)}, bf16[8,32,256]{2,1,0:T(8,128)(2,1)S(1)}, u32[]{:S(2)}, u32[]{:S(2)}) collective-permute-start(bf16[8,32,256]{2,1,0:T(8,128)(2,1)} %get-tuple-element.286), channel_id=1, source_target_pairs={{0,6},{2,4},{4,2},{6,0},{8,14},{10,12},{12,10},{14,8},{16,22},{18,... | collective-permute-start | bytes 393224 | tf_op jit(solution)/shard_map/ppermute | solution.py:479
  57.6 1.3 collective-permute-done.74.refs_4_
  58.9 2.5 %collective-permute-done.75.refs_5_ = bf16[8,32,256]{2,1,0:T(8,128)(2,1)S(1)} collective-permute-done((bf16[8,32,256]{2,1,0:T(8,128)(2,1)}, bf16[8,32,256]{2,1,0:T(8,128)(2,1)S(1)}, u32[]{:S(2)}, u32[]{:S(2)}) %collective-permute-start.75) | collective-permute-done | bytes 131104 | tf_op jit(solution)/shard_map/ppermute | solution.py:479
  61.4 1.0 collective-permute-done.76.refs_6_
  62.4 0.4 collective-permute-done.77.refs_7_
  62.8 1.1 block_products.1.mine_ref
  64.0 0.1 collective-permute-start.78
  64.1 2.6 %collective-permute-done.78.other_ref = f32[1024,256]{1,0:T(8,128)S(1)} collective-permute-done((f32[1024,256]{1,0:T(8,128)S(1)}, f32[1024,256]{1,0:T(8,128)S(1)}, u32[]{:S(2)}, u32[]{:S(2)}) %collective-permute-start.78) | collective-permute-done | bytes 1048608 | tf_op jit(solution)/shard_map/ppermute | solution.py:540
  66.7 1.5 %sum_and_gram.1 = (f32[512,256]{1,0:T(8,128)S(1)}, f32[64,128]{1,0:T(8,128)S(1)}, f32[64,128]{1,0:T(8,128)S(1)}, f32[64,128]{1,0:T(8,128)S(1)}, f32[64,128]{1,0:T(8,128)S(1)}) custom-call(f32[1024,256]{1,0:T(8,128)S(1)} %block_products.1.mine_ref, f32[1024,256]{1,0:T(8,128)S(1)} %collective-permute-done.78.other_ref), custom_call_target="tpu_custom_call" | custom-call | tf_op jit(solution)/shard_map/sum_and_gram/pallas_call | solution.py:315
  68.2 1.9 %collective-permute-start.79 = (f32[64,128]{1,0:T(8,128)S(1)}, f32[64,128]{1,0:T(8,128)S(1)}, u32[]{:S(2)}, u32[]{:S(2)}) collective-permute-start(f32[64,128]{1,0:T(8,128)S(1)} %get-tuple-element.288), channel_id=1, source_target_pairs={{0,6},{2,4},{4,2},{6,0},{8,14},{10,12},{12,10},{14,8},{16,22},{18,... | collective-permute-start | bytes 98312 | tf_op jit(solution)/shard_map/ppermute | solution.py:520
  70.2 1.1 collective-permute-start.80
  71.3 0.5 collective-permute-start.81
  71.8 1.3 collective-permute-done.79.refs_1_
  73.1 0.9 collective-permute-done.80.refs_2_
  74.1 1.1 collective-permute-done.81.refs_3_
  75.2 1.0 collective-permute-start.84
  76.2 0.7 collective-permute-start.83
  76.9 2.7 %collective-permute-start.82 = (f32[64,128]{1,0:T(8,128)S(1)}, f32[64,128]{1,0:T(8,128)S(1)}, u32[]{:S(2)}, u32[]{:S(2)}) collective-permute-start(f32[64,128]{1,0:T(8,128)S(1)} %add_pieces.1), channel_id=1, source_target_pairs={{0,8},{2,10},{4,12},{6,14},{8,0},{10,2},{12,4},{14,6},{16,24},{18,... | collective-permute-start | bytes 98312 | tf_op jit(solution)/shard_map/ppermute | solution.py:520
  79.7 1.4 collective-permute-done.84
  81.0 0.8 collective-permute-done.83
  81.8 0.1 collective-permute-done.82
  81.9 1.3 collective-permute-start.87
  83.2 1.1 collective-permute-start.86
  84.3 1.1 collective-permute-start.85
  85.4 1.3 collective-permute-done.87.refs_3_
  86.7 0.4 collective-permute-done.86.refs_2_
  87.1 1.1 collective-permute-done.85.refs_1_
  88.3 0.1 collective-permute-start.88
  88.3 1.3 collective-permute-done.88.refs_1_
  89.7 61.8 %factor_and_basis.1 = (f32[512,256]{1,0:T(8,128)}, f32[256,256]{1,0:T(8,128)}) custom-call(f32[256,128]{1,0:T(8,128)S(1)} %stack_quarters.1.refs_0_, f32[256,128]{1,0:T(8,128)S(1)} %collective-permute-done.88.refs_1_, f32[512,256]{1,0:T(8,128)S(1)} %get-tuple-element.291.refs_2_), custom_call_target="tpu_custom_call" | custom-call | tf_op jit(solution)/shard_map/factor_and_basis/pallas_call | solution.py:462
  (11 shorter events, 0.1 us)
Async XLA Ops:
  2.6 14.4 %all-to-all-start = ((s32[32,1,128]{2,1,0:T(1,128)}), s32[32,1,128]{2,1,0:T(1,128)S(1)}, u32[]{:S(2)}, u32[]{:S(2)}) async-start(s32[32,1,128]{2,1,0:T(1,128)} %table_copies.1), calls=%async_computation | async-start | bytes 32768 | tf_op jit(solution)/shard_map/all_to_all | solution.py:496
  9.9 1.6 %copy-start = (bf16[4096,256]{1,0:T(8,128)(2,1)S(1)}, bf16[4096,256]{1,0:T(8,128)(2,1)}, u32[]{:S(2)}) copy-start(bf16[4096,256]{1,0:T(8,128)(2,1)} %param.28) | copy-start | bytes 6291460
  20.2 5.6 %collective-permute-start.7 = (bf16[6,32,256]{2,1,0:T(8,128)(2,1)S(1)}, bf16[6,32,256]{2,1,0:T(8,128)(2,1)S(1)}, u32[]{:S(2)}, u32[]{:S(2)}) collective-permute-start(bf16[6,32,256]{2,1,0:T(8,128)(2,1)S(1)} %get-tuple-element.144), channel_id=1, source_target_pairs={{0,2},{2,0},{4,6},{6,4},{8,10},{10,8},{12,14},{14,12},{16,18},{18,... | collective-permute-start | bytes 294920 | tf_op jit(solution)/shard_map/cond/branch_1_fun/ppermute | solution.py:479
  20.8 6.5 %collective-permute-start.8 = (bf16[6,32,256]{2,1,0:T(8,128)(2,1)S(1)}, bf16[6,32,256]{2,1,0:T(8,128)(2,1)S(1)}, u32[]{:S(2)}, u32[]{:S(2)}) collective-permute-start(bf16[6,32,256]{2,1,0:T(8,128)(2,1)S(1)} %get-tuple-element.145), channel_id=1, source_target_pairs={{0,12},{2,14},{4,8},{6,10},{8,4},{10,6},{12,0},{14,2},{16,28},{18,... | collective-permute-start | bytes 294920 | tf_op jit(solution)/shard_map/cond/branch_1_fun/ppermute | solution.py:479
  21.5 8.2 %collective-permute-start.9 = (bf16[6,32,256]{2,1,0:T(8,128)(2,1)S(1)}, bf16[6,32,256]{2,1,0:T(8,128)(2,1)S(1)}, u32[]{:S(2)}, u32[]{:S(2)}) collective-permute-start(bf16[6,32,256]{2,1,0:T(8,128)(2,1)S(1)} %get-tuple-element.146), channel_id=1, source_target_pairs={{0,4},{2,6},{4,0},{6,2},{8,12},{10,14},{12,8},{14,10},{16,20},{18,... | collective-permute-start | bytes 294920 | tf_op jit(solution)/shard_map/cond/branch_1_fun/ppermute | solution.py:479
  22.9 6.8 %collective-permute-start.10 = (bf16[6,32,256]{2,1,0:T(8,128)(2,1)S(1)}, bf16[6,32,256]{2,1,0:T(8,128)(2,1)S(1)}, u32[]{:S(2)}, u32[]{:S(2)}) collective-permute-start(bf16[6,32,256]{2,1,0:T(8,128)(2,1)S(1)} %get-tuple-element.147), channel_id=1, source_target_pairs={{0,10},{2,8},{4,14},{6,12},{8,2},{10,0},{12,6},{14,4},{16,26},{18,... | collective-permute-start | bytes 294920 | tf_op jit(solution)/shard_map/cond/branch_1_fun/ppermute | solution.py:479
  25.2 7.0 %collective-permute-start.11 = (bf16[6,32,256]{2,1,0:T(8,128)(2,1)S(1)}, bf16[6,32,256]{2,1,0:T(8,128)(2,1)S(1)}, u32[]{:S(2)}, u32[]{:S(2)}) collective-permute-start(bf16[6,32,256]{2,1,0:T(8,128)(2,1)S(1)} %get-tuple-element.148), channel_id=1, source_target_pairs={{0,14},{2,12},{4,10},{6,8},{8,6},{10,4},{12,2},{14,0},{16,30},{18,... | collective-permute-start | bytes 294920 | tf_op jit(solution)/shard_map/cond/branch_1_fun/ppermute | solution.py:479
  25.9 6.4 %collective-permute-start.12 = (bf16[6,32,256]{2,1,0:T(8,128)(2,1)S(1)}, bf16[6,32,256]{2,1,0:T(8,128)(2,1)S(1)}, u32[]{:S(2)}, u32[]{:S(2)}) collective-permute-start(bf16[6,32,256]{2,1,0:T(8,128)(2,1)S(1)} %get-tuple-element.149), channel_id=1, source_target_pairs={{0,8},{2,10},{4,12},{6,14},{8,0},{10,2},{12,4},{14,6},{16,24},{18,... | collective-permute-start | bytes 294920 | tf_op jit(solution)/shard_map/cond/branch_1_fun/ppermute | solution.py:479
  27.3 6.0 %collective-permute-start.13 = (bf16[6,32,256]{2,1,0:T(8,128)(2,1)S(1)}, bf16[6,32,256]{2,1,0:T(8,128)(2,1)S(1)}, u32[]{:S(2)}, u32[]{:S(2)}) collective-permute-start(bf16[6,32,256]{2,1,0:T(8,128)(2,1)S(1)} %get-tuple-element.150), channel_id=1, source_target_pairs={{0,6},{2,4},{4,2},{6,0},{8,14},{10,12},{12,10},{14,8},{16,22},{18,... | collective-permute-start | bytes 294920 | tf_op jit(solution)/shard_map/cond/branch_1_fun/ppermute | solution.py:479
  33.4 29.4 %copy-start.1 = (bf16[8,256,256]{2,1,0:T(8,128)(2,1)S(1)}, bf16[8,256,256]{2,1,0:T(8,128)(2,1)}, u32[]{:S(2)}) copy-start(bf16[8,256,256]{2,1,0:T(8,128)(2,1)} %blocks_ref.1) | copy-start | bytes 3145732
  33.4 29.4 %copy-start.2 = (s32[8]{0:T(128)S(1)}, s32[8]{0:T(128)}, u32[]{:S(2)}) copy-start(s32[8]{0:T(128)} %rows_ref.1) | copy-start | bytes 100
  34.1 11.9 %collective-permute-start.59 = (bf16[14,32,256]{2,1,0:T(8,128)(2,1)S(1)}, bf16[14,32,256]{2,1,0:T(8,128)(2,1)S(1)}, u32[]{:S(2)}, u32[]{:S(2)}) collective-permute-start(bf16[14,32,256]{2,1,0:T(8,128)(2,1)S(1)} %listed_stripes.18), channel_id=1, source_target_pairs={{0,16},{2,18},{4,20},{6,22},{8,24},{10,26},{12,28},{14,30},{16,0},... | collective-permute-start | bytes 688136 | tf_op jit(solution)/shard_map/cond/branch_3_fun/ppermute | solution.py:510
  47.6 5.5 %collective-permute-start.71 = (bf16[8,32,256]{2,1,0:T(8,128)(2,1)S(1)}, bf16[8,32,256]{2,1,0:T(8,128)(2,1)S(1)}, u32[]{:S(2)}, u32[]{:S(2)}) collective-permute-start(bf16[8,32,256]{2,1,0:T(8,128)(2,1)S(1)} %get-tuple-element.280), channel_id=1, source_target_pairs={{0,2},{2,0},{4,6},{6,4},{8,10},{10,8},{12,14},{14,12},{16,18},{18,... | collective-permute-start | bytes 393224 | tf_op jit(solution)/shard_map/ppermute | solution.py:479
  48.3 7.4 %collective-permute-start.72 = (bf16[8,32,256]{2,1,0:T(8,128)(2,1)S(1)}, bf16[8,32,256]{2,1,0:T(8,128)(2,1)S(1)}, u32[]{:S(2)}, u32[]{:S(2)}) collective-permute-start(bf16[8,32,256]{2,1,0:T(8,128)(2,1)S(1)} %get-tuple-element.281), channel_id=1, source_target_pairs={{0,12},{2,14},{4,8},{6,10},{8,4},{10,6},{12,0},{14,2},{16,28},{18,... | collective-permute-start | bytes 393224 | tf_op jit(solution)/shard_map/ppermute | solution.py:479
  48.3 9.2 %collective-permute-start.73 = (bf16[8,32,256]{2,1,0:T(8,128)(2,1)}, bf16[8,32,256]{2,1,0:T(8,128)(2,1)S(1)}, u32[]{:S(2)}, u32[]{:S(2)}) collective-permute-start(bf16[8,32,256]{2,1,0:T(8,128)(2,1)} %get-tuple-element.282), channel_id=1, source_target_pairs={{0,4},{2,6},{4,0},{6,2},{8,12},{10,14},{12,8},{14,10},{16,20},{18,... | collective-permute-start | bytes 393224 | tf_op jit(solution)/shard_map/ppermute | solution.py:479
  49.9 9.0 %collective-permute-start.74 = (bf16[8,32,256]{2,1,0:T(8,128)(2,1)}, bf16[8,32,256]{2,1,0:T(8,128)(2,1)S(1)}, u32[]{:S(2)}, u32[]{:S(2)}) collective-permute-start(bf16[8,32,256]{2,1,0:T(8,128)(2,1)} %get-tuple-element.283), channel_id=1, source_target_pairs={{0,10},{2,8},{4,14},{6,12},{8,2},{10,0},{12,6},{14,4},{16,26},{18,... | collective-permute-start | bytes 393224 | tf_op jit(solution)/shard_map/ppermute | solution.py:479
  52.6 8.9 %collective-permute-start.75 = (bf16[8,32,256]{2,1,0:T(8,128)(2,1)}, bf16[8,32,256]{2,1,0:T(8,128)(2,1)S(1)}, u32[]{:S(2)}, u32[]{:S(2)}) collective-permute-start(bf16[8,32,256]{2,1,0:T(8,128)(2,1)} %get-tuple-element.284), channel_id=1, source_target_pairs={{0,14},{2,12},{4,10},{6,8},{8,6},{10,4},{12,2},{14,0},{16,30},{18,... | collective-permute-start | bytes 393224 | tf_op jit(solution)/shard_map/ppermute | solution.py:479
  53.1 9.3 %collective-permute-start.76 = (bf16[8,32,256]{2,1,0:T(8,128)(2,1)}, bf16[8,32,256]{2,1,0:T(8,128)(2,1)S(1)}, u32[]{:S(2)}, u32[]{:S(2)}) collective-permute-start(bf16[8,32,256]{2,1,0:T(8,128)(2,1)} %get-tuple-element.285), channel_id=1, source_target_pairs={{0,8},{2,10},{4,12},{6,14},{8,0},{10,2},{12,4},{14,6},{16,24},{18,... | collective-permute-start | bytes 393224 | tf_op jit(solution)/shard_map/ppermute | solution.py:479
  55.7 7.1 %collective-permute-start.77 = (bf16[8,32,256]{2,1,0:T(8,128)(2,1)}, bf16[8,32,256]{2,1,0:T(8,128)(2,1)S(1)}, u32[]{:S(2)}, u32[]{:S(2)}) collective-permute-start(bf16[8,32,256]{2,1,0:T(8,128)(2,1)} %get-tuple-element.286), channel_id=1, source_target_pairs={{0,6},{2,4},{4,2},{6,0},{8,14},{10,12},{12,10},{14,8},{16,22},{18,... | collective-permute-start | bytes 393224 | tf_op jit(solution)/shard_map/ppermute | solution.py:479
  64.0 2.7 %collective-permute-start.78 = (f32[1024,256]{1,0:T(8,128)S(1)}, f32[1024,256]{1,0:T(8,128)S(1)}, u32[]{:S(2)}, u32[]{:S(2)}) collective-permute-start(f32[1024,256]{1,0:T(8,128)S(1)} %block_products.1.mine_ref), channel_id=1, source_target_pairs={{0,1},{1,0},{2,3},{3,2},{4,5},{5,4},{6,7},{7,6},{8,9},{9,8},{10,11... | collective-permute-start | bytes 3145736 | tf_op jit(solution)/shard_map/ppermute | solution.py:540
  68.2 4.9 %collective-permute-start.79 = (f32[64,128]{1,0:T(8,128)S(1)}, f32[64,128]{1,0:T(8,128)S(1)}, u32[]{:S(2)}, u32[]{:S(2)}) collective-permute-start(f32[64,128]{1,0:T(8,128)S(1)} %get-tuple-element.288), channel_id=1, source_target_pairs={{0,6},{2,4},{4,2},{6,0},{8,14},{10,12},{12,10},{14,8},{16,22},{18,... | collective-permute-start | bytes 98312 | tf_op jit(solution)/shard_map/ppermute | solution.py:520
  70.2 3.9 %collective-permute-start.80 = (f32[64,128]{1,0:T(8,128)S(1)}, f32[64,128]{1,0:T(8,128)S(1)}, u32[]{:S(2)}, u32[]{:S(2)}) collective-permute-start(f32[64,128]{1,0:T(8,128)S(1)} %get-tuple-element.289), channel_id=1, source_target_pairs={{0,2},{2,0},{4,6},{6,4},{8,10},{10,8},{12,14},{14,12},{16,18},{18,... | collective-permute-start | bytes 98312 | tf_op jit(solution)/shard_map/ppermute | solution.py:520
  71.3 3.9 %collective-permute-start.81 = (f32[64,128]{1,0:T(8,128)S(1)}, f32[64,128]{1,0:T(8,128)S(1)}, u32[]{:S(2)}, u32[]{:S(2)}) collective-permute-start(f32[64,128]{1,0:T(8,128)S(1)} %get-tuple-element.290), channel_id=1, source_target_pairs={{0,4},{2,6},{4,0},{6,2},{8,12},{10,14},{12,8},{14,10},{16,20},{18,... | collective-permute-start | bytes 98312 | tf_op jit(solution)/shard_map/ppermute | solution.py:520
  75.2 5.8 %collective-permute-start.84 = (f32[64,128]{1,0:T(8,128)S(1)}, f32[64,128]{1,0:T(8,128)S(1)}, u32[]{:S(2)}, u32[]{:S(2)}) collective-permute-start(f32[64,128]{1,0:T(8,128)S(1)} %add_pieces.1), channel_id=1, source_target_pairs={{0,24},{2,26},{4,28},{6,30},{8,16},{10,18},{12,20},{14,22},{16,8},... | collective-permute-start | bytes 98312 | tf_op jit(solution)/shard_map/ppermute | solution.py:520
  76.2 5.5 %collective-permute-start.83 = (f32[64,128]{1,0:T(8,128)S(1)}, f32[64,128]{1,0:T(8,128)S(1)}, u32[]{:S(2)}, u32[]{:S(2)}) collective-permute-start(f32[64,128]{1,0:T(8,128)S(1)} %add_pieces.1), channel_id=1, source_target_pairs={{0,16},{2,18},{4,20},{6,22},{8,24},{10,26},{12,28},{14,30},{16,0},... | collective-permute-start | bytes 98312 | tf_op jit(solution)/shard_map/ppermute | solution.py:520
  76.9 4.9 %collective-permute-start.82 = (f32[64,128]{1,0:T(8,128)S(1)}, f32[64,128]{1,0:T(8,128)S(1)}, u32[]{:S(2)}, u32[]{:S(2)}) collective-permute-start(f32[64,128]{1,0:T(8,128)S(1)} %add_pieces.1), channel_id=1, source_target_pairs={{0,8},{2,10},{4,12},{6,14},{8,0},{10,2},{12,4},{14,6},{16,24},{18,... | collective-permute-start | bytes 98312 | tf_op jit(solution)/shard_map/ppermute | solution.py:520
  81.9 4.9 %collective-permute-start.87 = (f32[64,128]{1,0:T(8,128)S(1)}, f32[64,128]{1,0:T(8,128)S(1)}, u32[]{:S(2)}, u32[]{:S(2)}) collective-permute-start(f32[64,128]{1,0:T(8,128)S(1)} %add_add_fusion.refs_0_), channel_id=1, source_target_pairs={{0,6},{2,4},{4,2},{6,0},{8,14},{10,12},{12,10},{14,8},{16,22},{18,... | collective-permute-start | bytes 98312 | tf_op jit(solution)/shard_map/ppermute | solution.py:520
  83.2 3.9 %collective-permute-start.86 = (f32[64,128]{1,0:T(8,128)S(1)}, f32[64,128]{1,0:T(8,128)S(1)}, u32[]{:S(2)}, u32[]{:S(2)}) collective-permute-start(f32[64,128]{1,0:T(8,128)S(1)} %add_add_fusion.refs_0_), channel_id=1, source_target_pairs={{0,4},{2,6},{4,0},{6,2},{8,12},{10,14},{12,8},{14,10},{16,20},{18,... | collective-permute-start | bytes 98312 | tf_op jit(solution)/shard_map/ppermute | solution.py:520
  84.3 3.9 %collective-permute-start.85 = (f32[64,128]{1,0:T(8,128)S(1)}, f32[64,128]{1,0:T(8,128)S(1)}, u32[]{:S(2)}, u32[]{:S(2)}) collective-permute-start(f32[64,128]{1,0:T(8,128)S(1)} %add_add_fusion.refs_0_), channel_id=1, source_target_pairs={{0,2},{2,0},{4,6},{6,4},{8,10},{10,8},{12,14},{14,12},{16,18},{18,... | collective-permute-start | bytes 98312 | tf_op jit(solution)/shard_map/ppermute | solution.py:520
  88.3 1.4 collective-permute-start.88

commit v3 on v2

--- a/solution.py
+++ b/solution.py
@@ -149,7 +149,7 @@
         ),
         in_specs=[VMEM],
         out_specs=(VMEM, VMEM, SMEM, SMEM),
-        compiler_params=pltpu.CompilerParams(vmem_limit_bytes=48 * MIB),
+        compiler_params=pltpu.CompilerParams(vmem_limit_bytes=(16 if devices <= 64 else 48) * MIB),
         name="plan",
     )(table)
 
@@ -177,7 +177,7 @@
         out_shape=jax.ShapeDtypeStruct((members, blocks, height, columns), sketch.dtype),
         in_specs=[VMEM],
         out_specs=VMEM,
-        compiler_params=pltpu.CompilerParams(vmem_limit_bytes=24 * MIB),
+        compiler_params=pltpu.CompilerParams(vmem_limit_bytes=10 * MIB),
         cost_estimate=pl.CostEstimate(flops=0, bytes_accessed=4 * sketch.size, transcendentals=0),
         name="turn_stripes",
     )(sketch)
@@ -196,7 +196,7 @@
         out_shape=(jax.ShapeDtypeStruct((count, height, columns), stripes.dtype),) * members,
         in_specs=[SMEM, VMEM],
         out_specs=(VMEM,) * members,
-        compiler_params=pltpu.CompilerParams(vmem_limit_bytes=24 * MIB),
+        compiler_params=pltpu.CompilerParams(vmem_limit_bytes=10 * MIB),
         name="cut_stripes",
     )(lists, stripes)
 
@@ -217,7 +217,7 @@
         out_shape=jax.ShapeDtypeStruct((len(stripes) * per, height, columns), stripes[0].dtype),
         in_specs=[VMEM] * len(stripes),
         out_specs=VMEM,
-        compiler_params=pltpu.CompilerParams(vmem_limit_bytes=24 * MIB),
+        compiler_params=pltpu.CompilerParams(vmem_limit_bytes=10 * MIB),
         name="order_stripes",
     )(*stripes)
 
@@ -233,7 +233,7 @@
         out_shape=jax.ShapeDtypeStruct((count, *stripes.shape[1:]), stripes.dtype),
         in_specs=[SMEM, VMEM],
         out_specs=VMEM,
-        compiler_params=pltpu.CompilerParams(vmem_limit_bytes=24 * MIB),
+        compiler_params=pltpu.CompilerParams(vmem_limit_bytes=10 * MIB),
         name="listed_stripes",
     )(numbers, stripes)
 
@@ -256,7 +256,7 @@
         in_specs=[SMEM, VMEM, VMEM],
         out_specs=(VMEM,) * members,
         scratch_shapes=[pltpu.VMEM((own.shape[0] + other.shape[0], *shape), own.dtype)],
-        compiler_params=pltpu.CompilerParams(vmem_limit_bytes=24 * MIB),
+        compiler_params=pltpu.CompilerParams(vmem_limit_bytes=10 * MIB),
         name="pick_stripes",
     )(places, own, other)
 
@@ -286,7 +286,7 @@
         in_specs=[SMEM, SMEM, VMEM] + [VMEM] * len(chosen),
         out_specs=VMEM,
         scratch_shapes=[pltpu.VMEM((len(chosen), *chosen[0].shape), chosen[0].dtype)],
-        compiler_params=pltpu.CompilerParams(vmem_limit_bytes=24 * MIB),
+        compiler_params=pltpu.CompilerParams(vmem_limit_bytes=10 * MIB),
         name="block_products",
     )(block_rows, counts, blocks, *chosen)
 
@@ -321,7 +321,7 @@
         in_specs=[VMEM, VMEM],
         out_specs=(VMEM,) * 5,
         scratch_shapes=[pltpu.VMEM((rows, columns), jnp.float32)],
-        compiler_params=pltpu.CompilerParams(vmem_limit_bytes=24 * MIB),
+        compiler_params=pltpu.CompilerParams(vmem_limit_bytes=10 * MIB),
         name="sum_and_gram",
     )(mine, other)
 
@@ -337,7 +337,7 @@
         out_shape=jax.ShapeDtypeStruct(pieces[0].shape, jnp.float32),
         in_specs=[VMEM] * len(pieces),
         out_specs=VMEM,
-        compiler_params=pltpu.CompilerParams(vmem_limit_bytes=24 * MIB),
+        compiler_params=pltpu.CompilerParams(vmem_limit_bytes=10 * MIB),
         name="add_pieces",
     )(*pieces)
 
@@ -357,7 +357,7 @@
         out_shape=jax.ShapeDtypeStruct((len(quarters) * height, width), jnp.float32),
         in_specs=[VMEM] * len(quarters),
         out_specs=VMEM,
-        compiler_params=pltpu.CompilerParams(vmem_limit_bytes=24 * MIB),
+        compiler_params=pltpu.CompilerParams(vmem_limit_bytes=10 * MIB),
         name="stack_quarters",
     )(*quarters)
 
@@ -468,7 +468,7 @@
         in_specs=[VMEM] * (len(grams) + 1),
         out_specs=(VMEM, VMEM),
         scratch_shapes=[pltpu.VMEM((columns, columns), jnp.float32)] * 4,
-        compiler_params=pltpu.CompilerParams(vmem_limit_bytes=24 * MIB),
+        compiler_params=pltpu.CompilerParams(vmem_limit_bytes=10 * MIB),
         name="factor_and_basis",
     )(*grams, own)
 

time: 153 us -> 155 us (1.013); the launches traced: 151 us -> 157 us
  waiting for transfers between devices: 38.1 us -> 46.4 us
  starting transfers between devices: 38.9 us -> 36.4 us
    ppermute x14, waiting for transfers between devices: 8.94 us -> 14.5 us  [exchange(): lax.ppermute(piece, 'rows', [(r, r ^ d) for r in range(rows)])]
    ppermute x1, waiting for transfers between devices: 11.4 us -> 15.3 us  [run(): other = lax.ppermute(listed(lists, own, count), 'rows', swap)]
    ppermute x14, starting transfers between devices: 19.3 us -> 16.9 us  [exchange(): lax.ppermute(piece, 'rows', [(r, r ^ d) for r in range(rows)])]
  transfers between devices with their start and end apart: 27 -> 27, of which waited for: 19 -> 20; matrix products, arithmetic and copies ran while one was open for 0% -> 0% of each run, Pallas kernels for 0% -> 0%
where the time goes in v3:
time: 155 us; the launch traced here: 157 us
  Pallas kernels  70.2 us (45%)
  waiting for transfers between devices  46.4 us (30%)
  starting transfers between devices  36.4 us (23%)
  between operations  2.69 us (2%)
  local copies, waits for them, and re-layouts  1.6 us (1%)
    pallas_call x1, Pallas kernels, factor_and_basis(): pl.pallas_call(functools.partial(factor_kernel, total_rows), out_shape=(j...  61.8 us
    ppermute x14, starting transfers between devices, exchange(): lax.ppermute(piece, 'rows', [(r, r ^ d) for r in range(rows)])  16.9 us
    ppermute x1, waiting for transfers between devices, run(): other = lax.ppermute(listed(lists, own, count), 'rows', swap)  15.3 us
    ppermute x14, waiting for transfers between devices, exchange(): lax.ppermute(piece, 'rows', [(r, r ^ d) for r in range(rows)])  14.5 us
    ppermute x9, starting transfers between devices, moved(): return lax.ppermute(piece, 'rows', [(r, r ^ d) for r in range(rows)])  11.6 us
    ppermute x9, waiting for transfers between devices, moved(): return lax.ppermute(piece, 'rows', [(r, r ^ d) for r in range(rows)])  7.33 us
    all_to_all x1, starting transfers between devices, fetch(): lax.all_to_all(table, ('rows', 'cols'), split_axis=0, concat_axis=0, tile...  7.3 us
    all_to_all x1, waiting for transfers between devices, fetch(): lax.all_to_all(table, ('rows', 'cols'), split_axis=0, concat_axis=0, tile...  5.34 us
  transfers between devices with their start and end apart: 27, of which 20 were waited for; matrix products, arithmetic and copies ran while one was open for 0% of the time, Pallas kernels for 0%

profile of v3, /device:TPU:0, one launch (start us, length us, event | category | flops | bytes accessed | tf_op | source)
XLA Modules:
  0.0 157.5 jit_solution(8384991295033187971)
XLA Ops:
  1.3 1.3 table_copies.1
  2.6 7.3 %all-to-all-start = ((s32[32,1,128]{2,1,0:T(1,128)}), s32[32,1,128]{2,1,0:T(1,128)S(1)}, u32[]{:S(2)}, u32[]{:S(2)}) async-start(s32[32,1,128]{2,1,0:T(1,128)} %table_copies.1), calls=%async_computation | async-start | bytes 32768 | tf_op jit(solution)/shard_map/all_to_all | solution.py:496
  9.9 0.0 copy-start
  9.9 1.6 %copy-done = bf16[4096,256]{1,0:T(8,128)(2,1)S(1)} copy-done((bf16[4096,256]{1,0:T(8,128)(2,1)S(1)}, bf16[4096,256]{1,0:T(8,128)(2,1)}, u32[]{:S(2)}) %copy-start) | copy-done | bytes 2097176
  11.5 0.1 turn_stripes.1
  11.6 5.3 %all-to-all-done.table_ref = s32[32,1,128]{2,1,0:T(1,128)S(1)} async-done(((s32[32,1,128]{2,1,0:T(1,128)}), s32[32,1,128]{2,1,0:T(1,128)S(1)}, u32[]{:S(2)}, u32[]{:S(2)}) %all-to-all-start) | async-done | bytes 16416 | tf_op jit(solution)/shard_map/all_to_all | solution.py:496
  16.9 1.3 plan.1
  19.5 16.7 %conditional.2 = (bf16[128,32,256]{2,1,0:T(8,128)(2,1)S(1)}) conditional(s32[]{:T(128)} %bitcast.1, (s32[8,128]{1,0:T(8,128)S(1)}, bf16[8,16,32,256]{3,2,1,0:T(8,128)(2,1)S(1)}) %tuple.76, (s32[8,128]{1,0:T(8,128)S(1)}, bf16[8,16,32,256]{3,2,1,0:T(8,128)(2,1)S(1)}) %tuple.76, (s32[8,128]{1,0:T(8,128)S(1)}, ...), branch_computations={%region_0.0_spmd, %region_1.0_spmd, %region_2.0_spmd, %region_3.0_... | conditional | bytes 7340320 | solution.py:505
  19.6 0.7 cut_stripes.11
  20.2 0.6 collective-permute-start.21
  20.8 0.7 collective-permute-start.22
  21.5 1.4 collective-permute-start.23
  22.9 2.4 %collective-permute-start.24 = (bf16[8,32,256]{2,1,0:T(8,128)(2,1)S(1)}, bf16[8,32,256]{2,1,0:T(8,128)(2,1)S(1)}, u32[]{:S(2)}, u32[]{:S(2)}) collective-permute-start(bf16[8,32,256]{2,1,0:T(8,128)(2,1)S(1)} %get-tuple-element.167), channel_id=1, source_target_pairs={{0,10},{2,8},{4,14},{6,12},{8,2},{10,0},{12,6},{14,4},{16,26},{18,... | collective-permute-start | bytes 393224 | tf_op jit(solution)/shard_map/cond/branch_3_fun/ppermute | solution.py:479
  25.3 0.6 collective-permute-start.25
  25.9 0.0 collective-permute-done.21.refs_1_
  25.9 1.4 collective-permute-start.26
  27.3 0.8 collective-permute-done.22.refs_2_
  28.2 1.5 collective-permute-start.27
  29.7 0.0 collective-permute-done.23.refs_3_
  29.7 1.3 collective-permute-done.24.refs_4_
  30.9 3.8 %collective-permute-done.25.refs_5_ = bf16[8,32,256]{2,1,0:T(8,128)(2,1)S(1)} collective-permute-done((bf16[8,32,256]{2,1,0:T(8,128)(2,1)S(1)}, bf16[8,32,256]{2,1,0:T(8,128)(2,1)S(1)}, u32[]{:S(2)}, u32[]{:S(2)}) %collective-permute-start.25) | collective-permute-done | bytes 131104 | tf_op jit(solution)/shard_map/cond/branch_3_fun/ppermute | solution.py:479
  34.8 1.3 collective-permute-done.27.refs_7_
  36.1 0.1 order_stripes.11
  36.2 0.0 copy-start.1
  36.2 0.0 copy-start.2
  36.2 18.1 %conditional.3 = ((bf16[8,32,256]{2,1,0:T(8,128)(2,1)S(1)}, bf16[8,32,256]{2,1,0:T(8,128)(2,1)S(1)}, bf16[8,32,256]{2,1,0:T(8,128)(2,1)S(1)}, bf16[8,32,256]{2,1...) conditional(s32[]{:T(128)} %bitcast, (s32[8,128]{1,0:T(8,128)S(1)}, ...), branch_computations={%region_8.0_spmd, %region_9.0_spmd, %region_10.0_spmd, %region_11.... | conditional | bytes 4194352 | solution.py:515
  36.3 0.6 listed_stripes.22
  36.9 0.5 collective-permute-start.63
  37.4 15.3 %collective-permute-done.63.other_ref = bf16[18,32,256]{2,1,0:T(8,128)(2,1)S(1)} collective-permute-done((bf16[18,32,256]{2,1,0:T(8,128)(2,1)S(1)}, bf16[18,32,256]{2,1,0:T(8,128)(2,1)S(1)}, u32[]{:S(2)}, u32[]{:S(2)}) %collective-permute-start.63) | collective-permute-done | bytes 294944 | tf_op jit(solution)/shard_map/cond/branch_7_fun/ppermute | solution.py:510
  52.7 1.6 %pick_stripes.22 = (bf16[8,32,256]{2,1,0:T(8,128)(2,1)S(1)}, bf16[8,32,256]{2,1,0:T(8,128)(2,1)S(1)}, bf16[8,32,256]{2,1,0:T(8,128)(2,1)S(1)}, bf16[8,32,256]{2,...) custom-call(s32[8,128]{1,0:T(8,128)S(1)} %get-tuple-element.232.plac, ...), custom_call_target="tpu_custom_call" | custom-call | tf_op jit(solution)/shard_map/cond/branch_7_fun/pick_stripes/pallas_call | solution.py:253
  54.3 0.1 collective-permute-start.71
  54.5 0.5 collective-permute-start.73
  55.0 4.3 %collective-permute-start.74 = (bf16[8,32,256]{2,1,0:T(8,128)(2,1)}, bf16[8,32,256]{2,1,0:T(8,128)(2,1)S(1)}, u32[]{:S(2)}, u32[]{:S(2)}) collective-permute-start(bf16[8,32,256]{2,1,0:T(8,128)(2,1)} %get-tuple-element.283), channel_id=1, source_target_pairs={{0,10},{2,8},{4,14},{6,12},{8,2},{10,0},{12,6},{14,4},{16,26},{18,... | collective-permute-start | bytes 393224 | tf_op jit(solution)/shard_map/ppermute | solution.py:479
  59.3 0.0 collective-permute-start.75
  59.3 0.1 collective-permute-done.71.refs_1_
  59.3 1.5 collective-permute-start.76
  60.8 0.9 collective-permute-done.72.refs_2_
  61.8 1.9 %collective-permute-start.77 = (bf16[8,32,256]{2,1,0:T(8,128)(2,1)}, bf16[8,32,256]{2,1,0:T(8,128)(2,1)S(1)}, u32[]{:S(2)}, u32[]{:S(2)}) collective-permute-start(bf16[8,32,256]{2,1,0:T(8,128)(2,1)} %get-tuple-element.286), channel_id=1, source_target_pairs={{0,6},{2,4},{4,2},{6,0},{8,14},{10,12},{12,10},{14,8},{16,22},{18,... | collective-permute-start | bytes 393224 | tf_op jit(solution)/shard_map/ppermute | solution.py:479
  63.7 1.3 collective-permute-done.74.refs_4_
  65.0 3.6 %collective-permute-done.75.refs_5_ = bf16[8,32,256]{2,1,0:T(8,128)(2,1)S(1)} collective-permute-done((bf16[8,32,256]{2,1,0:T(8,128)(2,1)}, bf16[8,32,256]{2,1,0:T(8,128)(2,1)S(1)}, u32[]{:S(2)}, u32[]{:S(2)}) %collective-permute-start.75) | collective-permute-done | bytes 131104 | tf_op jit(solution)/shard_map/ppermute | solution.py:479
  68.5 1.4 collective-permute-done.77.refs_7_
  69.9 1.1 block_products.1.mine_ref
  71.1 0.1 collective-permute-start.78
  71.1 2.6 %collective-permute-done.78.other_ref = f32[1024,256]{1,0:T(8,128)S(1)} collective-permute-done((f32[1024,256]{1,0:T(8,128)S(1)}, f32[1024,256]{1,0:T(8,128)S(1)}, u32[]{:S(2)}, u32[]{:S(2)}) %collective-permute-start.78) | collective-permute-done | bytes 1048608 | tf_op jit(solution)/shard_map/ppermute | solution.py:540
  73.8 1.5 sum_and_gram.1
  75.3 0.7 collective-permute-start.79
  76.0 1.7 %collective-permute-start.80 = (f32[64,128]{1,0:T(8,128)S(1)}, f32[64,128]{1,0:T(8,128)S(1)}, u32[]{:S(2)}, u32[]{:S(2)}) collective-permute-start(f32[64,128]{1,0:T(8,128)S(1)} %get-tuple-element.289), channel_id=1, source_target_pairs={{0,2},{2,0},{4,6},{6,4},{8,10},{10,8},{12,14},{14,12},{16,18},{18,... | collective-permute-start | bytes 98312 | tf_op jit(solution)/shard_map/ppermute | solution.py:520
  77.7 1.2 collective-permute-start.81
  78.9 1.4 collective-permute-done.79.refs_1_
  80.2 1.4 collective-permute-done.81.refs_3_
  81.6 0.4 collective-permute-start.84
  82.0 1.1 collective-permute-start.83
  83.1 3.0 %collective-permute-start.82 = (f32[64,128]{1,0:T(8,128)S(1)}, f32[64,128]{1,0:T(8,128)S(1)}, u32[]{:S(2)}, u32[]{:S(2)}) collective-permute-start(f32[64,128]{1,0:T(8,128)S(1)} %add_pieces.1), channel_id=1, source_target_pairs={{0,8},{2,10},{4,12},{6,14},{8,0},{10,2},{12,4},{14,6},{16,24},{18,... | collective-permute-start | bytes 98312 | tf_op jit(solution)/shard_map/ppermute | solution.py:520
  86.1 1.3 collective-permute-done.84
  87.4 0.6 collective-permute-done.82
  88.0 1.3 collective-permute-start.87
  89.3 1.0 collective-permute-start.86
  90.3 1.2 collective-permute-start.85
  91.5 1.3 collective-permute-done.87.refs_3_
  92.8 0.4 collective-permute-done.86.refs_2_
  93.2 1.0 collective-permute-done.85.refs_1_
  94.2 0.1 collective-permute-start.88
  94.3 1.3 collective-permute-done.88.refs_1_
  95.7 61.8 %factor_and_basis.1 = (f32[512,256]{1,0:T(8,128)}, f32[256,256]{1,0:T(8,128)}) custom-call(f32[256,128]{1,0:T(8,128)S(1)} %stack_quarters.1.refs_0_, f32[256,128]{1,0:T(8,128)S(1)} %collective-permute-done.88.refs_1_, f32[512,256]{1,0:T(8,128)S(1)} %get-tuple-element.291.refs_2_), custom_call_target="tpu_custom_call" | custom-call | tf_op jit(solution)/shard_map/factor_and_basis/pallas_call | solution.py:462
  (11 shorter events, 0.1 us)
Async XLA Ops:
  2.6 14.4 %all-to-all-start = ((s32[32,1,128]{2,1,0:T(1,128)}), s32[32,1,128]{2,1,0:T(1,128)S(1)}, u32[]{:S(2)}, u32[]{:S(2)}) async-start(s32[32,1,128]{2,1,0:T(1,128)} %table_copies.1), calls=%async_computation | async-start | bytes 32768 | tf_op jit(solution)/shard_map/all_to_all | solution.py:496
  9.9 1.6 %copy-start = (bf16[4096,256]{1,0:T(8,128)(2,1)S(1)}, bf16[4096,256]{1,0:T(8,128)(2,1)}, u32[]{:S(2)}) copy-start(bf16[4096,256]{1,0:T(8,128)(2,1)} %param.28) | copy-start | bytes 6291460
  20.2 5.6 %collective-permute-start.21 = (bf16[8,32,256]{2,1,0:T(8,128)(2,1)S(1)}, bf16[8,32,256]{2,1,0:T(8,128)(2,1)S(1)}, u32[]{:S(2)}, u32[]{:S(2)}) collective-permute-start(bf16[8,32,256]{2,1,0:T(8,128)(2,1)S(1)} %get-tuple-element.164), channel_id=1, source_target_pairs={{0,2},{2,0},{4,6},{6,4},{8,10},{10,8},{12,14},{14,12},{16,18},{18,... | collective-permute-start | bytes 393224 | tf_op jit(solution)/shard_map/cond/branch_3_fun/ppermute | solution.py:479
  20.8 7.3 %collective-permute-start.22 = (bf16[8,32,256]{2,1,0:T(8,128)(2,1)S(1)}, bf16[8,32,256]{2,1,0:T(8,128)(2,1)S(1)}, u32[]{:S(2)}, u32[]{:S(2)}) collective-permute-start(bf16[8,32,256]{2,1,0:T(8,128)(2,1)S(1)} %get-tuple-element.165), channel_id=1, source_target_pairs={{0,12},{2,14},{4,8},{6,10},{8,4},{10,6},{12,0},{14,2},{16,28},{18,... | collective-permute-start | bytes 393224 | tf_op jit(solution)/shard_map/cond/branch_3_fun/ppermute | solution.py:479
  21.5 8.2 %collective-permute-start.23 = (bf16[8,32,256]{2,1,0:T(8,128)(2,1)S(1)}, bf16[8,32,256]{2,1,0:T(8,128)(2,1)S(1)}, u32[]{:S(2)}, u32[]{:S(2)}) collective-permute-start(bf16[8,32,256]{2,1,0:T(8,128)(2,1)S(1)} %get-tuple-element.166), channel_id=1, source_target_pairs={{0,4},{2,6},{4,0},{6,2},{8,12},{10,14},{12,8},{14,10},{16,20},{18,... | collective-permute-start | bytes 393224 | tf_op jit(solution)/shard_map/cond/branch_3_fun/ppermute | solution.py:479
  22.9 8.1 %collective-permute-start.24 = (bf16[8,32,256]{2,1,0:T(8,128)(2,1)S(1)}, bf16[8,32,256]{2,1,0:T(8,128)(2,1)S(1)}, u32[]{:S(2)}, u32[]{:S(2)}) collective-permute-start(bf16[8,32,256]{2,1,0:T(8,128)(2,1)S(1)} %get-tuple-element.167), channel_id=1, source_target_pairs={{0,10},{2,8},{4,14},{6,12},{8,2},{10,0},{12,6},{14,4},{16,26},{18,... | collective-permute-start | bytes 393224 | tf_op jit(solution)/shard_map/cond/branch_3_fun/ppermute | solution.py:479
  25.3 9.5 %collective-permute-start.25 = (bf16[8,32,256]{2,1,0:T(8,128)(2,1)S(1)}, bf16[8,32,256]{2,1,0:T(8,128)(2,1)S(1)}, u32[]{:S(2)}, u32[]{:S(2)}) collective-permute-start(bf16[8,32,256]{2,1,0:T(8,128)(2,1)S(1)} %get-tuple-element.168), channel_id=1, source_target_pairs={{0,14},{2,12},{4,10},{6,8},{8,6},{10,4},{12,2},{14,0},{16,30},{18,... | collective-permute-start | bytes 393224 | tf_op jit(solution)/shard_map/cond/branch_3_fun/ppermute | solution.py:479
  25.9 8.9 %collective-permute-start.26 = (bf16[8,32,256]{2,1,0:T(8,128)(2,1)S(1)}, bf16[8,32,256]{2,1,0:T(8,128)(2,1)S(1)}, u32[]{:S(2)}, u32[]{:S(2)}) collective-permute-start(bf16[8,32,256]{2,1,0:T(8,128)(2,1)S(1)} %get-tuple-element.169), channel_id=1, source_target_pairs={{0,8},{2,10},{4,12},{6,14},{8,0},{10,2},{12,4},{14,6},{16,24},{18,... | collective-permute-start | bytes 393224 | tf_op jit(solution)/shard_map/cond/branch_3_fun/ppermute | solution.py:479
  28.2 7.9 %collective-permute-start.27 = (bf16[8,32,256]{2,1,0:T(8,128)(2,1)S(1)}, bf16[8,32,256]{2,1,0:T(8,128)(2,1)S(1)}, u32[]{:S(2)}, u32[]{:S(2)}) collective-permute-start(bf16[8,32,256]{2,1,0:T(8,128)(2,1)S(1)} %get-tuple-element.170), channel_id=1, source_target_pairs={{0,6},{2,4},{4,2},{6,0},{8,14},{10,12},{12,10},{14,8},{16,22},{18,... | collective-permute-start | bytes 393224 | tf_op jit(solution)/shard_map/cond/branch_3_fun/ppermute | solution.py:479
  36.2 33.7 %copy-start.1 = (bf16[8,256,256]{2,1,0:T(8,128)(2,1)S(1)}, bf16[8,256,256]{2,1,0:T(8,128)(2,1)}, u32[]{:S(2)}) copy-start(bf16[8,256,256]{2,1,0:T(8,128)(2,1)} %blocks_ref.1) | copy-start | bytes 3145732
  36.2 33.7 %copy-start.2 = (s32[8]{0:T(128)S(1)}, s32[8]{0:T(128)}, u32[]{:S(2)}) copy-start(s32[8]{0:T(128)} %rows_ref.1) | copy-start | bytes 100
  36.9 15.8 %collective-permute-start.63 = (bf16[18,32,256]{2,1,0:T(8,128)(2,1)S(1)}, bf16[18,32,256]{2,1,0:T(8,128)(2,1)S(1)}, u32[]{:S(2)}, u32[]{:S(2)}) collective-permute-start(bf16[18,32,256]{2,1,0:T(8,128)(2,1)S(1)} %listed_stripes.22), channel_id=1, source_target_pairs={{0,16},{2,18},{4,20},{6,22},{8,24},{10,26},{12,28},{14,30},{16,0},... | collective-permute-start | bytes 884744 | tf_op jit(solution)/shard_map/cond/branch_7_fun/ppermute | solution.py:510
  54.3 5.0 %collective-permute-start.71 = (bf16[8,32,256]{2,1,0:T(8,128)(2,1)S(1)}, bf16[8,32,256]{2,1,0:T(8,128)(2,1)S(1)}, u32[]{:S(2)}, u32[]{:S(2)}) collective-permute-start(bf16[8,32,256]{2,1,0:T(8,128)(2,1)S(1)} %get-tuple-element.280), channel_id=1, source_target_pairs={{0,2},{2,0},{4,6},{6,4},{8,10},{10,8},{12,14},{14,12},{16,18},{18,... | collective-permute-start | bytes 393224 | tf_op jit(solution)/shard_map/ppermute | solution.py:479
  54.5 7.3 %collective-permute-start.72 = (bf16[8,32,256]{2,1,0:T(8,128)(2,1)S(1)}, bf16[8,32,256]{2,1,0:T(8,128)(2,1)S(1)}, u32[]{:S(2)}, u32[]{:S(2)}) collective-permute-start(bf16[8,32,256]{2,1,0:T(8,128)(2,1)S(1)} %get-tuple-element.281), channel_id=1, source_target_pairs={{0,12},{2,14},{4,8},{6,10},{8,4},{10,6},{12,0},{14,2},{16,28},{18,... | collective-permute-start | bytes 393224 | tf_op jit(solution)/shard_map/ppermute | solution.py:479
  54.5 9.2 %collective-permute-start.73 = (bf16[8,32,256]{2,1,0:T(8,128)(2,1)}, bf16[8,32,256]{2,1,0:T(8,128)(2,1)S(1)}, u32[]{:S(2)}, u32[]{:S(2)}) collective-permute-start(bf16[8,32,256]{2,1,0:T(8,128)(2,1)} %get-tuple-element.282), channel_id=1, source_target_pairs={{0,4},{2,6},{4,0},{6,2},{8,12},{10,14},{12,8},{14,10},{16,20},{18,... | collective-permute-start | bytes 393224 | tf_op jit(solution)/shard_map/ppermute | solution.py:479
  55.0 10.0 %collective-permute-start.74 = (bf16[8,32,256]{2,1,0:T(8,128)(2,1)}, bf16[8,32,256]{2,1,0:T(8,128)(2,1)S(1)}, u32[]{:S(2)}, u32[]{:S(2)}) collective-permute-start(bf16[8,32,256]{2,1,0:T(8,128)(2,1)} %get-tuple-element.283), channel_id=1, source_target_pairs={{0,10},{2,8},{4,14},{6,12},{8,2},{10,0},{12,6},{14,4},{16,26},{18,... | collective-permute-start | bytes 393224 | tf_op jit(solution)/shard_map/ppermute | solution.py:479
  59.3 9.3 %collective-permute-start.75 = (bf16[8,32,256]{2,1,0:T(8,128)(2,1)}, bf16[8,32,256]{2,1,0:T(8,128)(2,1)S(1)}, u32[]{:S(2)}, u32[]{:S(2)}) collective-permute-start(bf16[8,32,256]{2,1,0:T(8,128)(2,1)} %get-tuple-element.284), channel_id=1, source_target_pairs={{0,14},{2,12},{4,10},{6,8},{8,6},{10,4},{12,2},{14,0},{16,30},{18,... | collective-permute-start | bytes 393224 | tf_op jit(solution)/shard_map/ppermute | solution.py:479
  59.3 9.2 %collective-permute-start.76 = (bf16[8,32,256]{2,1,0:T(8,128)(2,1)}, bf16[8,32,256]{2,1,0:T(8,128)(2,1)S(1)}, u32[]{:S(2)}, u32[]{:S(2)}) collective-permute-start(bf16[8,32,256]{2,1,0:T(8,128)(2,1)} %get-tuple-element.285), channel_id=1, source_target_pairs={{0,8},{2,10},{4,12},{6,14},{8,0},{10,2},{12,4},{14,6},{16,24},{18,... | collective-permute-start | bytes 393224 | tf_op jit(solution)/shard_map/ppermute | solution.py:479
  61.8 8.1 %collective-permute-start.77 = (bf16[8,32,256]{2,1,0:T(8,128)(2,1)}, bf16[8,32,256]{2,1,0:T(8,128)(2,1)S(1)}, u32[]{:S(2)}, u32[]{:S(2)}) collective-permute-start(bf16[8,32,256]{2,1,0:T(8,128)(2,1)} %get-tuple-element.286), channel_id=1, source_target_pairs={{0,6},{2,4},{4,2},{6,0},{8,14},{10,12},{12,10},{14,8},{16,22},{18,... | collective-permute-start | bytes 393224 | tf_op jit(solution)/shard_map/ppermute | solution.py:479
  71.1 2.7 %collective-permute-start.78 = (f32[1024,256]{1,0:T(8,128)S(1)}, f32[1024,256]{1,0:T(8,128)S(1)}, u32[]{:S(2)}, u32[]{:S(2)}) collective-permute-start(f32[1024,256]{1,0:T(8,128)S(1)} %block_products.1.mine_ref), channel_id=1, source_target_pairs={{0,1},{1,0},{2,3},{3,2},{4,5},{5,4},{6,7},{7,6},{8,9},{9,8},{10,11... | collective-permute-start | bytes 3145736 | tf_op jit(solution)/shard_map/ppermute | solution.py:540
  75.3 4.9 %collective-permute-start.79 = (f32[64,128]{1,0:T(8,128)S(1)}, f32[64,128]{1,0:T(8,128)S(1)}, u32[]{:S(2)}, u32[]{:S(2)}) collective-permute-start(f32[64,128]{1,0:T(8,128)S(1)} %get-tuple-element.288), channel_id=1, source_target_pairs={{0,6},{2,4},{4,2},{6,0},{8,14},{10,12},{12,10},{14,8},{16,22},{18,... | collective-permute-start | bytes 98312 | tf_op jit(solution)/shard_map/ppermute | solution.py:520
  76.0 4.2 %collective-permute-start.80 = (f32[64,128]{1,0:T(8,128)S(1)}, f32[64,128]{1,0:T(8,128)S(1)}, u32[]{:S(2)}, u32[]{:S(2)}) collective-permute-start(f32[64,128]{1,0:T(8,128)S(1)} %get-tuple-element.289), channel_id=1, source_target_pairs={{0,2},{2,0},{4,6},{6,4},{8,10},{10,8},{12,14},{14,12},{16,18},{18,... | collective-permute-start | bytes 98312 | tf_op jit(solution)/shard_map/ppermute | solution.py:520
  77.7 3.9 %collective-permute-start.81 = (f32[64,128]{1,0:T(8,128)S(1)}, f32[64,128]{1,0:T(8,128)S(1)}, u32[]{:S(2)}, u32[]{:S(2)}) collective-permute-start(f32[64,128]{1,0:T(8,128)S(1)} %get-tuple-element.290), channel_id=1, source_target_pairs={{0,4},{2,6},{4,0},{6,2},{8,12},{10,14},{12,8},{14,10},{16,20},{18,... | collective-permute-start | bytes 98312 | tf_op jit(solution)/shard_map/ppermute | solution.py:520
  81.6 5.8 %collective-permute-start.84 = (f32[64,128]{1,0:T(8,128)S(1)}, f32[64,128]{1,0:T(8,128)S(1)}, u32[]{:S(2)}, u32[]{:S(2)}) collective-permute-start(f32[64,128]{1,0:T(8,128)S(1)} %add_pieces.1), channel_id=1, source_target_pairs={{0,24},{2,26},{4,28},{6,30},{8,16},{10,18},{12,20},{14,22},{16,8},... | collective-permute-start | bytes 98312 | tf_op jit(solution)/shard_map/ppermute | solution.py:520
  82.0 5.4 %collective-permute-start.83 = (f32[64,128]{1,0:T(8,128)S(1)}, f32[64,128]{1,0:T(8,128)S(1)}, u32[]{:S(2)}, u32[]{:S(2)}) collective-permute-start(f32[64,128]{1,0:T(8,128)S(1)} %add_pieces.1), channel_id=1, source_target_pairs={{0,16},{2,18},{4,20},{6,22},{8,24},{10,26},{12,28},{14,30},{16,0},... | collective-permute-start | bytes 98312 | tf_op jit(solution)/shard_map/ppermute | solution.py:520
  83.1 4.8 %collective-permute-start.82 = (f32[64,128]{1,0:T(8,128)S(1)}, f32[64,128]{1,0:T(8,128)S(1)}, u32[]{:S(2)}, u32[]{:S(2)}) collective-permute-start(f32[64,128]{1,0:T(8,128)S(1)} %add_pieces.1), channel_id=1, source_target_pairs={{0,8},{2,10},{4,12},{6,14},{8,0},{10,2},{12,4},{14,6},{16,24},{18,... | collective-permute-start | bytes 98312 | tf_op jit(solution)/shard_map/ppermute | solution.py:520
  88.0 4.9 %collective-permute-start.87 = (f32[64,128]{1,0:T(8,128)S(1)}, f32[64,128]{1,0:T(8,128)S(1)}, u32[]{:S(2)}, u32[]{:S(2)}) collective-permute-start(f32[64,128]{1,0:T(8,128)S(1)} %add_add_fusion.refs_0_), channel_id=1, source_target_pairs={{0,6},{2,4},{4,2},{6,0},{8,14},{10,12},{12,10},{14,8},{16,22},{18,... | collective-permute-start | bytes 98312 | tf_op jit(solution)/shard_map/ppermute | solution.py:520
  89.3 3.9 %collective-permute-start.86 = (f32[64,128]{1,0:T(8,128)S(1)}, f32[64,128]{1,0:T(8,128)S(1)}, u32[]{:S(2)}, u32[]{:S(2)}) collective-permute-start(f32[64,128]{1,0:T(8,128)S(1)} %add_add_fusion.refs_0_), channel_id=1, source_target_pairs={{0,4},{2,6},{4,0},{6,2},{8,12},{10,14},{12,8},{14,10},{16,20},{18,... | collective-permute-start | bytes 98312 | tf_op jit(solution)/shard_map/ppermute | solution.py:520
  90.3 3.9 %collective-permute-start.85 = (f32[64,128]{1,0:T(8,128)S(1)}, f32[64,128]{1,0:T(8,128)S(1)}, u32[]{:S(2)}, u32[]{:S(2)}) collective-permute-start(f32[64,128]{1,0:T(8,128)S(1)} %add_add_fusion.refs_0_), channel_id=1, source_target_pairs={{0,2},{2,0},{4,6},{6,4},{8,10},{10,8},{12,14},{14,12},{16,18},{18,... | collective-permute-start | bytes 98312 | tf_op jit(solution)/shard_map/ppermute | solution.py:520
  94.2 1.4 collective-permute-start.88

commit v4 on v2

--- a/solution.py
+++ b/solution.py
@@ -261,17 +261,12 @@
     )(places, own, other)
 
 
-def product_kernel(rows_ref, counts_ref, blocks_ref, *refs):
-    *chosen_refs, out_ref, whole = refs
+def product_kernel(rows_ref, counts_ref, blocks_ref, chosen_ref, out_ref):
     slots, width, _ = blocks_ref.shape
     columns = out_ref.shape[1]
-    members = len(chosen_refs)
-    me = lax.axis_index("rows") % members
-    for ref, d in zip(chosen_refs, distances(members) if members > 1 else [0]):
-        whole[me ^ d] = ref[...]
     out_ref[...] = jnp.zeros_like(out_ref)
     for s in range(slots):
-        piece = whole[:, s].reshape(width, columns)
+        piece = chosen_ref[:, s].reshape(width, columns)
         product = jnp.dot(blocks_ref[s], piece, preferred_element_type=jnp.float32)
         at = pl.ds(pl.multiple_of(rows_ref[s] * width, width), width)
         out_ref[at, :] += jnp.where(s < counts_ref[0], product, 0.0)
@@ -279,16 +274,15 @@
 
 def block_products(block_rows, counts, blocks, chosen):
     _, width, _ = blocks.shape
-    columns = chosen[0].shape[-1]
+    columns = chosen.shape[-1]
     return pl.pallas_call(
         product_kernel,
         out_shape=jax.ShapeDtypeStruct((RB * width, columns), jnp.float32),
-        in_specs=[SMEM, SMEM, VMEM] + [VMEM] * len(chosen),
-        out_specs=VMEM,
-        scratch_shapes=[pltpu.VMEM((len(chosen), *chosen[0].shape), chosen[0].dtype)],
+        in_specs=[SMEM, SMEM, VMEM, VMEM],
+        out_specs=VMEM,
         compiler_params=pltpu.CompilerParams(vmem_limit_bytes=24 * MIB),
         name="block_products",
-    )(block_rows, counts, blocks, *chosen)
+    )(block_rows, counts, blocks, chosen)
 
 
 def gram_kernel(mine_ref, other_ref, own_ref, *refs):
@@ -508,12 +502,12 @@
         def run():
             swap = [(r, (r + members) % rows) for r in range(rows)]
             other = lax.ppermute(listed(lists, own, count), "rows", swap)
-            return pick(places, own, other, slots, members)
+            return order(exchange(pick(places, own, other, slots, members), rows), slots)
 
         return run
 
-    picked = lax.switch(far[0], [across_halves(count) for count in (*across, largest)])
-    return exchange(picked, rows)
+    chosen = lax.switch(far[0], [across_halves(count) for count in (*across, largest)])
+    return chosen.reshape(members, slots, height, columns)
 
 
 def moved(piece, rows, d):
@@ -532,9 +526,8 @@
     columns = sketch.shape[1]
     rows, cols = lax.axis_size("rows"), lax.axis_size("cols")
     chosen = fetch(sketch, block_cols, counts, slots, width)
-    if chosen[0].shape[1] % 16:
-        order = jnp.argsort(lax.axis_index("rows") % len(chosen) ^ jnp.array(distances(len(chosen))))
-        chosen = [jnp.stack(chosen)[order].swapaxes(0, 1).reshape(1, slots, width, columns)[0]]
+    if chosen.shape[2] % 16:
+        chosen = chosen.swapaxes(0, 1).reshape(1, slots, width, columns)
     partial_rows = block_products(block_rows, counts, blocks, chosen)
     if (rows, cols) == (16, 2):
         other = lax.ppermute(partial_rows, "cols", [(0, 1), (1, 0)])

time: 153 us -> 152 us (level); the launches traced: 151 us -> 155 us
  waiting for transfers between devices: 38.1 us -> 43.5 us
  starting transfers between devices: 38.9 us -> 36.9 us
    ppermute x14, waiting for transfers between devices: 8.94 us -> 12.4 us  [exchange(): lax.ppermute(piece, 'rows', [(r, r ^ d) for r in range(rows)])]
    ppermute x1, waiting for transfers between devices: 11.4 us -> 14.4 us  [run(): other = lax.ppermute(listed(lists, own, count), 'rows', swap)]
    ppermute x14, starting transfers between devices: 19.3 us -> 17.4 us  [exchange(): lax.ppermute(piece, 'rows', [(r, r ^ d) for r in range(rows)])]
where the time goes in v4:
time: 152 us; the launch traced here: 155 us
  Pallas kernels  69.6 us (46%)
  waiting for transfers between devices  43.5 us (29%)
  starting transfers between devices  36.9 us (24%)
  between operations  2.7 us (2%)
  local copies, waits for them, and re-layouts  1.6 us (1%)
    pallas_call x1, Pallas kernels, factor_and_basis(): pl.pallas_call(functools.partial(factor_kernel, total_rows), out_shape=(j...  61.8 us
    ppermute x14, starting transfers between devices, exchange(): lax.ppermute(piece, 'rows', [(r, r ^ d) for r in range(rows)])  17.4 us
    ppermute x1, waiting for transfers between devices, run(): other = lax.ppermute(listed(lists, own, count), 'rows', swap)  14.4 us
    ppermute x14, waiting for transfers between devices, exchange(): lax.ppermute(piece, 'rows', [(r, r ^ d) for r in range(rows)])  12.4 us
    ppermute x9, starting transfers between devices, moved(): return lax.ppermute(piece, 'rows', [(r, r ^ d) for r in range(rows)])  11.6 us
    ppermute x9, waiting for transfers between devices, moved(): return lax.ppermute(piece, 'rows', [(r, r ^ d) for r in range(rows)])  7.49 us
    all_to_all x1, starting transfers between devices, fetch(): lax.all_to_all(table, ('rows', 'cols'), split_axis=0, concat_axis=0, tile...  7.3 us
    all_to_all x1, waiting for transfers between devices, fetch(): lax.all_to_all(table, ('rows', 'cols'), split_axis=0, concat_axis=0, tile...  5.34 us
  transfers between devices with their start and end apart: 27, of which 19 were waited for; matrix products, arithmetic and copies ran while one was open for 0% of the time, Pallas kernels for 0%

profile of v4, /device:TPU:0, one launch (start us, length us, event | category | flops | bytes accessed | tf_op | source)
XLA Modules:
  0.0 154.7 jit_solution(13192331513359822771)
XLA Ops:
  1.3 1.3 table_copies.1
  2.6 7.3 %all-to-all-start = ((s32[32,1,128]{2,1,0:T(1,128)}), s32[32,1,128]{2,1,0:T(1,128)S(1)}, u32[]{:S(2)}, u32[]{:S(2)}) async-start(s32[32,1,128]{2,1,0:T(1,128)} %table_copies.1), calls=%async_computation | async-start | bytes 32768 | tf_op jit(solution)/shard_map/all_to_all | solution.py:490
  9.9 0.0 copy-start
  9.9 1.6 %copy-done = bf16[4096,256]{1,0:T(8,128)(2,1)S(1)} copy-done((bf16[4096,256]{1,0:T(8,128)(2,1)S(1)}, bf16[4096,256]{1,0:T(8,128)(2,1)}, u32[]{:S(2)}) %copy-start) | copy-done | bytes 2097176
  11.5 0.1 turn_stripes.1
  11.6 5.3 %all-to-all-done.table_ref = s32[32,1,128]{2,1,0:T(1,128)S(1)} async-done(((s32[32,1,128]{2,1,0:T(1,128)}), s32[32,1,128]{2,1,0:T(1,128)S(1)}, u32[]{:S(2)}, u32[]{:S(2)}) %all-to-all-start) | async-done | bytes 16416 | tf_op jit(solution)/shard_map/all_to_all | solution.py:490
  16.9 1.3 plan.1
  19.5 15.3 %conditional.2 = (bf16[128,32,256]{2,1,0:T(8,128)(2,1)S(1)}) conditional(s32[]{:T(128)} %bitcast.16, (s32[8,128]{1,0:T(8,128)S(1)}, bf16[8,16,32,256]{3,2,1,0:T(8,128)(2,1)S(1)}) %tuple.91, (s32[8,128]{1,0:T(8,128)S(1)}, bf16[8,16,32,256]{3,2,1,0:T(8,128)(2,1)S(1)}) %tuple.91, (s32[8,128]{1,0:T(8,128)S(1)}, ...), branch_computations={%region_0.0_spmd, %region_1.0_spmd, %region_2.0_spmd, %region_3.0_... | conditional | bytes 7340320 | solution.py:499
  19.6 0.7 cut_stripes.10
  20.2 0.6 collective-permute-start.14
  20.8 0.7 collective-permute-start.15
  21.5 1.4 collective-permute-start.16
  22.9 2.4 %collective-permute-start.17 = (bf16[7,32,256]{2,1,0:T(8,128)(2,1)S(1)}, bf16[7,32,256]{2,1,0:T(8,128)(2,1)S(1)}, u32[]{:S(2)}, u32[]{:S(2)}) collective-permute-start(bf16[7,32,256]{2,1,0:T(8,128)(2,1)S(1)} %get-tuple-element.174), channel_id=1, source_target_pairs={{0,10},{2,8},{4,14},{6,12},{8,2},{10,0},{12,6},{14,4},{16,26},{18,... | collective-permute-start | bytes 344072 | tf_op jit(solution)/shard_map/cond/branch_2_fun/ppermute | solution.py:473
  25.2 0.6 collective-permute-start.18
  25.9 1.4 collective-permute-start.19
  27.3 0.4 collective-permute-done.15.refs_2_
  27.7 2.0 %collective-permute-start.20 = (bf16[7,32,256]{2,1,0:T(8,128)(2,1)S(1)}, bf16[7,32,256]{2,1,0:T(8,128)(2,1)S(1)}, u32[]{:S(2)}, u32[]{:S(2)}) collective-permute-start(bf16[7,32,256]{2,1,0:T(8,128)(2,1)S(1)} %get-tuple-element.177), channel_id=1, source_target_pairs={{0,6},{2,4},{4,2},{6,0},{8,14},{10,12},{12,10},{14,8},{16,22},{18,... | collective-permute-start | bytes 344072 | tf_op jit(solution)/shard_map/cond/branch_2_fun/ppermute | solution.py:473
  29.6 0.6 collective-permute-done.17.refs_4_
  30.2 3.3 %collective-permute-done.18.refs_5_ = bf16[7,32,256]{2,1,0:T(8,128)(2,1)S(1)} collective-permute-done((bf16[7,32,256]{2,1,0:T(8,128)(2,1)S(1)}, bf16[7,32,256]{2,1,0:T(8,128)(2,1)S(1)}, u32[]{:S(2)}, u32[]{:S(2)}) %collective-permute-start.18) | collective-permute-done | bytes 114720 | tf_op jit(solution)/shard_map/cond/branch_2_fun/ppermute | solution.py:473
  33.5 1.2 collective-permute-done.20.refs_7_
  34.7 0.1 order_stripes.25
  34.8 0.0 copy-start.1
  34.8 0.0 copy-start.2
  34.8 32.0 %conditional.3 = (bf16[8,8,32,256]{3,2,1,0:T(8,128)(2,1)S(1)}) conditional(s32[]{:T(128)} %bitcast.15, (s32[8,128]{1,0:T(8,128)S(1)}, bf16[128,32,256]{2,1,0:T(8,128)(2,1)S(1)}, s32[8,128]{1,0:T(8,128)S(1)}) %tuple.92, (s32[8,128]{1,0:T(8,128)S(1)}, bf16[128,32,256]{2,1,0:T(8,128)(2,1)S(1)}, ...), branch_computations={%region_8.0_spmd, %region_9.0_spmd, %region_10.0_spmd, %region_11.... | conditional | bytes 7864648 | solution.py:509
  34.9 0.6 listed_stripes.21
  35.5 0.5 collective-permute-start.104
  36.1 14.4 %collective-permute-done.104.other_ref = bf16[17,32,256]{2,1,0:T(8,128)(2,1)S(1)} collective-permute-done((bf16[17,32,256]{2,1,0:T(8,128)(2,1)S(1)}, bf16[17,32,256]{2,1,0:T(8,128)(2,1)S(1)}, u32[]{:S(2)}, u32[]{:S(2)}) %collective-permute-start.104) | collective-permute-done | bytes 278560 | tf_op jit(solution)/shard_map/cond/branch_6_fun/ppermute | solution.py:504
  50.4 0.8 pick_stripes.21
  51.3 0.1 collective-permute-start.105
  51.3 0.1 collective-permute-start.106
  51.4 0.5 collective-permute-start.107
  51.9 4.4 %collective-permute-start.108 = (bf16[8,32,256]{2,1,0:T(8,128)(2,1)S(1)}, bf16[8,32,256]{2,1,0:T(8,128)(2,1)S(1)}, u32[]{:S(2)}, u32[]{:S(2)}) collective-permute-start(bf16[8,32,256]{2,1,0:T(8,128)(2,1)S(1)} %get-tuple-element.301), channel_id=1, source_target_pairs={{0,10},{2,8},{4,14},{6,12},{8,2},{10,0},{12,6},{14,4},{16,26},{18,... | collective-permute-start | bytes 393224 | tf_op jit(solution)/shard_map/cond/branch_6_fun/ppermute | solution.py:473
  56.3 0.0 collective-permute-done.105.refs_1_
  56.3 1.4 collective-permute-start.110
  57.7 1.1 collective-permute-done.106.refs_2_
  58.7 1.9 %collective-permute-start.111 = (bf16[8,32,256]{2,1,0:T(8,128)(2,1)S(1)}, bf16[8,32,256]{2,1,0:T(8,128)(2,1)S(1)}, u32[]{:S(2)}, u32[]{:S(2)}) collective-permute-start(bf16[8,32,256]{2,1,0:T(8,128)(2,1)S(1)} %get-tuple-element.304), channel_id=1, source_target_pairs={{0,6},{2,4},{4,2},{6,0},{8,14},{10,12},{12,10},{14,8},{16,22},{18,... | collective-permute-start | bytes 393224 | tf_op jit(solution)/shard_map/cond/branch_6_fun/ppermute | solution.py:473
  60.7 1.2 collective-permute-done.108.refs_4_
  61.9 3.4 %collective-permute-done.109.refs_5_ = bf16[8,32,256]{2,1,0:T(8,128)(2,1)S(1)} collective-permute-done((bf16[8,32,256]{2,1,0:T(8,128)(2,1)S(1)}, bf16[8,32,256]{2,1,0:T(8,128)(2,1)S(1)}, u32[]{:S(2)}, u32[]{:S(2)}) %collective-permute-start.109) | collective-permute-done | bytes 131104 | tf_op jit(solution)/shard_map/cond/branch_6_fun/ppermute | solution.py:473
  65.4 1.2 collective-permute-done.111.refs_7_
  66.5 0.1 order_stripes.37
  66.8 1.1 block_products.1.mine_ref
  67.9 0.1 collective-permute-start.176
  68.0 2.6 %collective-permute-done.176.other_ref = f32[1024,256]{1,0:T(8,128)S(1)} collective-permute-done((f32[1024,256]{1,0:T(8,128)S(1)}, f32[1024,256]{1,0:T(8,128)S(1)}, u32[]{:S(2)}, u32[]{:S(2)}) %collective-permute-start.176) | collective-permute-done | bytes 1048608 | tf_op jit(solution)/shard_map/ppermute | solution.py:533
  70.6 1.7 %sum_and_gram.1 = (f32[512,256]{1,0:T(8,128)S(1)}, f32[64,128]{1,0:T(8,128)S(1)}, f32[64,128]{1,0:T(8,128)S(1)}, f32[64,128]{1,0:T(8,128)S(1)}, f32[64,128]{1,0:T(8,128)S(1)}) custom-call(f32[1024,256]{1,0:T(8,128)S(1)} %block_products.1.mine_ref, f32[1024,256]{1,0:T(8,128)S(1)} %collective-permute-done.176.other_ref), custom_call_target="tpu_custom_call" | custom-call | tf_op jit(solution)/shard_map/sum_and_gram/pallas_call | solution.py:309
  72.4 1.0 collective-permute-start.177
  73.4 1.7 %collective-permute-start.178 = (f32[64,128]{1,0:T(8,128)S(1)}, f32[64,128]{1,0:T(8,128)S(1)}, u32[]{:S(2)}, u32[]{:S(2)}) collective-permute-start(f32[64,128]{1,0:T(8,128)S(1)} %get-tuple-element.410), channel_id=1, source_target_pairs={{0,2},{2,0},{4,6},{6,4},{8,10},{10,8},{12,14},{14,12},{16,18},{18,... | collective-permute-start | bytes 98312 | tf_op jit(solution)/shard_map/ppermute | solution.py:514
  75.0 0.9 collective-permute-start.179
  75.9 1.3 collective-permute-done.177.refs_1_
  77.3 0.0 collective-permute-done.178.refs_2_
  77.3 1.7 %collective-permute-done.179.refs_3_ = f32[64,128]{1,0:T(8,128)S(1)} collective-permute-done((f32[64,128]{1,0:T(8,128)S(1)}, f32[64,128]{1,0:T(8,128)S(1)}, u32[]{:S(2)}, u32[]{:S(2)}) %collective-permute-start.179) | collective-permute-done | bytes 32800 | tf_op jit(solution)/shard_map/ppermute | solution.py:514
  79.0 0.5 collective-permute-start.182
  79.5 1.0 collective-permute-start.181
  80.5 3.0 %collective-permute-start.180 = (f32[64,128]{1,0:T(8,128)S(1)}, f32[64,128]{1,0:T(8,128)S(1)}, u32[]{:S(2)}, u32[]{:S(2)}) collective-permute-start(f32[64,128]{1,0:T(8,128)S(1)} %add_pieces.1), channel_id=1, source_target_pairs={{0,8},{2,10},{4,12},{6,14},{8,0},{10,2},{12,4},{14,6},{16,24},{18,... | collective-permute-start | bytes 98312 | tf_op jit(solution)/shard_map/ppermute | solution.py:514
  83.4 1.3 collective-permute-done.182
  84.8 0.6 collective-permute-done.180
  85.3 1.3 collective-permute-start.185
  86.6 0.9 collective-permute-start.184
  87.6 1.3 collective-permute-start.183
  88.9 1.3 collective-permute-done.185.refs_3_
  90.2 0.4 collective-permute-done.184.refs_2_
  90.6 0.9 collective-permute-done.183.refs_1_
  91.5 0.1 collective-permute-start.186
  91.6 1.3 collective-permute-done.186.refs_1_
  92.9 61.8 %factor_and_basis.1 = (f32[512,256]{1,0:T(8,128)}, f32[256,256]{1,0:T(8,128)}) custom-call(f32[256,128]{1,0:T(8,128)S(1)} %stack_quarters.1.refs_0_, f32[256,128]{1,0:T(8,128)S(1)} %collective-permute-done.186.refs_1_, f32[512,256]{1,0:T(8,128)S(1)} %get-tuple-element.412.refs_2_), custom_call_target="tpu_custom_call" | custom-call | tf_op jit(solution)/shard_map/factor_and_basis/pallas_call | solution.py:456
  (12 shorter events, 0.1 us)
Async XLA Ops:
  2.6 14.4 %all-to-all-start = ((s32[32,1,128]{2,1,0:T(1,128)}), s32[32,1,128]{2,1,0:T(1,128)S(1)}, u32[]{:S(2)}, u32[]{:S(2)}) async-start(s32[32,1,128]{2,1,0:T(1,128)} %table_copies.1), calls=%async_computation | async-start | bytes 32768 | tf_op jit(solution)/shard_map/all_to_all | solution.py:490
  9.9 1.6 %copy-start = (bf16[4096,256]{1,0:T(8,128)(2,1)S(1)}, bf16[4096,256]{1,0:T(8,128)(2,1)}, u32[]{:S(2)}) copy-start(bf16[4096,256]{1,0:T(8,128)(2,1)} %param.28) | copy-start | bytes 6291460
  20.2 5.6 %collective-permute-start.14 = (bf16[7,32,256]{2,1,0:T(8,128)(2,1)S(1)}, bf16[7,32,256]{2,1,0:T(8,128)(2,1)S(1)}, u32[]{:S(2)}, u32[]{:S(2)}) collective-permute-start(bf16[7,32,256]{2,1,0:T(8,128)(2,1)S(1)} %get-tuple-element.171), channel_id=1, source_target_pairs={{0,2},{2,0},{4,6},{6,4},{8,10},{10,8},{12,14},{14,12},{16,18},{18,... | collective-permute-start | bytes 344072 | tf_op jit(solution)/shard_map/cond/branch_2_fun/ppermute | solution.py:473
  20.8 6.8 %collective-permute-start.15 = (bf16[7,32,256]{2,1,0:T(8,128)(2,1)S(1)}, bf16[7,32,256]{2,1,0:T(8,128)(2,1)S(1)}, u32[]{:S(2)}, u32[]{:S(2)}) collective-permute-start(bf16[7,32,256]{2,1,0:T(8,128)(2,1)S(1)} %get-tuple-element.172), channel_id=1, source_target_pairs={{0,12},{2,14},{4,8},{6,10},{8,4},{10,6},{12,0},{14,2},{16,28},{18,... | collective-permute-start | bytes 344072 | tf_op jit(solution)/shard_map/cond/branch_2_fun/ppermute | solution.py:473
  21.5 8.2 %collective-permute-start.16 = (bf16[7,32,256]{2,1,0:T(8,128)(2,1)S(1)}, bf16[7,32,256]{2,1,0:T(8,128)(2,1)S(1)}, u32[]{:S(2)}, u32[]{:S(2)}) collective-permute-start(bf16[7,32,256]{2,1,0:T(8,128)(2,1)S(1)} %get-tuple-element.173), channel_id=1, source_target_pairs={{0,4},{2,6},{4,0},{6,2},{8,12},{10,14},{12,8},{14,10},{16,20},{18,... | collective-permute-start | bytes 344072 | tf_op jit(solution)/shard_map/cond/branch_2_fun/ppermute | solution.py:473
  22.9 7.4 %collective-permute-start.17 = (bf16[7,32,256]{2,1,0:T(8,128)(2,1)S(1)}, bf16[7,32,256]{2,1,0:T(8,128)(2,1)S(1)}, u32[]{:S(2)}, u32[]{:S(2)}) collective-permute-start(bf16[7,32,256]{2,1,0:T(8,128)(2,1)S(1)} %get-tuple-element.174), channel_id=1, source_target_pairs={{0,10},{2,8},{4,14},{6,12},{8,2},{10,0},{12,6},{14,4},{16,26},{18,... | collective-permute-start | bytes 344072 | tf_op jit(solution)/shard_map/cond/branch_2_fun/ppermute | solution.py:473
  25.2 8.3 %collective-permute-start.18 = (bf16[7,32,256]{2,1,0:T(8,128)(2,1)S(1)}, bf16[7,32,256]{2,1,0:T(8,128)(2,1)S(1)}, u32[]{:S(2)}, u32[]{:S(2)}) collective-permute-start(bf16[7,32,256]{2,1,0:T(8,128)(2,1)S(1)} %get-tuple-element.175), channel_id=1, source_target_pairs={{0,14},{2,12},{4,10},{6,8},{8,6},{10,4},{12,2},{14,0},{16,30},{18,... | collective-permute-start | bytes 344072 | tf_op jit(solution)/shard_map/cond/branch_2_fun/ppermute | solution.py:473
  25.9 7.7 %collective-permute-start.19 = (bf16[7,32,256]{2,1,0:T(8,128)(2,1)S(1)}, bf16[7,32,256]{2,1,0:T(8,128)(2,1)S(1)}, u32[]{:S(2)}, u32[]{:S(2)}) collective-permute-start(bf16[7,32,256]{2,1,0:T(8,128)(2,1)S(1)} %get-tuple-element.176), channel_id=1, source_target_pairs={{0,8},{2,10},{4,12},{6,14},{8,0},{10,2},{12,4},{14,6},{16,24},{18,... | collective-permute-start | bytes 344072 | tf_op jit(solution)/shard_map/cond/branch_2_fun/ppermute | solution.py:473
  27.7 7.0 %collective-permute-start.20 = (bf16[7,32,256]{2,1,0:T(8,128)(2,1)S(1)}, bf16[7,32,256]{2,1,0:T(8,128)(2,1)S(1)}, u32[]{:S(2)}, u32[]{:S(2)}) collective-permute-start(bf16[7,32,256]{2,1,0:T(8,128)(2,1)S(1)} %get-tuple-element.177), channel_id=1, source_target_pairs={{0,6},{2,4},{4,2},{6,0},{8,14},{10,12},{12,10},{14,8},{16,22},{18,... | collective-permute-start | bytes 344072 | tf_op jit(solution)/shard_map/cond/branch_2_fun/ppermute | solution.py:473
  34.8 32.0 %copy-start.1 = (bf16[8,256,256]{2,1,0:T(8,128)(2,1)S(1)}, bf16[8,256,256]{2,1,0:T(8,128)(2,1)}, u32[]{:S(2)}) copy-start(bf16[8,256,256]{2,1,0:T(8,128)(2,1)} %blocks_ref.1) | copy-start | bytes 3145732
  34.8 32.0 %copy-start.2 = (s32[8]{0:T(128)S(1)}, s32[8]{0:T(128)}, u32[]{:S(2)}) copy-start(s32[8]{0:T(128)} %rows_ref.1) | copy-start | bytes 100
  35.5 14.9 %collective-permute-start.104 = (bf16[17,32,256]{2,1,0:T(8,128)(2,1)S(1)}, bf16[17,32,256]{2,1,0:T(8,128)(2,1)S(1)}, u32[]{:S(2)}, u32[]{:S(2)}) collective-permute-start(bf16[17,32,256]{2,1,0:T(8,128)(2,1)S(1)} %listed_stripes.21), channel_id=1, source_target_pairs={{0,16},{2,18},{4,20},{6,22},{8,24},{10,26},{12,28},{14,30},{16,0},... | collective-permute-start | bytes 835592 | tf_op jit(solution)/shard_map/cond/branch_6_fun/ppermute | solution.py:504
  51.3 5.0 %collective-permute-start.105 = (bf16[8,32,256]{2,1,0:T(8,128)(2,1)S(1)}, bf16[8,32,256]{2,1,0:T(8,128)(2,1)S(1)}, u32[]{:S(2)}, u32[]{:S(2)}) collective-permute-start(bf16[8,32,256]{2,1,0:T(8,128)(2,1)S(1)} %get-tuple-element.298), channel_id=1, source_target_pairs={{0,2},{2,0},{4,6},{6,4},{8,10},{10,8},{12,14},{14,12},{16,18},{18,... | collective-permute-start | bytes 393224 | tf_op jit(solution)/shard_map/cond/branch_6_fun/ppermute | solution.py:473
  51.3 7.4 %collective-permute-start.106 = (bf16[8,32,256]{2,1,0:T(8,128)(2,1)S(1)}, bf16[8,32,256]{2,1,0:T(8,128)(2,1)S(1)}, u32[]{:S(2)}, u32[]{:S(2)}) collective-permute-start(bf16[8,32,256]{2,1,0:T(8,128)(2,1)S(1)} %get-tuple-element.299), channel_id=1, source_target_pairs={{0,12},{2,14},{4,8},{6,10},{8,4},{10,6},{12,0},{14,2},{16,28},{18,... | collective-permute-start | bytes 393224 | tf_op jit(solution)/shard_map/cond/branch_6_fun/ppermute | solution.py:473
  51.4 9.3 %collective-permute-start.107 = (bf16[8,32,256]{2,1,0:T(8,128)(2,1)S(1)}, bf16[8,32,256]{2,1,0:T(8,128)(2,1)S(1)}, u32[]{:S(2)}, u32[]{:S(2)}) collective-permute-start(bf16[8,32,256]{2,1,0:T(8,128)(2,1)S(1)} %get-tuple-element.300), channel_id=1, source_target_pairs={{0,4},{2,6},{4,0},{6,2},{8,12},{10,14},{12,8},{14,10},{16,20},{18,... | collective-permute-start | bytes 393224 | tf_op jit(solution)/shard_map/cond/branch_6_fun/ppermute | solution.py:473
  51.9 10.1 %collective-permute-start.108 = (bf16[8,32,256]{2,1,0:T(8,128)(2,1)S(1)}, bf16[8,32,256]{2,1,0:T(8,128)(2,1)S(1)}, u32[]{:S(2)}, u32[]{:S(2)}) collective-permute-start(bf16[8,32,256]{2,1,0:T(8,128)(2,1)S(1)} %get-tuple-element.301), channel_id=1, source_target_pairs={{0,10},{2,8},{4,14},{6,12},{8,2},{10,0},{12,6},{14,4},{16,26},{18,... | collective-permute-start | bytes 393224 | tf_op jit(solution)/shard_map/cond/branch_6_fun/ppermute | solution.py:473
  56.3 9.1 %collective-permute-start.109 = (bf16[8,32,256]{2,1,0:T(8,128)(2,1)S(1)}, bf16[8,32,256]{2,1,0:T(8,128)(2,1)S(1)}, u32[]{:S(2)}, u32[]{:S(2)}) collective-permute-start(bf16[8,32,256]{2,1,0:T(8,128)(2,1)S(1)} %get-tuple-element.302), channel_id=1, source_target_pairs={{0,14},{2,12},{4,10},{6,8},{8,6},{10,4},{12,2},{14,0},{16,30},{18,... | collective-permute-start | bytes 393224 | tf_op jit(solution)/shard_map/cond/branch_6_fun/ppermute | solution.py:473
  56.3 9.1 %collective-permute-start.110 = (bf16[8,32,256]{2,1,0:T(8,128)(2,1)S(1)}, bf16[8,32,256]{2,1,0:T(8,128)(2,1)S(1)}, u32[]{:S(2)}, u32[]{:S(2)}) collective-permute-start(bf16[8,32,256]{2,1,0:T(8,128)(2,1)S(1)} %get-tuple-element.303), channel_id=1, source_target_pairs={{0,8},{2,10},{4,12},{6,14},{8,0},{10,2},{12,4},{14,6},{16,24},{18,... | collective-permute-start | bytes 393224 | tf_op jit(solution)/shard_map/cond/branch_6_fun/ppermute | solution.py:473
  58.7 7.8 %collective-permute-start.111 = (bf16[8,32,256]{2,1,0:T(8,128)(2,1)S(1)}, bf16[8,32,256]{2,1,0:T(8,128)(2,1)S(1)}, u32[]{:S(2)}, u32[]{:S(2)}) collective-permute-start(bf16[8,32,256]{2,1,0:T(8,128)(2,1)S(1)} %get-tuple-element.304), channel_id=1, source_target_pairs={{0,6},{2,4},{4,2},{6,0},{8,14},{10,12},{12,10},{14,8},{16,22},{18,... | collective-permute-start | bytes 393224 | tf_op jit(solution)/shard_map/cond/branch_6_fun/ppermute | solution.py:473
  67.9 2.7 %collective-permute-start.176 = (f32[1024,256]{1,0:T(8,128)S(1)}, f32[1024,256]{1,0:T(8,128)S(1)}, u32[]{:S(2)}, u32[]{:S(2)}) collective-permute-start(f32[1024,256]{1,0:T(8,128)S(1)} %block_products.1.mine_ref), channel_id=1, source_target_pairs={{0,1},{1,0},{2,3},{3,2},{4,5},{5,4},{6,7},{7,6},{8,9},{9,8},{10,11... | collective-permute-start | bytes 3145736 | tf_op jit(solution)/shard_map/ppermute | solution.py:533
  72.4 4.9 %collective-permute-start.177 = (f32[64,128]{1,0:T(8,128)S(1)}, f32[64,128]{1,0:T(8,128)S(1)}, u32[]{:S(2)}, u32[]{:S(2)}) collective-permute-start(f32[64,128]{1,0:T(8,128)S(1)} %get-tuple-element.409), channel_id=1, source_target_pairs={{0,6},{2,4},{4,2},{6,0},{8,14},{10,12},{12,10},{14,8},{16,22},{18,... | collective-permute-start | bytes 98312 | tf_op jit(solution)/shard_map/ppermute | solution.py:514
  73.4 3.9 %collective-permute-start.178 = (f32[64,128]{1,0:T(8,128)S(1)}, f32[64,128]{1,0:T(8,128)S(1)}, u32[]{:S(2)}, u32[]{:S(2)}) collective-permute-start(f32[64,128]{1,0:T(8,128)S(1)} %get-tuple-element.410), channel_id=1, source_target_pairs={{0,2},{2,0},{4,6},{6,4},{8,10},{10,8},{12,14},{14,12},{16,18},{18,... | collective-permute-start | bytes 98312 | tf_op jit(solution)/shard_map/ppermute | solution.py:514
  75.0 3.9 %collective-permute-start.179 = (f32[64,128]{1,0:T(8,128)S(1)}, f32[64,128]{1,0:T(8,128)S(1)}, u32[]{:S(2)}, u32[]{:S(2)}) collective-permute-start(f32[64,128]{1,0:T(8,128)S(1)} %get-tuple-element.411), channel_id=1, source_target_pairs={{0,4},{2,6},{4,0},{6,2},{8,12},{10,14},{12,8},{14,10},{16,20},{18,... | collective-permute-start | bytes 98312 | tf_op jit(solution)/shard_map/ppermute | solution.py:514
  79.0 5.8 %collective-permute-start.182 = (f32[64,128]{1,0:T(8,128)S(1)}, f32[64,128]{1,0:T(8,128)S(1)}, u32[]{:S(2)}, u32[]{:S(2)}) collective-permute-start(f32[64,128]{1,0:T(8,128)S(1)} %add_pieces.1), channel_id=1, source_target_pairs={{0,24},{2,26},{4,28},{6,30},{8,16},{10,18},{12,20},{14,22},{16,8},... | collective-permute-start | bytes 98312 | tf_op jit(solution)/shard_map/ppermute | solution.py:514
  79.5 5.3 %collective-permute-start.181 = (f32[64,128]{1,0:T(8,128)S(1)}, f32[64,128]{1,0:T(8,128)S(1)}, u32[]{:S(2)}, u32[]{:S(2)}) collective-permute-start(f32[64,128]{1,0:T(8,128)S(1)} %add_pieces.1), channel_id=1, source_target_pairs={{0,16},{2,18},{4,20},{6,22},{8,24},{10,26},{12,28},{14,30},{16,0},... | collective-permute-start | bytes 98312 | tf_op jit(solution)/shard_map/ppermute | solution.py:514
  80.5 4.9 %collective-permute-start.180 = (f32[64,128]{1,0:T(8,128)S(1)}, f32[64,128]{1,0:T(8,128)S(1)}, u32[]{:S(2)}, u32[]{:S(2)}) collective-permute-start(f32[64,128]{1,0:T(8,128)S(1)} %add_pieces.1), channel_id=1, source_target_pairs={{0,8},{2,10},{4,12},{6,14},{8,0},{10,2},{12,4},{14,6},{16,24},{18,... | collective-permute-start | bytes 98312 | tf_op jit(solution)/shard_map/ppermute | solution.py:514
  85.3 4.9 %collective-permute-start.185 = (f32[64,128]{1,0:T(8,128)S(1)}, f32[64,128]{1,0:T(8,128)S(1)}, u32[]{:S(2)}, u32[]{:S(2)}) collective-permute-start(f32[64,128]{1,0:T(8,128)S(1)} %add_add_fusion.refs_0_), channel_id=1, source_target_pairs={{0,6},{2,4},{4,2},{6,0},{8,14},{10,12},{12,10},{14,8},{16,22},{18,... | collective-permute-start | bytes 98312 | tf_op jit(solution)/shard_map/ppermute | solution.py:514
  86.6 4.0 %collective-permute-start.184 = (f32[64,128]{1,0:T(8,128)S(1)}, f32[64,128]{1,0:T(8,128)S(1)}, u32[]{:S(2)}, u32[]{:S(2)}) collective-permute-start(f32[64,128]{1,0:T(8,128)S(1)} %add_add_fusion.refs_0_), channel_id=1, source_target_pairs={{0,4},{2,6},{4,0},{6,2},{8,12},{10,14},{12,8},{14,10},{16,20},{18,... | collective-permute-start | bytes 98312 | tf_op jit(solution)/shard_map/ppermute | solution.py:514
  87.6 3.9 %collective-permute-start.183 = (f32[64,128]{1,0:T(8,128)S(1)}, f32[64,128]{1,0:T(8,128)S(1)}, u32[]{:S(2)}, u32[]{:S(2)}) collective-permute-start(f32[64,128]{1,0:T(8,128)S(1)} %add_add_fusion.refs_0_), channel_id=1, source_target_pairs={{0,2},{2,0},{4,6},{6,4},{8,10},{10,8},{12,14},{14,12},{16,18},{18,... | collective-permute-start | bytes 98312 | tf_op jit(solution)/shard_map/ppermute | solution.py:514
  91.5 1.4 collective-permute-start.186

commit v5 on v4

--- a/solution.py
+++ b/solution.py
@@ -160,7 +160,7 @@
         far = (members - 1) ^ near
         if near not in order and far:
             order += [near, far]
-    return [*order[:-2], members - 1, *order[-2:]] if members > 2 else list(range(members))
+    return [*order[:3], members - 1, *order[3:]] if members > 2 else list(range(members))
 
 
 def turn_kernel(sketch_ref, out_ref):

time: 152 us -> 153 us (level); the launches traced: 155 us -> 153 us
  waiting for transfers between devices: 43.5 us -> 40.8 us
    ppermute x14, waiting for transfers between devices: 12.4 us -> 10.5 us  [exchange(): lax.ppermute(piece, 'rows', [(r, r ^ d) for r in range(rows)])]
  transfers between devices with their start and end apart: 27 -> 27, of which waited for: 19 -> 23; matrix products, arithmetic and copies ran while one was open for 0% -> 0% of each run, Pallas kernels for 0% -> 0%
where the time goes in v5:
time: 153 us
  Pallas kernels  69.6 us (45%)
  waiting for transfers between devices  40.8 us (27%)
  starting transfers between devices  37.9 us (25%)
  between operations  2.7 us (2%)
  local copies, waits for them, and re-layouts  1.6 us (1%)
    pallas_call x1, Pallas kernels, factor_and_basis(): pl.pallas_call(functools.partial(factor_kernel, total_rows), out_shape=(j...  61.8 us
    ppermute x14, starting transfers between devices, exchange(): lax.ppermute(piece, 'rows', [(r, r ^ d) for r in range(rows)])  18.4 us
    ppermute x1, waiting for transfers between devices, run(): other = lax.ppermute(listed(lists, own, count), 'rows', swap)  13.3 us
    ppermute x9, starting transfers between devices, moved(): return lax.ppermute(piece, 'rows', [(r, r ^ d) for r in range(rows)])  11.6 us
    ppermute x14, waiting for transfers between devices, exchange(): lax.ppermute(piece, 'rows', [(r, r ^ d) for r in range(rows)])  10.5 us
    ppermute x9, waiting for transfers between devices, moved(): return lax.ppermute(piece, 'rows', [(r, r ^ d) for r in range(rows)])  7.64 us
    all_to_all x1, starting transfers between devices, fetch(): lax.all_to_all(table, ('rows', 'cols'), split_axis=0, concat_axis=0, tile...  7.3 us
    all_to_all x1, waiting for transfers between devices, fetch(): lax.all_to_all(table, ('rows', 'cols'), split_axis=0, concat_axis=0, tile...  5.34 us
  transfers between devices with their start and end apart: 27, of which 23 were waited for; matrix products, arithmetic and copies ran while one was open for 0% of the time, Pallas kernels for 0%

profile of v5, /device:TPU:0, one launch (start us, length us, event | category | flops | bytes accessed | tf_op | source)
XLA Modules:
  0.0 153.0 jit_solution(99033242680006182)
XLA Ops:
  1.3 1.3 table_copies.1
  2.6 7.3 %all-to-all-start = ((s32[32,1,128]{2,1,0:T(1,128)}), s32[32,1,128]{2,1,0:T(1,128)S(1)}, u32[]{:S(2)}, u32[]{:S(2)}) async-start(s32[32,1,128]{2,1,0:T(1,128)} %table_copies.1), calls=%async_computation | async-start | bytes 32768 | tf_op jit(solution)/shard_map/all_to_all | solution.py:490
  9.9 1.6 %copy-done = bf16[4096,256]{1,0:T(8,128)(2,1)S(1)} copy-done((bf16[4096,256]{1,0:T(8,128)(2,1)S(1)}, bf16[4096,256]{1,0:T(8,128)(2,1)}, u32[]{:S(2)}) %copy-start) | copy-done | bytes 2097176
  11.5 0.1 turn_stripes.1
  11.6 5.3 %all-to-all-done.table_ref = s32[32,1,128]{2,1,0:T(1,128)S(1)} async-done(((s32[32,1,128]{2,1,0:T(1,128)}), s32[32,1,128]{2,1,0:T(1,128)S(1)}, u32[]{:S(2)}, u32[]{:S(2)}) %all-to-all-start) | async-done | bytes 16416 | tf_op jit(solution)/shard_map/all_to_all | solution.py:490
  16.9 1.3 plan.1
  19.5 13.8 %conditional.2 = (bf16[128,32,256]{2,1,0:T(8,128)(2,1)S(1)}) conditional(s32[]{:T(128)} %bitcast.16, (s32[8,128]{1,0:T(8,128)S(1)}, bf16[8,16,32,256]{3,2,1,0:T(8,128)(2,1)S(1)}) %tuple.91, (s32[8,128]{1,0:T(8,128)S(1)}, bf16[8,16,32,256]{3,2,1,0:T(8,128)(2,1)S(1)}) %tuple.91, (s32[8,128]{1,0:T(8,128)S(1)}, ...), branch_computations={%region_0.0_spmd, %region_1.0_spmd, %region_2.0_spmd, %region_3.0_... | conditional | bytes 7340320 | solution.py:499
  19.6 0.7 cut_stripes.9
  20.2 0.6 collective-permute-start.7
  20.8 0.7 collective-permute-start.8
  21.5 3.2 %collective-permute-start.9 = (bf16[6,32,256]{2,1,0:T(8,128)(2,1)S(1)}, bf16[6,32,256]{2,1,0:T(8,128)(2,1)S(1)}, u32[]{:S(2)}, u32[]{:S(2)}) collective-permute-start(bf16[6,32,256]{2,1,0:T(8,128)(2,1)S(1)} %get-tuple-element.155), channel_id=1, source_target_pairs={{0,14},{2,12},{4,10},{6,8},{8,6},{10,4},{12,2},{14,0},{16,30},{18,... | collective-permute-start | bytes 294920 | tf_op jit(solution)/shard_map/cond/branch_1_fun/ppermute | solution.py:473
  24.7 0.5 collective-permute-start.10
  25.2 0.6 collective-permute-start.11
  25.9 1.4 collective-permute-start.12
  27.3 0.3 collective-permute-done.8.refs_2_
  27.6 2.1 %collective-permute-start.13 = (bf16[6,32,256]{2,1,0:T(8,128)(2,1)S(1)}, bf16[6,32,256]{2,1,0:T(8,128)(2,1)S(1)}, u32[]{:S(2)}, u32[]{:S(2)}) collective-permute-start(bf16[6,32,256]{2,1,0:T(8,128)(2,1)S(1)} %get-tuple-element.163), channel_id=1, source_target_pairs={{0,6},{2,4},{4,2},{6,0},{8,14},{10,12},{12,10},{14,8},{16,22},{18,... | collective-permute-start | bytes 294920 | tf_op jit(solution)/shard_map/cond/branch_1_fun/ppermute | solution.py:473
  29.6 0.1 collective-permute-done.9.refs_3_
  29.7 2.2 %collective-permute-done.10.refs_4_ = bf16[6,32,256]{2,1,0:T(8,128)(2,1)S(1)} collective-permute-done((bf16[6,32,256]{2,1,0:T(8,128)(2,1)S(1)}, bf16[6,32,256]{2,1,0:T(8,128)(2,1)S(1)}, u32[]{:S(2)}, u32[]{:S(2)}) %collective-permute-start.10) | collective-permute-done | bytes 98336 | tf_op jit(solution)/shard_map/cond/branch_1_fun/ppermute | solution.py:473
  31.9 1.3 collective-permute-done.13.refs_7_
  33.3 0.1 order_stripes.24
  33.4 0.0 copy-start.1
  33.4 31.5 %conditional.3 = (bf16[8,8,32,256]{3,2,1,0:T(8,128)(2,1)S(1)}) conditional(s32[]{:T(128)} %bitcast.15, (s32[8,128]{1,0:T(8,128)S(1)}, bf16[128,32,256]{2,1,0:T(8,128)(2,1)S(1)}, s32[8,128]{1,0:T(8,128)S(1)}) %tuple.92, (s32[8,128]{1,0:T(8,128)S(1)}, bf16[128,32,256]{2,1,0:T(8,128)(2,1)S(1)}, ...), branch_computations={%region_8.0_spmd, %region_9.0_spmd, %region_10.0_spmd, %region_11.... | conditional | bytes 7864648 | solution.py:509
  33.4 0.6 listed_stripes.21
  34.1 0.5 collective-permute-start.104
  34.6 13.3 %collective-permute-done.104.other_ref = bf16[17,32,256]{2,1,0:T(8,128)(2,1)S(1)} collective-permute-done((bf16[17,32,256]{2,1,0:T(8,128)(2,1)S(1)}, bf16[17,32,256]{2,1,0:T(8,128)(2,1)S(1)}, u32[]{:S(2)}, u32[]{:S(2)}) %collective-permute-start.104) | collective-permute-done | bytes 278560 | tf_op jit(solution)/shard_map/cond/branch_6_fun/ppermute | solution.py:504
  47.9 0.8 pick_stripes.21
  48.8 1.3 collective-permute-start.105
  50.1 3.2 %collective-permute-start.107 = (bf16[8,32,256]{2,1,0:T(8,128)(2,1)S(1)}, bf16[8,32,256]{2,1,0:T(8,128)(2,1)S(1)}, u32[]{:S(2)}, u32[]{:S(2)}) collective-permute-start(bf16[8,32,256]{2,1,0:T(8,128)(2,1)S(1)} %get-tuple-element.300), channel_id=1, source_target_pairs={{0,14},{2,12},{4,10},{6,8},{8,6},{10,4},{12,2},{14,0},{16,30},{18,... | collective-permute-start | bytes 393224 | tf_op jit(solution)/shard_map/cond/branch_6_fun/ppermute | solution.py:473
  53.2 0.9 collective-permute-start.108
  54.1 0.3 collective-permute-start.109
  54.5 0.2 collective-permute-done.105.refs_1_
  54.7 2.2 %collective-permute-start.110 = (bf16[8,32,256]{2,1,0:T(8,128)(2,1)S(1)}, bf16[8,32,256]{2,1,0:T(8,128)(2,1)S(1)}, u32[]{:S(2)}, u32[]{:S(2)}) collective-permute-start(bf16[8,32,256]{2,1,0:T(8,128)(2,1)S(1)} %get-tuple-element.303), channel_id=1, source_target_pairs={{0,8},{2,10},{4,12},{6,14},{8,0},{10,2},{12,4},{14,6},{16,24},{18,... | collective-permute-start | bytes 393224 | tf_op jit(solution)/shard_map/cond/branch_6_fun/ppermute | solution.py:473
  56.9 0.6 collective-permute-done.106.refs_2_
  57.5 1.4 collective-permute-start.111
  58.9 1.7 %collective-permute-done.107.refs_3_ = bf16[8,32,256]{2,1,0:T(8,128)(2,1)S(1)} collective-permute-done((bf16[8,32,256]{2,1,0:T(8,128)(2,1)S(1)}, bf16[8,32,256]{2,1,0:T(8,128)(2,1)S(1)}, u32[]{:S(2)}, u32[]{:S(2)}) %collective-permute-start.107) | collective-permute-done | bytes 131104 | tf_op jit(solution)/shard_map/cond/branch_6_fun/ppermute | solution.py:473
  60.5 2.5 %collective-permute-done.108.refs_4_ = bf16[8,32,256]{2,1,0:T(8,128)(2,1)S(1)} collective-permute-done((bf16[8,32,256]{2,1,0:T(8,128)(2,1)S(1)}, bf16[8,32,256]{2,1,0:T(8,128)(2,1)S(1)}, u32[]{:S(2)}, u32[]{:S(2)}) %collective-permute-start.108) | collective-permute-done | bytes 131104 | tf_op jit(solution)/shard_map/cond/branch_6_fun/ppermute | solution.py:473
  63.1 0.4 collective-permute-done.110.refs_6_
  63.5 1.1 collective-permute-done.111.refs_7_
  64.6 0.1 order_stripes.37
  64.9 1.1 block_products.1.mine_ref
  66.0 0.1 collective-permute-start.176
  66.1 2.6 %collective-permute-done.176.other_ref = f32[1024,256]{1,0:T(8,128)S(1)} collective-permute-done((f32[1024,256]{1,0:T(8,128)S(1)}, f32[1024,256]{1,0:T(8,128)S(1)}, u32[]{:S(2)}, u32[]{:S(2)}) %collective-permute-start.176) | collective-permute-done | bytes 1048608 | tf_op jit(solution)/shard_map/ppermute | solution.py:533
  68.7 1.7 %sum_and_gram.1 = (f32[512,256]{1,0:T(8,128)S(1)}, f32[64,128]{1,0:T(8,128)S(1)}, f32[64,128]{1,0:T(8,128)S(1)}, f32[64,128]{1,0:T(8,128)S(1)}, f32[64,128]{1,0:T(8,128)S(1)}) custom-call(f32[1024,256]{1,0:T(8,128)S(1)} %block_products.1.mine_ref, f32[1024,256]{1,0:T(8,128)S(1)} %collective-permute-done.176.other_ref), custom_call_target="tpu_custom_call" | custom-call | tf_op jit(solution)/shard_map/sum_and_gram/pallas_call | solution.py:309
  70.5 1.3 collective-permute-start.177
  71.8 0.9 collective-permute-start.178
  72.6 1.4 collective-permute-start.179
  74.0 1.4 collective-permute-done.177.refs_1_
  75.5 0.2 collective-permute-done.178.refs_2_
  75.7 0.9 collective-permute-done.179.refs_3_
  76.6 1.0 collective-permute-start.182
  77.6 1.1 collective-permute-start.181
  78.6 2.4 %collective-permute-start.180 = (f32[64,128]{1,0:T(8,128)S(1)}, f32[64,128]{1,0:T(8,128)S(1)}, u32[]{:S(2)}, u32[]{:S(2)}) collective-permute-start(f32[64,128]{1,0:T(8,128)S(1)} %add_pieces.1), channel_id=1, source_target_pairs={{0,8},{2,10},{4,12},{6,14},{8,0},{10,2},{12,4},{14,6},{16,24},{18,... | collective-permute-start | bytes 98312 | tf_op jit(solution)/shard_map/ppermute | solution.py:514
  81.0 1.4 collective-permute-done.182
  82.4 0.8 collective-permute-done.181
  83.1 0.1 collective-permute-done.180
  83.2 1.9 %collective-permute-start.185 = (f32[64,128]{1,0:T(8,128)S(1)}, f32[64,128]{1,0:T(8,128)S(1)}, u32[]{:S(2)}, u32[]{:S(2)}) collective-permute-start(f32[64,128]{1,0:T(8,128)S(1)} %add_add_fusion.refs_0_), channel_id=1, source_target_pairs={{0,6},{2,4},{4,2},{6,0},{8,14},{10,12},{12,10},{14,8},{16,22},{18,... | collective-permute-start | bytes 98312 | tf_op jit(solution)/shard_map/ppermute | solution.py:514
  85.2 0.6 collective-permute-start.184
  85.8 1.0 collective-permute-start.183
  86.8 1.3 collective-permute-done.185.refs_3_
  88.1 1.0 collective-permute-done.184.refs_2_
  89.1 0.6 collective-permute-done.183.refs_1_
  89.7 0.1 collective-permute-start.186
  89.8 1.3 collective-permute-done.186.refs_1_
  91.1 61.8 %factor_and_basis.1 = (f32[512,256]{1,0:T(8,128)}, f32[256,256]{1,0:T(8,128)}) custom-call(f32[256,128]{1,0:T(8,128)S(1)} %stack_quarters.1.refs_0_, f32[256,128]{1,0:T(8,128)S(1)} %collective-permute-done.186.refs_1_, f32[512,256]{1,0:T(8,128)S(1)} %get-tuple-element.412.refs_2_), custom_call_target="tpu_custom_call" | custom-call | tf_op jit(solution)/shard_map/factor_and_basis/pallas_call | solution.py:456
  (12 shorter events, 0.1 us)
Async XLA Ops:
  2.6 14.4 %all-to-all-start = ((s32[32,1,128]{2,1,0:T(1,128)}), s32[32,1,128]{2,1,0:T(1,128)S(1)}, u32[]{:S(2)}, u32[]{:S(2)}) async-start(s32[32,1,128]{2,1,0:T(1,128)} %table_copies.1), calls=%async_computation | async-start | bytes 32768 | tf_op jit(solution)/shard_map/all_to_all | solution.py:490
  9.9 1.6 %copy-start = (bf16[4096,256]{1,0:T(8,128)(2,1)S(1)}, bf16[4096,256]{1,0:T(8,128)(2,1)}, u32[]{:S(2)}) copy-start(bf16[4096,256]{1,0:T(8,128)(2,1)} %param.28) | copy-start | bytes 6291460
  20.2 5.6 %collective-permute-start.7 = (bf16[6,32,256]{2,1,0:T(8,128)(2,1)S(1)}, bf16[6,32,256]{2,1,0:T(8,128)(2,1)S(1)}, u32[]{:S(2)}, u32[]{:S(2)}) collective-permute-start(bf16[6,32,256]{2,1,0:T(8,128)(2,1)S(1)} %get-tuple-element.153), channel_id=1, source_target_pairs={{0,2},{2,0},{4,6},{6,4},{8,10},{10,8},{12,14},{14,12},{16,18},{18,... | collective-permute-start | bytes 294920 | tf_op jit(solution)/shard_map/cond/branch_1_fun/ppermute | solution.py:473
  20.8 6.8 %collective-permute-start.8 = (bf16[6,32,256]{2,1,0:T(8,128)(2,1)S(1)}, bf16[6,32,256]{2,1,0:T(8,128)(2,1)S(1)}, u32[]{:S(2)}, u32[]{:S(2)}) collective-permute-start(bf16[6,32,256]{2,1,0:T(8,128)(2,1)S(1)} %get-tuple-element.154), channel_id=1, source_target_pairs={{0,12},{2,14},{4,8},{6,10},{8,4},{10,6},{12,0},{14,2},{16,28},{18,... | collective-permute-start | bytes 294920 | tf_op jit(solution)/shard_map/cond/branch_1_fun/ppermute | solution.py:473
  21.5 8.3 %collective-permute-start.9 = (bf16[6,32,256]{2,1,0:T(8,128)(2,1)S(1)}, bf16[6,32,256]{2,1,0:T(8,128)(2,1)S(1)}, u32[]{:S(2)}, u32[]{:S(2)}) collective-permute-start(bf16[6,32,256]{2,1,0:T(8,128)(2,1)S(1)} %get-tuple-element.155), channel_id=1, source_target_pairs={{0,14},{2,12},{4,10},{6,8},{8,6},{10,4},{12,2},{14,0},{16,30},{18,... | collective-permute-start | bytes 294920 | tf_op jit(solution)/shard_map/cond/branch_1_fun/ppermute | solution.py:473
  24.7 7.2 %collective-permute-start.10 = (bf16[6,32,256]{2,1,0:T(8,128)(2,1)S(1)}, bf16[6,32,256]{2,1,0:T(8,128)(2,1)S(1)}, u32[]{:S(2)}, u32[]{:S(2)}) collective-permute-start(bf16[6,32,256]{2,1,0:T(8,128)(2,1)S(1)} %get-tuple-element.160), channel_id=1, source_target_pairs={{0,4},{2,6},{4,0},{6,2},{8,12},{10,14},{12,8},{14,10},{16,20},{18,... | collective-permute-start | bytes 294920 | tf_op jit(solution)/shard_map/cond/branch_1_fun/ppermute | solution.py:473
  25.2 6.7 %collective-permute-start.11 = (bf16[6,32,256]{2,1,0:T(8,128)(2,1)S(1)}, bf16[6,32,256]{2,1,0:T(8,128)(2,1)S(1)}, u32[]{:S(2)}, u32[]{:S(2)}) collective-permute-start(bf16[6,32,256]{2,1,0:T(8,128)(2,1)S(1)} %get-tuple-element.161), channel_id=1, source_target_pairs={{0,10},{2,8},{4,14},{6,12},{8,2},{10,0},{12,6},{14,4},{16,26},{18,... | collective-permute-start | bytes 294920 | tf_op jit(solution)/shard_map/cond/branch_1_fun/ppermute | solution.py:473
  25.9 6.0 %collective-permute-start.12 = (bf16[6,32,256]{2,1,0:T(8,128)(2,1)S(1)}, bf16[6,32,256]{2,1,0:T(8,128)(2,1)S(1)}, u32[]{:S(2)}, u32[]{:S(2)}) collective-permute-start(bf16[6,32,256]{2,1,0:T(8,128)(2,1)S(1)} %get-tuple-element.162), channel_id=1, source_target_pairs={{0,8},{2,10},{4,12},{6,14},{8,0},{10,2},{12,4},{14,6},{16,24},{18,... | collective-permute-start | bytes 294920 | tf_op jit(solution)/shard_map/cond/branch_1_fun/ppermute | solution.py:473
  27.6 5.7 %collective-permute-start.13 = (bf16[6,32,256]{2,1,0:T(8,128)(2,1)S(1)}, bf16[6,32,256]{2,1,0:T(8,128)(2,1)S(1)}, u32[]{:S(2)}, u32[]{:S(2)}) collective-permute-start(bf16[6,32,256]{2,1,0:T(8,128)(2,1)S(1)} %get-tuple-element.163), channel_id=1, source_target_pairs={{0,6},{2,4},{4,2},{6,0},{8,14},{10,12},{12,10},{14,8},{16,22},{18,... | collective-permute-start | bytes 294920 | tf_op jit(solution)/shard_map/cond/branch_1_fun/ppermute | solution.py:473
  33.4 31.6 %copy-start.1 = (bf16[8,256,256]{2,1,0:T(8,128)(2,1)S(1)}, bf16[8,256,256]{2,1,0:T(8,128)(2,1)}, u32[]{:S(2)}) copy-start(bf16[8,256,256]{2,1,0:T(8,128)(2,1)} %blocks_ref.1) | copy-start | bytes 3145732
  33.4 31.6 %copy-start.2 = (s32[8]{0:T(128)S(1)}, s32[8]{0:T(128)}, u32[]{:S(2)}) copy-start(s32[8]{0:T(128)} %rows_ref.1) | copy-start | bytes 100
  34.1 13.9 %collective-permute-start.104 = (bf16[17,32,256]{2,1,0:T(8,128)(2,1)S(1)}, bf16[17,32,256]{2,1,0:T(8,128)(2,1)S(1)}, u32[]{:S(2)}, u32[]{:S(2)}) collective-permute-start(bf16[17,32,256]{2,1,0:T(8,128)(2,1)S(1)} %listed_stripes.21), channel_id=1, source_target_pairs={{0,16},{2,18},{4,20},{6,22},{8,24},{10,26},{12,28},{14,30},{16,0},... | collective-permute-start | bytes 835592 | tf_op jit(solution)/shard_map/cond/branch_6_fun/ppermute | solution.py:504
  48.8 5.9 %collective-permute-start.105 = (bf16[8,32,256]{2,1,0:T(8,128)(2,1)S(1)}, bf16[8,32,256]{2,1,0:T(8,128)(2,1)S(1)}, u32[]{:S(2)}, u32[]{:S(2)}) collective-permute-start(bf16[8,32,256]{2,1,0:T(8,128)(2,1)S(1)} %get-tuple-element.298), channel_id=1, source_target_pairs={{0,2},{2,0},{4,6},{6,4},{8,10},{10,8},{12,14},{14,12},{16,18},{18,... | collective-permute-start | bytes 393224 | tf_op jit(solution)/shard_map/cond/branch_6_fun/ppermute | solution.py:473
  50.1 7.4 %collective-permute-start.106 = (bf16[8,32,256]{2,1,0:T(8,128)(2,1)S(1)}, bf16[8,32,256]{2,1,0:T(8,128)(2,1)S(1)}, u32[]{:S(2)}, u32[]{:S(2)}) collective-permute-start(bf16[8,32,256]{2,1,0:T(8,128)(2,1)S(1)} %get-tuple-element.299), channel_id=1, source_target_pairs={{0,12},{2,14},{4,8},{6,10},{8,4},{10,6},{12,0},{14,2},{16,28},{18,... | collective-permute-start | bytes 393224 | tf_op jit(solution)/shard_map/cond/branch_6_fun/ppermute | solution.py:473
  50.1 10.5 %collective-permute-start.107 = (bf16[8,32,256]{2,1,0:T(8,128)(2,1)S(1)}, bf16[8,32,256]{2,1,0:T(8,128)(2,1)S(1)}, u32[]{:S(2)}, u32[]{:S(2)}) collective-permute-start(bf16[8,32,256]{2,1,0:T(8,128)(2,1)S(1)} %get-tuple-element.300), channel_id=1, source_target_pairs={{0,14},{2,12},{4,10},{6,8},{8,6},{10,4},{12,2},{14,0},{16,30},{18,... | collective-permute-start | bytes 393224 | tf_op jit(solution)/shard_map/cond/branch_6_fun/ppermute | solution.py:473
  53.2 9.8 %collective-permute-start.108 = (bf16[8,32,256]{2,1,0:T(8,128)(2,1)S(1)}, bf16[8,32,256]{2,1,0:T(8,128)(2,1)S(1)}, u32[]{:S(2)}, u32[]{:S(2)}) collective-permute-start(bf16[8,32,256]{2,1,0:T(8,128)(2,1)S(1)} %get-tuple-element.301), channel_id=1, source_target_pairs={{0,4},{2,6},{4,0},{6,2},{8,12},{10,14},{12,8},{14,10},{16,20},{18,... | collective-permute-start | bytes 393224 | tf_op jit(solution)/shard_map/cond/branch_6_fun/ppermute | solution.py:473
  54.1 8.9 %collective-permute-start.109 = (bf16[8,32,256]{2,1,0:T(8,128)(2,1)S(1)}, bf16[8,32,256]{2,1,0:T(8,128)(2,1)S(1)}, u32[]{:S(2)}, u32[]{:S(2)}) collective-permute-start(bf16[8,32,256]{2,1,0:T(8,128)(2,1)S(1)} %get-tuple-element.302), channel_id=1, source_target_pairs={{0,10},{2,8},{4,14},{6,12},{8,2},{10,0},{12,6},{14,4},{16,26},{18,... | collective-permute-start | bytes 393224 | tf_op jit(solution)/shard_map/cond/branch_6_fun/ppermute | solution.py:473
  54.7 8.8 %collective-permute-start.110 = (bf16[8,32,256]{2,1,0:T(8,128)(2,1)S(1)}, bf16[8,32,256]{2,1,0:T(8,128)(2,1)S(1)}, u32[]{:S(2)}, u32[]{:S(2)}) collective-permute-start(bf16[8,32,256]{2,1,0:T(8,128)(2,1)S(1)} %get-tuple-element.303), channel_id=1, source_target_pairs={{0,8},{2,10},{4,12},{6,14},{8,0},{10,2},{12,4},{14,6},{16,24},{18,... | collective-permute-start | bytes 393224 | tf_op jit(solution)/shard_map/cond/branch_6_fun/ppermute | solution.py:473
  57.5 7.2 %collective-permute-start.111 = (bf16[8,32,256]{2,1,0:T(8,128)(2,1)S(1)}, bf16[8,32,256]{2,1,0:T(8,128)(2,1)S(1)}, u32[]{:S(2)}, u32[]{:S(2)}) collective-permute-start(bf16[8,32,256]{2,1,0:T(8,128)(2,1)S(1)} %get-tuple-element.304), channel_id=1, source_target_pairs={{0,6},{2,4},{4,2},{6,0},{8,14},{10,12},{12,10},{14,8},{16,22},{18,... | collective-permute-start | bytes 393224 | tf_op jit(solution)/shard_map/cond/branch_6_fun/ppermute | solution.py:473
  66.0 2.7 %collective-permute-start.176 = (f32[1024,256]{1,0:T(8,128)S(1)}, f32[1024,256]{1,0:T(8,128)S(1)}, u32[]{:S(2)}, u32[]{:S(2)}) collective-permute-start(f32[1024,256]{1,0:T(8,128)S(1)} %block_products.1.mine_ref), channel_id=1, source_target_pairs={{0,1},{1,0},{2,3},{3,2},{4,5},{5,4},{6,7},{7,6},{8,9},{9,8},{10,11... | collective-permute-start | bytes 3145736 | tf_op jit(solution)/shard_map/ppermute | solution.py:533
  70.5 5.0 %collective-permute-start.177 = (f32[64,128]{1,0:T(8,128)S(1)}, f32[64,128]{1,0:T(8,128)S(1)}, u32[]{:S(2)}, u32[]{:S(2)}) collective-permute-start(f32[64,128]{1,0:T(8,128)S(1)} %get-tuple-element.409), channel_id=1, source_target_pairs={{0,6},{2,4},{4,2},{6,0},{8,14},{10,12},{12,10},{14,8},{16,22},{18,... | collective-permute-start | bytes 98312 | tf_op jit(solution)/shard_map/ppermute | solution.py:514
  71.8 3.9 %collective-permute-start.178 = (f32[64,128]{1,0:T(8,128)S(1)}, f32[64,128]{1,0:T(8,128)S(1)}, u32[]{:S(2)}, u32[]{:S(2)}) collective-permute-start(f32[64,128]{1,0:T(8,128)S(1)} %get-tuple-element.410), channel_id=1, source_target_pairs={{0,2},{2,0},{4,6},{6,4},{8,10},{10,8},{12,14},{14,12},{16,18},{18,... | collective-permute-start | bytes 98312 | tf_op jit(solution)/shard_map/ppermute | solution.py:514
  72.6 3.9 %collective-permute-start.179 = (f32[64,128]{1,0:T(8,128)S(1)}, f32[64,128]{1,0:T(8,128)S(1)}, u32[]{:S(2)}, u32[]{:S(2)}) collective-permute-start(f32[64,128]{1,0:T(8,128)S(1)} %get-tuple-element.411), channel_id=1, source_target_pairs={{0,4},{2,6},{4,0},{6,2},{8,12},{10,14},{12,8},{14,10},{16,20},{18,... | collective-permute-start | bytes 98312 | tf_op jit(solution)/shard_map/ppermute | solution.py:514
  76.6 5.8 %collective-permute-start.182 = (f32[64,128]{1,0:T(8,128)S(1)}, f32[64,128]{1,0:T(8,128)S(1)}, u32[]{:S(2)}, u32[]{:S(2)}) collective-permute-start(f32[64,128]{1,0:T(8,128)S(1)} %add_pieces.1), channel_id=1, source_target_pairs={{0,24},{2,26},{4,28},{6,30},{8,16},{10,18},{12,20},{14,22},{16,8},... | collective-permute-start | bytes 98312 | tf_op jit(solution)/shard_map/ppermute | solution.py:514
  77.6 5.6 %collective-permute-start.181 = (f32[64,128]{1,0:T(8,128)S(1)}, f32[64,128]{1,0:T(8,128)S(1)}, u32[]{:S(2)}, u32[]{:S(2)}) collective-permute-start(f32[64,128]{1,0:T(8,128)S(1)} %add_pieces.1), channel_id=1, source_target_pairs={{0,16},{2,18},{4,20},{6,22},{8,24},{10,26},{12,28},{14,30},{16,0},... | collective-permute-start | bytes 98312 | tf_op jit(solution)/shard_map/ppermute | solution.py:514
  78.6 4.6 %collective-permute-start.180 = (f32[64,128]{1,0:T(8,128)S(1)}, f32[64,128]{1,0:T(8,128)S(1)}, u32[]{:S(2)}, u32[]{:S(2)}) collective-permute-start(f32[64,128]{1,0:T(8,128)S(1)} %add_pieces.1), channel_id=1, source_target_pairs={{0,8},{2,10},{4,12},{6,14},{8,0},{10,2},{12,4},{14,6},{16,24},{18,... | collective-permute-start | bytes 98312 | tf_op jit(solution)/shard_map/ppermute | solution.py:514
  83.2 4.9 %collective-permute-start.185 = (f32[64,128]{1,0:T(8,128)S(1)}, f32[64,128]{1,0:T(8,128)S(1)}, u32[]{:S(2)}, u32[]{:S(2)}) collective-permute-start(f32[64,128]{1,0:T(8,128)S(1)} %add_add_fusion.refs_0_), channel_id=1, source_target_pairs={{0,6},{2,4},{4,2},{6,0},{8,14},{10,12},{12,10},{14,8},{16,22},{18,... | collective-permute-start | bytes 98312 | tf_op jit(solution)/shard_map/ppermute | solution.py:514
  85.2 3.9 %collective-permute-start.184 = (f32[64,128]{1,0:T(8,128)S(1)}, f32[64,128]{1,0:T(8,128)S(1)}, u32[]{:S(2)}, u32[]{:S(2)}) collective-permute-start(f32[64,128]{1,0:T(8,128)S(1)} %add_add_fusion.refs_0_), channel_id=1, source_target_pairs={{0,4},{2,6},{4,0},{6,2},{8,12},{10,14},{12,8},{14,10},{16,20},{18,... | collective-permute-start | bytes 98312 | tf_op jit(solution)/shard_map/ppermute | solution.py:514
  85.8 3.9 %collective-permute-start.183 = (f32[64,128]{1,0:T(8,128)S(1)}, f32[64,128]{1,0:T(8,128)S(1)}, u32[]{:S(2)}, u32[]{:S(2)}) collective-permute-start(f32[64,128]{1,0:T(8,128)S(1)} %add_add_fusion.refs_0_), channel_id=1, source_target_pairs={{0,2},{2,0},{4,6},{6,4},{8,10},{10,8},{12,14},{14,12},{16,18},{18,... | collective-permute-start | bytes 98312 | tf_op jit(solution)/shard_map/ppermute | solution.py:514
  89.7 1.4 collective-permute-start.186
